TPU v7x, 32 devices: a whole 2x2x4 slice. The times are simulated.
32 devices in a mesh: dp: 8 (over y, x, core), tp: 4 (over z).
Axes of the slice: x: 2, y: 2, z: 4, core: 2. Of those that a mesh axis runs over, the one named last changes fastest.
Arguments:
- tokens: bfloat16 [16384, 1024], P(('dp', 'tp')), may hold values from -6 to 6
- segments: int32 [16, 1024], P('dp'), may hold values from 0 to 15, never falling along the last dimension, each value on 1 to 512 neighbouring positions
- cotangent: bfloat16 [16384, 1024], P(('dp', 'tp')), may hold values from -6 to 6
- attn_gain: bfloat16 [1024], P('dp'), may hold values from 0.099609375 to 1.8984375
- q_weight: bfloat16 [1024, 1024], P('dp', 'tp'), may hold values from -0.1875 to 0.1875
- k_weight: bfloat16 [1024, 512], P('dp', 'tp'), may hold values from -0.1875 to 0.1875
- v_weight: bfloat16 [1024, 512], P('dp', 'tp'), may hold values from -0.1875 to 0.1875
- query_gain: bfloat16 [64], P('dp'), may hold values from 0.099609375 to 1.8984375
- key_gain: bfloat16 [64], P('dp'), may hold values from 0.099609375 to 1.8984375
- o_weight: bfloat16 [1024, 1024], P('dp', 'tp'), may hold values from -0.75 to 0.75
- ffn_gain: bfloat16 [1024], P('dp'), may hold values from 0.099609375 to 1.8984375
- gate_weight: bfloat16 [1024, 4608], P('dp', 'tp'), may hold values from -0.1875 to 0.1875
- up_weight: bfloat16 [1024, 4608], P('dp', 'tp'), may hold values from -0.1875 to 0.1875
- down_weight: bfloat16 [1024, 4608], P('dp', 'tp'), may hold values from -0.09375 to 0.09375
Outputs:
- output: bfloat16 [16384, 1024], P(('dp', 'tp'))
- tokens_grad: bfloat16 [16384, 1024], P(('dp', 'tp'))
- attn_gain_grad: float32 [1024], P('dp')
- q_weight_grad: float32 [1024, 1024], P('dp', 'tp')
- k_weight_grad: float32 [1024, 512], P('dp', 'tp')
- v_weight_grad: float32 [1024, 512], P('dp', 'tp')
- query_gain_grad: float32 [64], P('dp')
- key_gain_grad: float32 [64], P('dp')
- o_weight_grad: float32 [1024, 1024], P('dp', 'tp')
- ffn_gain_grad: float32 [1024], P('dp')
- gate_weight_grad: float32 [1024, 4608], P('dp', 'tp')
- up_weight_grad: float32 [1024, 4608], P('dp', 'tp')
- down_weight_grad: float32 [1024, 4608], P('dp', 'tp')
Inputs may be any that keep to these rules, and one draw needn't show every extreme that they name: `segments`: within a sequence the document numbers never fall; every document has 1 to 512 tokens, and some document has exactly 512.
All inputs are finite; a program needn't handle non-finite values.
Results may differ from a plain program's by a relative error of at most 0.019.
Values may be sent and summed in bfloat16 or wider, within the bound.
No kernel may reach another device: no remote copies, remote signals or barrier semaphores. Data moves between devices by JAX's collectives and lax.ppermute only.
A program may use at most 192 MiB of HBM per device.

v0:
```python
import jax
import jax.numpy as jnp
from jax import lax
from jax.sharding import PartitionSpec as P

epsilon = 1e-05
theta_base = 1000000.0
masked_score = -1e30


def places(segments):
    token_index = lax.broadcasted_iota(jnp.int32, segments.shape, 1)
    previous = jnp.concatenate([segments[:, :1] - 1, segments[:, :-1]], axis=1)
    doc_first = lax.cummax(jnp.where(segments != previous, token_index, 0), axis=1)
    return token_index - doc_first


def rotary(segments, head_dim):
    half_dim = head_dim // 2
    frequency = theta_base ** (-2.0 * jnp.arange(half_dim, dtype=jnp.float32) / head_dim)
    angles = places(segments).astype(jnp.float32)[..., None] * frequency
    return (jnp.cos(angles)[:, :, None, :], jnp.sin(angles)[:, :, None, :])


def rotate(array_in, cosine_table, sine_table):
    half_dim = array_in.shape[-1] // 2
    first_half = array_in[..., :half_dim]
    second_half = array_in[..., half_dim:]
    return jnp.concatenate(
        [
            first_half * cosine_table - second_half * sine_table,
            second_half * cosine_table + first_half * sine_table,
        ],
        axis=-1,
    )


def row_norm(array_in):
    root_scale = lax.rsqrt(jnp.mean(array_in * array_in, axis=-1, keepdims=True) + epsilon)
    return (array_in * root_scale, root_scale)


def norm_back(grad_scaled, hatted, root_scale):
    return root_scale * (
        grad_scaled - hatted * jnp.mean(grad_scaled * hatted, axis=-1, keepdims=True)
    )


def contract_rows(left, right):
    return lax.dot_general(
        left, right, (((0,), (0,)), ((), ())), preferred_element_type=jnp.float32
    )


def contract_cols(left, right):
    return lax.dot_general(
        left, right, (((1,), (1,)), ((), ())), preferred_element_type=jnp.float32
    )


def scored(grouped, key_rot, segment):
    length = segment.shape[0]
    scores = jnp.einsum(
        "qkgd,skd->kgqs", grouped, key_rot, preferred_element_type=jnp.float32
    ) * grouped.shape[-1] ** (-0.5)
    row_index = lax.broadcasted_iota(jnp.int32, (length, length), 0)
    col_index = lax.broadcasted_iota(jnp.int32, (length, length), 1)
    allowed = (segment[:, None] == segment[None, :]) & (row_index >= col_index)
    return jnp.where(allowed, scores, masked_score)


def attend(operands):
    queries, key_rot, values, segment = operands
    length, kv_heads, head_dim = key_rot.shape
    grouped = queries.reshape(length, kv_heads, -1, head_dim)
    scores = scored(grouped, key_rot, segment)
    row_top = jnp.max(scores, axis=-1, keepdims=True)
    exponent = jnp.exp(scores - row_top)
    row_total = jnp.sum(exponent, axis=-1, keepdims=True)
    probability = (exponent / row_total).astype(jnp.bfloat16)
    context = jnp.einsum("kgqs,skd->qkgd", probability, values, preferred_element_type=jnp.float32)
    return (
        context.reshape(length, -1).astype(jnp.bfloat16),
        (row_top + jnp.log(row_total))[..., 0],
    )


def attend_back(operands):
    queries, key_rot, values, segment, log_total, grad_context = operands
    length, kv_heads, head_dim = key_rot.shape
    grouped = queries.reshape(length, kv_heads, -1, head_dim)
    grad_grouped = grad_context.reshape(length, kv_heads, -1, head_dim)
    scores = scored(grouped, key_rot, segment)
    probability = jnp.exp(scores - log_total[..., None])
    grad_probs = jnp.einsum(
        "qkgd,skd->kgqs", grad_grouped, values, preferred_element_type=jnp.float32
    )
    value_grad = jnp.einsum(
        "kgqs,qkgd->skd",
        probability.astype(jnp.bfloat16),
        grad_grouped,
        preferred_element_type=jnp.float32,
    )
    row_delta = jnp.sum(probability * grad_probs, axis=-1, keepdims=True)
    grad_scores = (probability * (grad_probs - row_delta)).astype(jnp.bfloat16)
    factor = head_dim ** (-0.5)
    query_grad = (
        jnp.einsum("kgqs,skd->qkgd", grad_scores, key_rot, preferred_element_type=jnp.float32)
        * factor
    )
    key_grad = (
        jnp.einsum("kgqs,qkgd->skd", grad_scores, grouped, preferred_element_type=jnp.float32)
        * factor
    )
    return (query_grad.reshape(length, -1, head_dim), key_grad, value_grad)


def shards(
    tokens,
    segments,
    cotangent,
    attn_gain,
    q_weight,
    k_weight,
    v_weight,
    query_gain,
    key_gain,
    o_weight,
    ffn_gain,
    gate_weight,
    up_weight,
    down_weight,
):
    gain_one, query_full, key_full, value_full, out_full, gain_query, gain_key = (
        lax.all_gather(attn_gain, "dp", axis=0, tiled=True),
        lax.all_gather(q_weight, "dp", axis=0, tiled=True),
        lax.all_gather(k_weight, "dp", axis=0, tiled=True),
        lax.all_gather(v_weight, "dp", axis=0, tiled=True),
        lax.all_gather(o_weight, "dp", axis=0, tiled=True),
        lax.all_gather(query_gain, "dp", axis=0, tiled=True),
        lax.all_gather(key_gain, "dp", axis=0, tiled=True),
    )
    head_dim = gain_query.shape[0]
    seq_count, length = segments.shape
    cosine_table, sine_table = rotary(segments, head_dim)
    inputs = tokens.astype(jnp.float32)
    hat_one, root_one = row_norm(inputs)
    normed_one = (hat_one * gain_one.astype(jnp.float32)).astype(jnp.bfloat16)
    rows_one = lax.all_gather(normed_one, "tp", axis=0, tiled=True)
    queries_raw = jnp.dot(rows_one, query_full, preferred_element_type=jnp.float32).reshape(
        seq_count, length, -1, head_dim
    )
    keys_raw = jnp.dot(rows_one, key_full, preferred_element_type=jnp.float32).reshape(
        seq_count, length, -1, head_dim
    )
    values = (
        jnp.dot(rows_one, value_full, preferred_element_type=jnp.float32)
        .astype(jnp.bfloat16)
        .reshape(seq_count, length, -1, head_dim)
    )
    query_hat, query_root = row_norm(queries_raw)
    key_hat, key_root = row_norm(keys_raw)
    query_rot = rotate(query_hat * gain_query.astype(jnp.float32), cosine_table, sine_table).astype(
        jnp.bfloat16
    )
    key_rot = rotate(key_hat * gain_key.astype(jnp.float32), cosine_table, sine_table).astype(
        jnp.bfloat16
    )
    context, log_total = lax.map(attend, (query_rot, key_rot, values, segments))
    context = context.reshape(seq_count * length, -1)
    attn_part = contract_cols(context, out_full)
    mid = inputs + lax.psum_scatter(attn_part, "tp", scatter_dimension=0, tiled=True)
    gain_two, gate_full, up_full, down_full = (
        lax.all_gather(ffn_gain, "dp", axis=0, tiled=True),
        lax.all_gather(gate_weight, "dp", axis=0, tiled=True),
        lax.all_gather(up_weight, "dp", axis=0, tiled=True),
        lax.all_gather(down_weight, "dp", axis=0, tiled=True),
    )
    hat_two, root_two = row_norm(mid)
    normed_two = (hat_two * gain_two.astype(jnp.float32)).astype(jnp.bfloat16)
    rows_two = lax.all_gather(normed_two, "tp", axis=0, tiled=True)
    gate_pre = jnp.dot(rows_two, gate_full, preferred_element_type=jnp.float32)
    up_pre = jnp.dot(rows_two, up_full, preferred_element_type=jnp.float32)
    gate_sig = jax.nn.sigmoid(gate_pre)
    hidden = (gate_pre * gate_sig * up_pre).astype(jnp.bfloat16)
    ffn_part = contract_cols(hidden, down_full)
    ffn_out = lax.psum_scatter(
        ffn_part.astype(jnp.bfloat16), "tp", scatter_dimension=0, tiled=True
    ).astype(jnp.float32)
    back_rows = lax.all_gather(cotangent, "tp", axis=0, tiled=True)
    output = (mid + ffn_out).astype(jnp.bfloat16)
    grad_hidden = jnp.dot(back_rows, down_full, preferred_element_type=jnp.float32)
    down_grad = contract_rows(back_rows, hidden)
    gate_grad = (grad_hidden * up_pre * gate_sig * (1.0 + gate_pre * (1.0 - gate_sig))).astype(
        jnp.bfloat16
    )
    up_grad = (grad_hidden * gate_pre * gate_sig).astype(jnp.bfloat16)
    gate_wgrad = contract_rows(rows_two, gate_grad)
    up_wgrad = contract_rows(rows_two, up_grad)
    ffn_back = contract_cols(gate_grad, gate_full) + contract_cols(up_grad, up_full)
    grad_normed_two = lax.psum_scatter(
        ffn_back.astype(jnp.bfloat16), "tp", scatter_dimension=0, tiled=True
    ).astype(jnp.float32)
    gate_wgrad, up_wgrad, down_grad = (
        lax.psum_scatter(gate_wgrad, "dp", scatter_dimension=0, tiled=True),
        lax.psum_scatter(up_wgrad, "dp", scatter_dimension=0, tiled=True),
        lax.psum_scatter(down_grad, "dp", scatter_dimension=0, tiled=True),
    )
    gain_two_part = jnp.sum(grad_normed_two * hat_two, axis=0)
    grad_mid = cotangent.astype(jnp.float32) + norm_back(
        grad_normed_two * gain_two.astype(jnp.float32), hat_two, root_two
    )
    branch_rows = lax.all_gather(grad_mid.astype(jnp.bfloat16), "tp", axis=0, tiled=True)
    grad_context = jnp.dot(branch_rows, out_full, preferred_element_type=jnp.float32).astype(
        jnp.bfloat16
    )
    out_grad = contract_rows(branch_rows, context)
    query_grad, key_grad, value_grad = lax.map(
        attend_back,
        (
            query_rot,
            key_rot,
            values,
            segments,
            log_total,
            grad_context.reshape(seq_count, length, -1),
        ),
    )
    query_normed_grad = rotate(query_grad, cosine_table, -sine_table)
    key_normed_grad = rotate(key_grad, cosine_table, -sine_table)
    gain_query_part = jnp.sum(query_normed_grad * query_hat, axis=(0, 1, 2))
    gain_key_part = jnp.sum(key_normed_grad * key_hat, axis=(0, 1, 2))
    query_raw_grad = norm_back(
        query_normed_grad * gain_query.astype(jnp.float32), query_hat, query_root
    )
    key_raw_grad = norm_back(key_normed_grad * gain_key.astype(jnp.float32), key_hat, key_root)
    query_raw_grad = query_raw_grad.astype(jnp.bfloat16).reshape(seq_count * length, -1)
    key_raw_grad = key_raw_grad.astype(jnp.bfloat16).reshape(seq_count * length, -1)
    value_grad = value_grad.astype(jnp.bfloat16).reshape(seq_count * length, -1)
    query_wgrad = contract_rows(rows_one, query_raw_grad)
    key_wgrad = contract_rows(rows_one, key_raw_grad)
    value_wgrad = contract_rows(rows_one, value_grad)
    attn_back = (
        contract_cols(query_raw_grad, query_full)
        + contract_cols(key_raw_grad, key_full)
        + contract_cols(value_grad, value_full)
    )
    grad_normed_one = lax.psum_scatter(
        attn_back.astype(jnp.bfloat16), "tp", scatter_dimension=0, tiled=True
    ).astype(jnp.float32)
    gain_one_part = jnp.sum(grad_normed_one * hat_one, axis=0)
    tokens_grad = (
        grad_mid + norm_back(grad_normed_one * gain_one.astype(jnp.float32), hat_one, root_one)
    ).astype(jnp.bfloat16)
    gain_one_sum, gain_two_sum, gain_query_sum, gain_key_sum = lax.psum(
        (gain_one_part, gain_two_part, gain_query_part, gain_key_part), "tp"
    )
    (
        query_wgrad,
        key_wgrad,
        value_wgrad,
        out_grad,
        gain_one_sum,
        gain_query_sum,
        gain_key_sum,
        gain_two_sum,
    ) = (
        lax.psum_scatter(query_wgrad, "dp", scatter_dimension=0, tiled=True),
        lax.psum_scatter(key_wgrad, "dp", scatter_dimension=0, tiled=True),
        lax.psum_scatter(value_wgrad, "dp", scatter_dimension=0, tiled=True),
        lax.psum_scatter(out_grad, "dp", scatter_dimension=0, tiled=True),
        lax.psum_scatter(gain_one_sum, "dp", scatter_dimension=0, tiled=True),
        lax.psum_scatter(gain_query_sum, "dp", scatter_dimension=0, tiled=True),
        lax.psum_scatter(gain_key_sum, "dp", scatter_dimension=0, tiled=True),
        lax.psum_scatter(gain_two_sum, "dp", scatter_dimension=0, tiled=True),
    )
    return (
        output,
        tokens_grad,
        gain_one_sum,
        query_wgrad,
        key_wgrad,
        value_wgrad,
        gain_query_sum,
        gain_key_sum,
        out_grad,
        gain_two_sum,
        gate_wgrad,
        up_wgrad,
        down_grad,
    )


def solution(mesh):
    placed = (
        P(("dp", "tp"), None),
        P("dp", None),
        P(("dp", "tp"), None),
        P("dp"),
        P("dp", "tp"),
        P("dp", "tp"),
        P("dp", "tp"),
        P("dp"),
        P("dp"),
        P("dp", "tp"),
        P("dp"),
        P("dp", "tp"),
        P("dp", "tp"),
        P("dp", "tp"),
    )
    return jax.shard_map(
        shards,
        mesh=mesh,
        in_specs=placed,
        out_specs=(
            P(("dp", "tp"), None),
            P(("dp", "tp"), None),
            P("dp"),
            P("dp", "tp"),
            P("dp", "tp"),
            P("dp", "tp"),
            P("dp"),
            P("dp"),
            P("dp", "tp"),
            P("dp"),
            P("dp", "tp"),
            P("dp", "tp"),
            P("dp", "tp"),
        ),
        check_vma=False,
    )
```

profile of v0, /device:TPU:1, one launch (start us, length us, event | category | flops | bytes accessed | tf_op | source)
XLA Modules:
  0.0 1365.4 jit_solution(12902632476411677527)
XLA Ops:
  82.9 20.8 %all-gather.10.cloned.1.call-done = bf16[2048,1024]{1,0:T(8,128)(2,1)} async-done(((bf16[512,1024]{1,0:T(8,128)(2,1)}), bf16[2048,1024]{1,0:T(8,128)(2,1)}) %all-gather.10.cloned.1.call-update) | async-done | bytes 4194320 | tf_op jit(solution)/shard_map/all_gather | solution.py:149
  131.3 29.3 %while.26 = (s32[]{:T(128)}, bf16[2,1024,256]{2,1,0:T(8,128)(2,1)}, f32[2,2,2,1024]{3,2,1,0:T(2,128)S(1)}, bf16[2,1024,2,64]{1,3,2,0:T(8,128)(2,1)}, s32[2,1024]...) while((s32[]{:T(128)}, bf16[2,1024,256]{2,1,0:T(8,128)(2,1)}, ...), condition=%wide.region_8.9_spmd, body=%wide.region_5.8_spmd.sunk | while | flops 1127477248 | bytes 61485200 | solution.py:169
  176.2 133.1 %reduce-scatter.12.cloned.1.call-done = f32[512,1024]{1,0:T(8,128)} async-done(((f32[2048,1024]{1,0:T(8,128)}), f32[512,1024]{1,0:T(8,128)}) %reduce-scatter.12.cloned.1.call-update) | async-done | bytes 2097168 | tf_op jit(solution)/shard_map/reduce_scatter | solution.py:172
  315.2 79.4 %all-gather.12.cloned.1.call-done = bf16[2048,1024]{1,0:T(8,128)(2,1)} async-done(((bf16[512,1024]{1,0:T(8,128)(2,1)}), bf16[2048,1024]{1,0:T(8,128)(2,1)}) %all-gather.12.cloned.1.call-update) | async-done | bytes 4194320 | tf_op jit(solution)/shard_map/all_gather | solution.py:181
  405.2 19.0 %all-gather.14.cloned.1.call-done = bf16[1024,1152]{1,0:T(8,128)(2,1)} async-done(((bf16[128,1152]{1,0:T(8,128)(2,1)}), bf16[1024,1152]{1,0:T(8,128)(2,1)}) %all-gather.14.cloned.1.call-update) | async-done | bytes 2359312 | tf_op jit(solution)/shard_map/all_gather | solution.py:175
  434.5 20.5 %all-gather.18.cloned.1.call-done = bf16[1024,1152]{1,0:T(8,128)(2,1)} async-done(((bf16[128,1152]{1,0:T(8,128)(2,1)}), bf16[1024,1152]{1,0:T(8,128)(2,1)}) %all-gather.18.cloned.1.call-update) | async-done | bytes 2359312 | tf_op jit(solution)/shard_map/all_gather | solution.py:177
  455.0 81.8 %all-gather.20.cloned.1.call-done = bf16[2048,1024]{1,0:T(8,128)(2,1)} async-done(((bf16[512,1024]{1,0:T(8,128)(2,1)}), bf16[2048,1024]{1,0:T(8,128)(2,1)}) %all-gather.20.cloned.1.call-update) | async-done | bytes 4194320 | tf_op jit(solution)/shard_map/all_gather | solution.py:190
  536.8 17.3 %multiply_convert_fusion = (bf16[2048,1152]{1,0:T(8,128)(2,1)}, bf16[2048,1152]{1,0:T(8,128)(2,1)S(1)}, bf16[2048,1152]{1,0:T(8,128)(2,1)}) fusion(f32[2048,1152]{1,0:T(8,128)} %fusion.71, f32[2048,1152]{1,0:T(8,128)} %fusion.72, bf16[2048,1024]{1,0:T(8,128)(2,1)} %all-gather.20.cloned.1.call-done, bf16[1024,1152]{1,0:T(8,128)(2,1)} %all-gather.18.cloned.1.call-done), kind=kOutput, calls=%fused_computation.58 | convolution fusion | flops 4869586944 | bytes 39583744 | tf_op jit(solution)/shard_map/dot_general | solution.py:192
  567.8 75.4 %reduce-scatter.16.cloned.1.call-done = bf16[512,1024]{1,0:T(8,128)(2,1)} async-done(((bf16[2048,1024]{1,0:T(8,128)(2,1)}), bf16[512,1024]{1,0:T(8,128)(2,1)}) %reduce-scatter.16.cloned.1.call-update) | async-done | bytes 1048592 | tf_op jit(solution)/shard_map/reduce_scatter | solution.py:201
  666.6 64.1 %all-gather.22.cloned.1.call-done = bf16[2048,1024]{1,0:T(8,128)(2,1)} async-done(((bf16[512,1024]{1,0:T(8,128)(2,1)}), bf16[2048,1024]{1,0:T(8,128)(2,1)}) %all-gather.22.cloned.1.call-update) | async-done | bytes 4194320 | tf_op jit(solution)/shard_map/all_gather | solution.py:213
  735.1 160.7 %while.27 = (s32[]{:T(128)}, f32[2,1024,4,64]{1,0,3,2:T(2,128)}, f32[2,1024,2,64]{1,0,3,2:T(2,128)}, bf16[2,1024,2,64]{1,3,2,0:T(8,128)(2,1)}, bf16[2,1024,2,64]...) while((s32[]{:T(128)}, f32[2,1024,4,64]{1,0,3,2:T(2,128)}, ...), condition=%wide.region_16.17_spmd, body=%wide.region_14.16_spmd.sunk | while | flops 2750803968 | bytes 209908208 | solution.py:218
  758.2 13.8 %fusion.169 = (f32[2,2,1024]{2,1,0:T(2,128)}, f32[2,1024,1024,2]{2,1,3,0:T(8,128)}) fusion(f32[2,1024,1024,2]{2,1,3,0:T(8,128)} %fusion.167, f32[2,2,1024]{2,1,0:T(2,128)} %dynamic-slice_bitcast_fusion.2, pred[1024,1024]{0,1:T(8,128)(4,1)S(1)} %fusion.168, bf16[1024,2,2,64]{0,3,2,1:T(8,128)(2,1)} %bitcast.282, ...), kind=kOutput, calls=%fused_computation.24.clone.1 | convolution fusion | flops 557838336 | bytes 35422212 | tf_op jit(solution)/shard_map/while/body/eval_jaxpr/qkgd,skd->kgqs/dot_general | solution.py:95
  797.6 18.7 %dynamic_update_slice.30 = f32[2,1024,4,64]{1,0,3,2:T(2,128)} dynamic-update-slice(f32[2,1024,4,64]{1,0,3,2:T(2,128)} %get-tuple-element.459, f32[1,1024,4,64]{1,0,3,2:T(1,128)S(1)} %copy.187, s32[]{:T(128)S(6)} %copy.209, s32[]{:T(128)} %constant.80.clone.1..sunk, s32[]{:T(128)} %constant.80.clone.1..sunk, s32[]{:T(128)} %constant.80.clone.1..sunk) | dynamic-update-slice | bytes 2097156 | tf_op jit(solution)/shard_map/while/body/jit(dynamic_update_index_in_dim)/dynamic_update_slice | solution.py:218
  838.1 13.6 fusion.169
  876.9 18.7 %dynamic_update_slice.30 = f32[2,1024,4,64]{1,0,3,2:T(2,128)} dynamic-update-slice(f32[2,1024,4,64]{1,0,3,2:T(2,128)} %get-tuple-element.459, f32[1,1024,4,64]{1,0,3,2:T(1,128)S(1)} %copy.187, s32[]{:T(128)S(6)} %copy.209, s32[]{:T(128)} %constant.80.clone.1..sunk, s32[]{:T(128)} %constant.80.clone.1..sunk, s32[]{:T(128)} %constant.80.clone.1..sunk) | dynamic-update-slice | bytes 2097156 | tf_op jit(solution)/shard_map/while/body/jit(dynamic_update_index_in_dim)/dynamic_update_slice | solution.py:218
  984.3 22.2 %reduce-scatter.18.cloned.1.call-done = bf16[512,1024]{1,0:T(8,128)(2,1)} async-done(((bf16[2048,1024]{1,0:T(8,128)(2,1)}), bf16[512,1024]{1,0:T(8,128)(2,1)}) %reduce-scatter.18.cloned.1.call-update) | async-done | bytes 1048592 | tf_op jit(solution)/shard_map/reduce_scatter | solution.py:248
  1008.6 12.7 all-reduce.6
  1031.5 54.8 %reduce-scatter.14.cloned.1.call-done = bf16[512,1024]{1,0:T(8,128)(2,1)} async-done(((bf16[2048,1024]{1,0:T(8,128)(2,1)}), bf16[512,1024]{1,0:T(8,128)(2,1)}) %reduce-scatter.14.cloned.1.call-update) | async-done | bytes 1048592 | tf_op jit(solution)/shard_map/reduce_scatter | solution.py:187
  1090.3 54.5 %reduce-scatter.30.cloned.1.call-done = f32[128,1152]{1,0:T(8,128)} async-done(((f32[1024,1152]{1,0:T(8,128)}), f32[128,1152]{1,0:T(8,128)}) %reduce-scatter.30.cloned.1.call-update) | async-done | bytes 589840 | tf_op jit(solution)/shard_map/reduce_scatter | solution.py:206
  1144.8 58.0 %reduce-scatter.28.cloned.1.call-done = f32[128,1152]{1,0:T(8,128)} async-done(((f32[1024,1152]{1,0:T(8,128)}), f32[128,1152]{1,0:T(8,128)}) %reduce-scatter.28.cloned.1.call-update) | async-done | bytes 589840 | tf_op jit(solution)/shard_map/reduce_scatter | solution.py:205
  1202.8 37.3 %reduce-scatter.24.cloned.1.call-done = f32[128,128]{1,0:T(8,128)} async-done(((f32[1024,128]{1,0:T(8,128)}), f32[128,128]{1,0:T(8,128)}) %reduce-scatter.24.cloned.1.call-update) | async-done | bytes 65552 | tf_op jit(solution)/shard_map/reduce_scatter | solution.py:270
  1240.1 37.9 %reduce-scatter.22.cloned.1.call-done = f32[128,128]{1,0:T(8,128)} async-done(((f32[1024,128]{1,0:T(8,128)}), f32[128,128]{1,0:T(8,128)}) %reduce-scatter.22.cloned.1.call-update) | async-done | bytes 65552 | tf_op jit(solution)/shard_map/reduce_scatter | solution.py:269
  1278.1 40.0 %reduce-scatter.26.cloned.1.call-done = f32[128,256]{1,0:T(8,128)} async-done(((f32[1024,256]{1,0:T(8,128)}), f32[128,256]{1,0:T(8,128)}) %reduce-scatter.26.cloned.1.call-update) | async-done | bytes 131088 | tf_op jit(solution)/shard_map/reduce_scatter | solution.py:271
  1318.1 39.7 %reduce-scatter.20.cloned.1.call-done = f32[128,256]{1,0:T(8,128)} async-done(((f32[1024,256]{1,0:T(8,128)}), f32[128,256]{1,0:T(8,128)}) %reduce-scatter.20.cloned.1.call-update) | async-done | bytes 131088 | tf_op jit(solution)/shard_map/reduce_scatter | solution.py:268
  (403 shorter events, 411.8 us)
Async XLA Ops:
  8.1 95.6 %all-gather.10.cloned.1.call-start = ((), (), s32[]{:S(2)}) async-start(), calls=%async_computation.11 | async-start | bytes 5242880 | tf_op jit(solution)/shard_map/all_gather | solution.py:149
  23.0 286.3 %reduce-scatter.12.cloned.1.call-start = ((), (), s32[]{:S(2)}) async-start(), calls=%async_computation.12 | async-start | bytes 10485760 | tf_op jit(solution)/shard_map/reduce_scatter | solution.py:172
  166.4 148.8 %all-gather.16.cloned.1.call-start = ((), (), s32[]{:S(2)}) async-start(), calls=%async_computation.15 | async-start | bytes 2654208 | tf_op jit(solution)/shard_map/all_gather | solution.py:176
  167.0 227.7 %all-gather.12.cloned.1.call-start = ((), (), s32[]{:S(2)}) async-start(), calls=%async_computation.13 | async-start | bytes 5242880 | tf_op jit(solution)/shard_map/all_gather | solution.py:181
  176.2 469.5 %copy-start.48 = (f32[8,1,128]{2,1,0:T(1,128)}, f32[8,1,128]{2,1,0:T(1,128)S(1)}, u32[]{:S(2)}) copy-start(f32[8,1,128]{2,1,0:T(1,128)S(1)} %convert_element_type.142) | copy-start | bytes 12292
  311.6 334.1 %copy-start.3 = (f32[512,1024]{1,0:T(8,128)}, f32[512,1024]{1,0:T(8,128)S(1)}, u32[]{:S(2)}) copy-start(f32[512,1024]{1,0:T(8,128)S(1)} %get-tuple-element.279) | copy-start | bytes 6291460
  311.6 334.1 %copy-start.54 = (f32[512]{0:T(512)}, f32[512]{0:T(512)S(1)}, u32[]{:S(2)}) copy-start(f32[512]{0:T(512)S(1)} %add_rsqrt_fusion.2) | copy-start | bytes 6148
  313.0 111.2 %all-gather.14.cloned.1.call-start = ((), (), s32[]{:S(2)}) async-start(), calls=%async_computation.14 | async-start | bytes 2654208 | tf_op jit(solution)/shard_map/all_gather | solution.py:175
  313.6 141.4 %all-gather.18.cloned.1.call-start = ((), (), s32[]{:S(2)}) async-start(), calls=%async_computation.16 | async-start | bytes 2654208 | tf_op jit(solution)/shard_map/all_gather | solution.py:177
  314.3 222.4 %all-gather.20.cloned.1.call-start = ((), (), s32[]{:S(2)}) async-start(), calls=%async_computation.18 | async-start | bytes 5242880 | tf_op jit(solution)/shard_map/all_gather | solution.py:190
  315.1 328.1 %reduce-scatter.16.cloned.1.call-start = ((), (), s32[]{:S(2)}) async-start(), calls=%async_computation.19 | async-start | bytes 5242880 | tf_op jit(solution)/shard_map/reduce_scatter | solution.py:201
  567.7 162.9 %all-gather.22.cloned.1.call-start = ((), (), s32[]{:S(2)}) async-start(), calls=%async_computation.20 | async-start | bytes 5242880 | tf_op jit(solution)/shard_map/all_gather | solution.py:213
  649.5 332.5 %reduce-scatter.32.cloned.1.call-start = ((), (), s32[]{:S(2)}) async-start(), calls=%async_computation.28 | async-start | bytes 5308416 | tf_op jit(solution)/shard_map/reduce_scatter | solution.py:207
  666.5 340.1 %reduce-scatter.18.cloned.1.call-start = ((), (), s32[]{:S(2)}) async-start(), calls=%async_computation.21 | async-start | bytes 5242880 | tf_op jit(solution)/shard_map/reduce_scatter | solution.py:248
  931.2 155.1 %reduce-scatter.14.cloned.1.call-start = ((), (), s32[]{:S(2)}) async-start(), calls=%async_computation.17 | async-start | bytes 5242880 | tf_op jit(solution)/shard_map/reduce_scatter | solution.py:187
  941.3 203.5 %reduce-scatter.30.cloned.1.call-start = ((), (), s32[]{:S(2)}) async-start(), calls=%async_computation.27 | async-start | bytes 5308416 | tf_op jit(solution)/shard_map/reduce_scatter | solution.py:206
  951.7 251.1 %reduce-scatter.28.cloned.1.call-start = ((), (), s32[]{:S(2)}) async-start(), calls=%async_computation.26 | async-start | bytes 5308416 | tf_op jit(solution)/shard_map/reduce_scatter | solution.py:205
  962.3 277.8 %reduce-scatter.24.cloned.1.call-start = ((), (), s32[]{:S(2)}) async-start(), calls=%async_computation.24 | async-start | bytes 589824 | tf_op jit(solution)/shard_map/reduce_scatter | solution.py:270
  966.7 311.3 %reduce-scatter.22.cloned.1.call-start = ((), (), s32[]{:S(2)}) async-start(), calls=%async_computation.23 | async-start | bytes 589824 | tf_op jit(solution)/shard_map/reduce_scatter | solution.py:269
  971.2 346.9 %reduce-scatter.26.cloned.1.call-start = ((), (), s32[]{:S(2)}) async-start(), calls=%async_computation.25 | async-start | bytes 1179648 | tf_op jit(solution)/shard_map/reduce_scatter | solution.py:271
  975.8 382.0 %reduce-scatter.20.cloned.1.call-start = ((), (), s32[]{:S(2)}) async-start(), calls=%async_computation.22 | async-start | bytes 1179648 | tf_op jit(solution)/shard_map/reduce_scatter | solution.py:268
  980.5 105.9 %copy-start.4 = (f32[512,1024]{1,0:T(8,128)S(1)}, f32[512,1024]{1,0:T(8,128)}, u32[]{:S(2)}) copy-start(f32[512,1024]{1,0:T(8,128)} %copy-done.3) | copy-start | bytes 6291460
  980.5 105.9 %copy-start.49 = (f32[8,1,128]{2,1,0:T(1,128)S(1)}, f32[8,1,128]{2,1,0:T(1,128)}, u32[]{:S(2)}) copy-start(f32[8,1,128]{2,1,0:T(1,128)} %copy-done.48) | copy-start | bytes 12292
  980.5 105.9 %copy-start.55 = (f32[512]{0:T(512)S(1)}, f32[512]{0:T(512)}, u32[]{:S(2)}) copy-start(f32[512]{0:T(512)} %copy-done.54) | copy-start | bytes 6148
  (92 other events, 1694.1 us)
Sparse Core Ops, SparseCore 0:
  23.1 80.4 all-gather.9
  166.5 142.8 reduce-scatter.11
  567.8 75.3 reduce-scatter.15
Sparse Core Ops, SparseCore 1:
  168.7 27.7 all-gather.15
  313.1 81.5 all-gather.11
  396.4 27.8 all-gather.13
  426.1 28.8 all-gather.17
  456.6 80.1 all-gather.19
  649.5 81.0 all-gather.21
  734.3 52.2 reduce-scatter.31
  931.3 75.2 reduce-scatter.17
  1008.8 77.4 reduce-scatter.13
  1090.4 54.3 reduce-scatter.29
  1149.1 53.7 reduce-scatter.27
  1206.5 33.6 reduce-scatter.23
  1244.0 34.1 reduce-scatter.21
  1281.8 36.2 reduce-scatter.25
  1321.9 35.9 reduce-scatter.19
where the time goes:
time: 1380 us; the launch traced here: 1370 us
  waiting for transfers between devices  841 us (61%)
  matrix products  228 us (17%)
  local copies, waits for them, and re-layouts  113 us (8%)
  blocking collectives  93.4 us (7%)
  other arithmetic  68.8 us (5%)
  between operations  19.1 us (1%)
    reduce_scatter x1, waiting for transfers between devices, shards(): lax.psum_scatter(attn_part, 'tp', scatter_dimension=0, tiled=True)  133 us
    all_gather x1, waiting for transfers between devices, shards(): back_rows = lax.all_gather(cotangent, 'tp', axis=0, tiled=True)  81.8 us
    all_gather x1, waiting for transfers between devices, shards(): rows_two = lax.all_gather(normed_two, 'tp', axis=0, tiled=True)  79.4 us
    reduce_scatter x1, waiting for transfers between devices, shards(): lax.psum_scatter(ffn_back.astype(jnp.bfloat16), 'tp', scatter_dimension=0...  75.4 us
    all_gather x1, waiting for transfers between devices, shards(): lax.all_gather(grad_mid.astype(jnp.bfloat16), 'tp', axis=0, tiled=True)  64.1 us
    dynamic_update_slice x8, local copies, waits for them, and re-layouts, shards(): lax.map(attend_back, (query_rot, key_rot, values, segments, log_total, gr...  60.5 us
    reduce_scatter x1, waiting for transfers between devices, shards(): lax.psum_scatter(gate_wgrad, 'dp', scatter_dimension=0, tiled=True)  58 us
    reduce_scatter x1, waiting for transfers between devices, shards(): lax.psum_scatter(ffn_part.astype(jnp.bfloat16), 'tp', scatter_dimension=0...  54.8 us
  transfers between devices with their start and end apart: 18, of which 16 were waited for; matrix products, arithmetic and copies ran while one was open for 22% of the time, Pallas kernels for 0%

commit v1 on v0

v1 whole, which is shorter than its diff:
```python
import functools

import jax
import jax.numpy as jnp
from jax import lax
from jax.experimental import pallas as pl
from jax.experimental.pallas import tpu as pltpu
from jax.sharding import Mesh, PartitionSpec as P

epsilon = 1e-05
theta_base = 1000000.0
bf16 = jnp.bfloat16
f32 = jnp.float32
tile = 256
span = 512


def dot(left, right, left_dim, right_dim):
    return lax.dot_general(
        left, right, (((left_dim,), (right_dim,)), ((), ())), preferred_element_type=f32
    )


def group_sum(value, ones):
    high = value.astype(bf16)
    low = (value - high.astype(f32)).astype(bf16)
    return dot(high, ones, 1, 0) + dot(low, ones, 1, 0)


def ones_by_head(lanes, head):
    row = lax.broadcasted_iota(jnp.int32, (lanes, lanes), 0) // head
    col = lax.broadcasted_iota(jnp.int32, (lanes, lanes), 1) // head
    return jnp.where(row == col, 1.0, 0.0).astype(bf16)


def half_swap(value, head):
    lanes = value.shape[-1]
    lane = lax.broadcasted_iota(jnp.int32, value.shape, 1) % head
    return jnp.where(
        lane < head // 2,
        pltpu.roll(value, lanes - head // 2, 1),
        pltpu.roll(value, head // 2, 1),
    )


def head_norm(raw, ones, head):
    root = lax.rsqrt(group_sum(raw * raw, ones) * (1.0 / head) + epsilon)
    return raw * root, root


def split_block(block, head):
    lanes = 2 * head
    queries = block[:, :lanes]
    both = block[:, lanes:]
    other = pltpu.roll(both, head, 1)
    first = lax.broadcasted_iota(jnp.int32, both.shape, 1) < head
    keys = jnp.where(first, both, other)
    values = jnp.where(first, other, both)
    return queries, keys, values


def stack_heads(block, head):
    first = lax.broadcasted_iota(jnp.int32, block.shape, 1) < head
    zero = jnp.zeros_like(block)
    return jnp.concatenate([jnp.where(first, block, zero), jnp.where(first, zero, block)], axis=0)


def merge_heads(stacked, head):
    half = stacked.shape[0] // 2
    first = lax.broadcasted_iota(jnp.int32, (half, stacked.shape[1]), 1) < head
    return jnp.where(first, stacked[:half], stacked[half:])


def attend_kernel(head, qkv_ref, cos_ref, sin_ref, seg_col, seg_row, gain_ref, ctx_ref, q_s, k_s, v_s):
    length = qkv_ref.shape[0]
    lanes = 2 * head
    ones = ones_by_head(lanes, head)
    queries, keys, values = split_block(qkv_ref[...], head)
    cosine, sine = cos_ref[...], sin_ref[...]

    def rotated(raw, gain):
        hat, _ = head_norm(raw, ones, head)
        scaled = hat * gain
        return (scaled * cosine + half_swap(scaled, head) * sine).astype(bf16)

    q_s[...] = rotated(queries, gain_ref[0:1, :]) * jnp.asarray(head**-0.5, bf16)
    k_s[...] = rotated(keys, gain_ref[1:2, :])
    v_s[...] = values.astype(bf16)
    for top in range(0, length, tile):
        low, high = max(0, top - span), top + tile
        stacked = stack_heads(q_s[top:high, :], head)
        scores = dot(stacked, k_s[low:high, :], 1, 1)
        row = lax.broadcasted_iota(jnp.int32, (tile, high - low), 0) + top
        col = lax.broadcasted_iota(jnp.int32, (tile, high - low), 1) + low
        allowed = (seg_col[top:high, 0:1] == seg_row[0:1, low:high]) & (row >= col)
        allowed = jnp.concatenate([allowed, allowed], axis=0)
        exponent = jnp.where(allowed, jnp.exp(scores), 0.0)
        total = jnp.sum(exponent, axis=1, keepdims=True)
        mixed = dot(exponent.astype(bf16), v_s[low:high, :], 1, 0) / total
        ctx_ref[top:high, :] = merge_heads(mixed, head).astype(bf16)


def attend(qkv, cosine, sine, seg_col, seg_row, gains, head):
    length, width = qkv.shape
    groups = width // (4 * head)
    lanes = 2 * head
    whole = lambda shape: pl.BlockSpec(shape, lambda j: (0, 0))
    return pl.pallas_call(
        functools.partial(attend_kernel, head),
        grid=(groups,),
        in_specs=[
            pl.BlockSpec((length, 2 * lanes), lambda j: (0, j)),
            whole((length, lanes)),
            whole((length, lanes)),
            whole((length, 1)),
            whole((1, length)),
            whole((8, lanes)),
        ],
        out_specs=pl.BlockSpec((length, lanes), lambda j: (0, j)),
        out_shape=jax.ShapeDtypeStruct((length, groups * lanes), bf16),
        scratch_shapes=[pltpu.VMEM((length, lanes), bf16)] * 3,
        compiler_params=pltpu.CompilerParams(vmem_limit_bytes=40 * 2**20),
        cost_estimate=pl.CostEstimate(flops=12 * 10**9, bytes_accessed=8 * 10**6, transcendentals=0),
        name="attend",
    )(qkv, cosine, sine, seg_col, seg_row, gains)


def attend_back_kernel(
    head, qkv_ref, cos_ref, sin_ref, seg_col, seg_row, gain_ref, do_ref, out_ref, sums_ref,
    q_s, k_s, v_s, dk_s, dv_s, dq_s,
):
    length = qkv_ref.shape[0]
    lanes = 2 * head
    ones = ones_by_head(lanes, head)
    queries, keys, values = split_block(qkv_ref[...], head)
    cosine, sine = cos_ref[...], sin_ref[...]

    def rotated(raw, gain):
        hat, _ = head_norm(raw, ones, head)
        scaled = hat * gain
        return (scaled * cosine + half_swap(scaled, head) * sine).astype(bf16)

    scale = jnp.asarray(head**-0.5, bf16)
    q_s[...] = rotated(queries, gain_ref[0:1, :]) * scale
    k_s[...] = rotated(keys, gain_ref[1:2, :])
    v_s[...] = values.astype(bf16)
    dk_s[...] = jnp.zeros_like(dk_s)
    dv_s[...] = jnp.zeros_like(dv_s)
    for top in range(0, length, tile):
        low, high = max(0, top - span), top + tile
        stacked = stack_heads(q_s[top:high, :], head)
        grads = stack_heads(do_ref[top:high, :], head)
        near_k, near_v = k_s[low:high, :], v_s[low:high, :]
        scores = dot(near_k, stacked, 1, 1)
        col = lax.broadcasted_iota(jnp.int32, (high - low, tile), 0) + low
        row = lax.broadcasted_iota(jnp.int32, (high - low, tile), 1) + top
        allowed = (seg_col[low:high, 0:1] == seg_row[0:1, top:high]) & (row >= col)
        allowed = jnp.concatenate([allowed, allowed], axis=1)
        exponent = jnp.where(allowed, jnp.exp(scores), 0.0)
        probs = exponent * (1.0 / jnp.sum(exponent, axis=0, keepdims=True))
        grad_probs = dot(near_v, grads, 1, 1)
        weighted = probs * grad_probs
        delta = jnp.sum(weighted, axis=0, keepdims=True)
        grad_scores = (weighted - probs * delta).astype(bf16)
        dv_s[low:high, :] += dot(probs.astype(bf16), grads, 1, 0)
        dk_s[low:high, :] += dot(grad_scores, stacked, 1, 0)
        dq_s[top:high, :] = merge_heads(dot(grad_scores, near_k, 0, 0), head) * head**-0.5

    def back(raw, gain, grad):
        hat, root = head_norm(raw, ones, head)
        normed = grad * cosine - half_swap(grad, head) * sine
        gain_part = jnp.sum(normed * hat, axis=0, keepdims=True)
        scaled = normed * gain
        mean = group_sum(scaled * hat, ones) * (1.0 / head)
        return root * (scaled - hat * mean), gain_part

    grad_q, q_sum = back(queries, gain_ref[0:1, :], dq_s[...])
    folded_k = dk_s[...] + pltpu.roll(dk_s[...], head, 1)
    grad_k, k_sum = back(keys, gain_ref[1:2, :], folded_k)
    folded_v = dv_s[...] + pltpu.roll(dv_s[...], head, 1)
    first = lax.broadcasted_iota(jnp.int32, (length, lanes), 1) < head
    out_ref[:, :lanes] = grad_q.astype(bf16)
    out_ref[:, lanes:] = jnp.where(first, grad_k, folded_v).astype(bf16)
    which = lax.broadcasted_iota(jnp.int32, sums_ref.shape, 0)
    sums_ref[...] = jnp.where(which == 0, q_sum, jnp.where(which == 1, k_sum, 0.0))


def attend_back(qkv, cosine, sine, seg_col, seg_row, gains, grad_context, head):
    length, width = qkv.shape
    groups = width // (4 * head)
    lanes = 2 * head
    whole = lambda shape: pl.BlockSpec(shape, lambda j: (0, 0))
    return pl.pallas_call(
        functools.partial(attend_back_kernel, head),
        grid=(groups,),
        in_specs=[
            pl.BlockSpec((length, 2 * lanes), lambda j: (0, j)),
            whole((length, lanes)),
            whole((length, lanes)),
            whole((length, 1)),
            whole((1, length)),
            whole((8, lanes)),
            pl.BlockSpec((length, lanes), lambda j: (0, j)),
        ],
        out_specs=(
            pl.BlockSpec((length, 2 * lanes), lambda j: (0, j)),
            pl.BlockSpec((8, lanes), lambda j: (j, 0)),
        ),
        out_shape=(
            jax.ShapeDtypeStruct((length, width), bf16),
            jax.ShapeDtypeStruct((8 * groups, lanes), f32),
        ),
        scratch_shapes=[pltpu.VMEM((length, lanes), bf16)] * 3 + [pltpu.VMEM((length, lanes), f32)] * 3,
        compiler_params=pltpu.CompilerParams(vmem_limit_bytes=48 * 2**20),
        cost_estimate=pl.CostEstimate(flops=30 * 10**9, bytes_accessed=10 * 10**6, transcendentals=0),
        name="attend_back",
    )(qkv, cosine, sine, seg_col, seg_row, gains, grad_context)


def ffn_kernel(w_ref, rows_ref, cot_ref, hid_ref, gate_ref, up_ref):
    rows, cot = rows_ref[...], cot_ref[...]
    gate = dot(w_ref[0], rows, 1, 1)
    up = dot(w_ref[1], rows, 1, 1)
    back = dot(w_ref[2], cot, 1, 1)
    sig = 1.0 / (1.0 + jnp.exp(-gate))
    act = gate * sig
    hid_ref[...] = (act * up).astype(bf16)
    gate_ref[...] = (back * up * (sig + act * (1.0 - sig))).astype(bf16)
    up_ref[...] = (back * act).astype(bf16)


def ffn_hidden(weights, rows, cot):
    _, hidden, width = weights.shape
    count = rows.shape[0]
    h_tile = 384 if hidden % 384 == 0 else hidden
    t_tile = 512
    out = jax.ShapeDtypeStruct((hidden, count), bf16)
    return pl.pallas_call(
        ffn_kernel,
        grid=(hidden // h_tile, count // t_tile),
        in_specs=[
            pl.BlockSpec((3, h_tile, width), lambda i, j: (0, i, 0)),
            pl.BlockSpec((t_tile, width), lambda i, j: (j, 0)),
            pl.BlockSpec((t_tile, width), lambda i, j: (j, 0)),
        ],
        out_specs=[pl.BlockSpec((h_tile, t_tile), lambda i, j: (i, j))] * 3,
        out_shape=[out] * 3,
        compiler_params=pltpu.CompilerParams(vmem_limit_bytes=40 * 2**20),
        cost_estimate=pl.CostEstimate(
            flops=6 * hidden * count * width, bytes_accessed=30 * 10**6, transcendentals=hidden * count
        ),
        name="ffn_hidden",
    )(weights, rows, cot)


def ring(size):
    return [(i, (i + 1) % size) for i in range(size)]


def swap(value, axis):
    return lax.ppermute(value, axis, [(0, 1), (1, 0)])


def gather_parts(value, axis, size):
    at = lax.axis_index(axis)
    if size > 4:
        full = lax.all_gather(value, axis, axis=0)
        return [(i, full[i]) for i in range(size)]
    parts = [(at, value)]
    for step in range(1, size):
        value = lax.ppermute(value, axis, ring(size))
        parts.append(((at - step) % size, value))
    return parts


def assemble(shape, blocks):
    full = jnp.zeros(shape, bf16)
    for start, value in blocks:
        full = lax.dynamic_update_slice(full, value, start)
    return full


def by_index(index, first, second, axis):
    return jnp.where(
        index == 0,
        jnp.concatenate([first, second], axis=axis),
        jnp.concatenate([second, first], axis=axis),
    )


def lane_block(value, index, width):
    start = [0] * (value.ndim - 1) + [index * width]
    return lax.dynamic_slice(value, start, (*value.shape[:-1], width))


def plus(left, right):
    return left.astype(f32) + right.astype(f32)


def scatter_ring(pick, axis, size):
    total = pick(1) if size > 1 else pick(0)
    for step in range(size - 1):
        arrived = lax.ppermute(total.astype(bf16), axis, ring(size))
        total = plus(arrived, pick((step + 2) % size))
    return total


def scatter_axis(block_of, axis, size):
    at = lax.axis_index(axis)
    if size > 4:
        stacked = jnp.stack([block_of(i) for i in range(size)]).astype(bf16)
        return lax.psum_scatter(stacked, axis, scatter_dimension=0, tiled=False).astype(f32)
    return scatter_ring(lambda i: block_of((at - i) % size), axis, size)


def shards(
    sizes,
    tokens,
    segments,
    cotangent,
    attn_gain,
    q_weight,
    k_weight,
    v_weight,
    query_gain,
    key_gain,
    o_weight,
    ffn_gain,
    gate_weight,
    up_weight,
    down_weight,
):
    y_size, x_size, c_size, z_size = sizes
    y, x, c, z = (lax.axis_index(name) for name in "yxcz")
    own_rows, width = tokens.shape
    part = q_weight.shape[0]
    parts = width // part
    head = query_gain.shape[0] * parts
    gain_part = query_gain.shape[0]
    seq_count, length = segments.shape

    pairs = []
    for low in range(0, z_size, 2):
        pairs += [(z_size + low, low + 1), (low + 1, z_size + low)]
    trades = (c + z) % 2 == 1

    def trade(value):
        return jnp.where(trades, lax.ppermute(value, ("c", "z"), pairs), value)

    qt, kt, vt, ot = q_weight.T, k_weight.T, v_weight.T, o_weight.T
    q_rows, k_rows = qt.shape[0] // 2, kt.shape[0] // 2
    gain_rows = jnp.concatenate(
        [attn_gain[None], ffn_gain[None]]
        + [jnp.pad(g, (0, part - gain_part))[None] for g in (query_gain, key_gain)]
        + [jnp.zeros((12, part), bf16)],
        axis=0,
    )
    qkv_pack = jnp.concatenate(
        [v.reshape(2, -1, part) for v in (qt, kt, vt)]
        + [jnp.broadcast_to(gain_rows, (2, 16, part))],
        axis=1,
    )
    o_pack = ot.reshape(2, q_rows, part)

    def core_join(pack):
        mine = lax.dynamic_index_in_dim(pack, c, 0, keepdims=False)
        other = lax.dynamic_index_in_dim(pack, 1 - c, 0, keepdims=False)
        return by_index(c, mine, swap(other, "c"), -1)

    qkv_own = core_join(qkv_pack)
    o_own = core_join(o_pack)
    qkv_rows = q_rows + 2 * k_rows
    qkv_block, o_block, gain_block = [], [], []
    for slot, (_, piece) in enumerate(gather_parts(qkv_own[:qkv_rows], "z", z_size)):
        if slot == 0:
            piece = qkv_own
        for y_at, y_piece in gather_parts(piece, "y", y_size):
            for x_at, x_piece in gather_parts(y_piece, "x", x_size):
                lane = (y_at * x_size + x_at) * c_size * part
                if slot == 0:
                    gain_block.append(((0, lane), x_piece[qkv_rows:]))
                    x_piece = x_piece[:qkv_rows]
                qkv_block.append(((slot * qkv_rows, lane), x_piece))
    for slot, (_, piece) in enumerate(gather_parts(o_own, "z", z_size)):
        for y_at, y_piece in gather_parts(piece, "y", y_size):
            for x_at, x_piece in gather_parts(y_piece, "x", x_size):
                o_block.append(((slot * q_rows, (y_at * x_size + x_at) * c_size * part), x_piece))
    qkv_full = assemble((z_size * qkv_rows, width), qkv_block)
    o_full = assemble((z_size * q_rows, width), o_block)
    gains = assemble((16, width), gain_block).astype(f32)
    gain_one, gain_two = gains[0:1], gains[1:2]
    gain_query, gain_key = (
        gains[i].reshape(parts, part)[:, :gain_part].reshape(1, head) for i in (2, 3)
    )
    head_gains = jnp.concatenate(
        [jnp.tile(gain_query, (1, 2)), jnp.tile(gain_key, (1, 2)), jnp.zeros((6, 2 * head), f32)], axis=0
    )

    sub = gate_weight.shape[1] // (x_size * c_size)
    ffn_pack = jnp.stack([gate_weight.T, up_weight.T, down_weight.T]).reshape(
        3, x_size, c_size, sub, part
    )
    mine = lax.dynamic_index_in_dim(ffn_pack, c, 2, keepdims=False)
    other = lax.dynamic_index_in_dim(ffn_pack, 1 - c, 2, keepdims=False)
    ffn_pack = by_index(c, mine, swap(other, "c"), -1)
    mine = lax.dynamic_index_in_dim(ffn_pack, x, 1, keepdims=False)
    other = lax.dynamic_index_in_dim(ffn_pack, 1 - x, 1, keepdims=False)
    ffn_own = by_index(x, mine, swap(other, "x"), -1)
    ffn_block = []
    quad = x_size * c_size * part
    for slot, (_, piece) in enumerate(gather_parts(ffn_own, "z", z_size)):
        for y_at, y_piece in gather_parts(piece, "y", y_size):
            ffn_block.append(((0, slot * sub, y_at * quad), y_piece))
    ffn_full = assemble((3, z_size * sub, width), ffn_block)

    tokens = trade(tokens)
    cotangent = trade(cotangent)
    other_segments = swap(segments, "c")
    segment = lax.dynamic_index_in_dim(
        jnp.where(c == z % 2, segments, other_segments), z // 2, 0, keepdims=False
    )
    place = lax.broadcasted_iota(jnp.int32, (length,), 0) - jnp.sum(
        (segment[None, :] < segment[:, None]).astype(jnp.int32), axis=1
    )
    frequency = theta_base ** (-2.0 * jnp.arange(head // 2, dtype=f32) / head)
    angles = place.astype(f32)[:, None] * frequency
    cosine, sine = jnp.cos(angles), jnp.sin(angles)
    cosine = jnp.concatenate([cosine] * 4, axis=1)
    sine = jnp.concatenate([-sine, sine] * 2, axis=1)
    seg_col, seg_row = segment[:, None], segment[None, :]

    inputs = tokens.astype(f32)
    root_one = lax.rsqrt(jnp.mean(inputs * inputs, axis=-1, keepdims=True) + epsilon)
    hat_one = inputs * root_one
    normed_own = (hat_one * gain_one).astype(bf16)
    normed_one = by_index(c, normed_own, swap(normed_own, "c"), 0)
    qkv = dot(normed_one, qkv_full, 1, 1)
    context = attend(qkv, cosine, sine, seg_col, seg_row, head_gains, head)

    def half_rows(value, index):
        return lax.dynamic_slice_in_dim(value, index * own_rows, own_rows, 0)

    def core_reduce(left, right, right_dim):
        sent = dot(half_rows(left, 1 - c), right, 1, right_dim).astype(bf16)
        kept = dot(half_rows(left, c), right, 1, right_dim)
        return kept + swap(sent, "c").astype(f32)

    mid = inputs + core_reduce(context, o_full, 0)
    root_two = lax.rsqrt(jnp.mean(mid * mid, axis=-1, keepdims=True) + epsilon)
    hat_two = mid * root_two
    normed_two = (hat_two * gain_two).astype(bf16)

    def spread(value):
        across = swap(value, "x")
        return jnp.concatenate([value, swap(value, "c"), across, swap(across, "c")], axis=0)

    def collect(value):
        quarter = [value[i * own_rows : (i + 1) * own_rows] for i in range(4)]
        across = plus(quarter[2], swap(quarter[3], "c")).astype(bf16)
        return plus(quarter[0], swap(quarter[1], "c")) + swap(across, "x").astype(f32)

    rows_two = spread(normed_two)
    back_rows = spread(cotangent)
    hidden, gate_grad, up_grad = ffn_hidden(ffn_full, rows_two, back_rows)
    ffn_back = (dot(gate_grad, ffn_full[0], 0, 0) + dot(up_grad, ffn_full[1], 0, 0)).astype(bf16)
    ffn_part = dot(hidden, ffn_full[2], 0, 0).astype(bf16)
    grad_normed_two = collect(ffn_back)
    output = (mid + collect(ffn_part)).astype(bf16)
    wgrads = jnp.stack(
        [
            dot(gate_grad, rows_two, 1, 0).astype(bf16),
            dot(up_grad, rows_two, 1, 0).astype(bf16),
            dot(hidden, back_rows, 1, 0).astype(bf16),
        ]
    )
    wgrads = scatter_axis(lambda i: lane_block(wgrads, i, quad), "y", y_size)
    wgrads = wgrads.astype(bf16)
    wgrads = scatter_ring(lambda i: wgrads[:, i * sub : (i + 1) * sub], "z", z_size).astype(bf16)
    kept = lane_block(wgrads, x, c_size * part)
    sent = swap(lane_block(wgrads, 1 - x, c_size * part), "x")
    wgrads = jnp.where(x == 0, jnp.stack([kept, sent], 1), jnp.stack([sent, kept], 1))
    kept = lane_block(wgrads, c, part)
    sent = swap(lane_block(wgrads, 1 - c, part), "c")
    wgrads = jnp.where(c == 0, jnp.stack([kept, sent], 2), jnp.stack([sent, kept], 2))
    wgrads = wgrads.reshape(3, x_size * c_size * sub, part)
    gate_wgrad, up_wgrad, down_wgrad = (wgrads[i].astype(f32).T for i in range(3))

    def norm_back(grad, hat, root):
        return root * (grad - hat * jnp.mean(grad * hat, axis=-1, keepdims=True))

    gain_two_part = jnp.sum(grad_normed_two * hat_two, axis=0)
    grad_mid = cotangent.astype(f32) + norm_back(grad_normed_two * gain_two, hat_two, root_two)

    branch_own = grad_mid.astype(bf16)
    branch = by_index(c, branch_own, swap(branch_own, "c"), 0)
    grad_context = dot(branch, o_full, 1, 1).astype(bf16)
    o_grad = dot(context, branch, 0, 0).astype(bf16)
    grad_qkv, head_sums = attend_back(
        qkv, cosine, sine, seg_col, seg_row, head_gains, grad_context, head
    )
    head_sums = jnp.sum(head_sums.reshape(-1, 8, 2 * head), axis=0)
    gain_query_part = head_sums[0, :head] + head_sums[0, head:]
    gain_key_part = head_sums[1, :head]
    grad_normed_one = core_reduce(grad_qkv, qkv_full, 0)
    qkv_grad = dot(grad_qkv, normed_one, 0, 0).astype(bf16)

    def attn_scatter(value, rows):
        pair = c_size * part
        per_y = []
        for y_at in range(y_size):
            sent = swap(lane_block(value, y_at * x_size + 1 - x, pair), "x")
            per_y.append(plus(lane_block(value, y_at * x_size + x, pair), sent).astype(bf16))
        joined = jnp.stack(per_y)
        value = scatter_axis(
            lambda i: lax.dynamic_index_in_dim(joined, i, 0, keepdims=False), "y", y_size
        ).astype(bf16)
        value = scatter_ring(lambda i: value[i * rows : (i + 1) * rows], "z", z_size).astype(bf16)
        kept = lane_block(value, c, part)
        sent = swap(lane_block(value, 1 - c, part), "c")
        return jnp.where(c == 0, jnp.stack([kept, sent]), jnp.stack([sent, kept])).astype(f32)

    o_wgrad = attn_scatter(o_grad, q_rows).reshape(2 * q_rows, part).T
    qkv_grad = attn_scatter(qkv_grad, qkv_rows)
    q_wgrad = qkv_grad[:, :q_rows].reshape(-1, part).T
    k_wgrad = qkv_grad[:, q_rows : q_rows + k_rows].reshape(-1, part).T
    v_wgrad = qkv_grad[:, q_rows + k_rows :].reshape(-1, part).T

    gain_one_part = jnp.sum(grad_normed_one * hat_one, axis=0)
    tokens_grad = (grad_mid + norm_back(grad_normed_one * gain_one, hat_one, root_one)).astype(bf16)
    sums = lax.psum(
        jnp.concatenate([gain_one_part, gain_two_part, gain_query_part, gain_key_part]),
        ("y", "x", "c", "z"),
    )
    mine = (y * x_size + x) * c_size + c
    gain_one_sum = lax.dynamic_slice(sums, (mine * part,), (part,))
    gain_two_sum = lax.dynamic_slice(sums, (width + mine * part,), (part,))
    gain_query_sum = lax.dynamic_slice(sums, (2 * width + mine * gain_part,), (gain_part,))
    gain_key_sum = lax.dynamic_slice(sums, (2 * width + head + mine * gain_part,), (gain_part,))
    return (
        trade(output),
        trade(tokens_grad),
        gain_one_sum,
        q_wgrad,
        k_wgrad,
        v_wgrad,
        gain_query_sum,
        gain_key_sum,
        o_wgrad,
        gain_two_sum,
        gate_wgrad,
        up_wgrad,
        down_wgrad,
    )


def solution(mesh):
    dp, tp = mesh.devices.shape
    sizes = (dp // 4, 2, 2, tp)
    fine = Mesh(mesh.devices.reshape(sizes), ("y", "x", "c", "z"))
    d = ("y", "x", "c")
    rows, weight, gain = P((*d, "z"), None), P(d, "z"), P(d)
    return jax.shard_map(
        functools.partial(shards, sizes),
        mesh=fine,
        in_specs=(rows, P(d, None), rows, gain, weight, weight, weight, gain, gain, weight, gain)
        + (weight,) * 3,
        out_specs=(rows, rows, gain, weight, weight, weight, gain, gain, weight, gain) + (weight,) * 3,
        check_vma=False,
    )
```

time: 1380 us -> 602 us (0.44)
  waiting for transfers between devices: 841 us -> 225 us
  matrix products: 228 us -> 73.4 us
  starting transfers between devices: 0.77 us -> 81.2 us
  Pallas kernels: 0 us -> 56.9 us
  local copies, waits for them, and re-layouts: 113 us -> 57 us
  blocking collectives: 93.4 us -> 50.1 us
  other arithmetic: 68.8 us -> 47.9 us
  between operations: 19.1 us -> 2.4 us
    reduce_scatter x11 -> x0, waiting for transfers between devices: 553 us -> none  [the longest x1 133 us: shards(): lax.psum_scatter(attn_part, 'tp', scatter_dimension=0, tiled=True)]
    all_gather x7 -> x0, waiting for transfers between devices: 286 us -> none  [the longest x1 81.8 us: shards(): back_rows = lax.all_gather(cotangent, 'tp', axis=0, tiled=True)]
    ppermute x0 -> x82, waiting for transfers between devices: none -> 225 us  [the longest x37 98.8 us: gather_parts(): value = lax.ppermute(value, axis, ring(size))]
    dot_general x35 -> x14, matrix products: 228 us -> 73.4 us  [dot(): lax.dot_general(left, right, (((left_dim,), (right_dim,)), ((), ())), pre...]
    ppermute x0 -> x82, starting transfers between devices: none -> 81.2 us  [the longest x29 33.3 us: swap(): return lax.ppermute(value, axis, [(0, 1), (1, 0)])]
    all_gather x6 -> x0, blocking collectives: 59.5 us -> none  [the longest x1 11 us: shards(): lax.all_gather(k_weight, 'dp', axis=0, tiled=True)]
    pallas_call x0 -> x3, Pallas kernels: none -> 56.9 us  [the longest x1 23.5 us: attend_back(): pl.pallas_call(functools.partial(attend_back_kernel, head), grid=(groups,...]
    psum x1, blocking collectives: 9.93 us -> 50.1 us  [shards(): lax.psum(jnp.concatenate([gain_one_part, gain_two_part, gain_query_part,...]
  transfers between devices with their start and end apart: 18 -> 82, of which waited for: 16 -> 30; matrix products, arithmetic and copies ran while one was open for 22% -> 26% of each run, Pallas kernels for 0% -> 6%
where the time goes in v1:
time: 602 us; the launch traced here: 594 us
  waiting for transfers between devices  225 us (37%)
  starting transfers between devices  81.2 us (13%)
  matrix products  73.4 us (12%)
  local copies, waits for them, and re-layouts  57 us (9%)
  Pallas kernels  56.9 us (9%)
  blocking collectives  50.1 us (8%)
  other arithmetic  47.9 us (8%)
    ppermute x37, waiting for transfers between devices, gather_parts(): value = lax.ppermute(value, axis, ring(size))  98.8 us
    ppermute x12, waiting for transfers between devices, scatter_ring(): arrived = lax.ppermute(total.astype(bf16), axis, ring(size))  85.8 us
    dot_general x14, matrix products, dot(): lax.dot_general(left, right, (((left_dim,), (right_dim,)), ((), ())), pre...  73.4 us
    psum x1, blocking collectives, shards(): lax.psum(jnp.concatenate([gain_one_part, gain_two_part, gain_query_part,...  50.1 us
    ppermute x29, waiting for transfers between devices, swap(): return lax.ppermute(value, axis, [(0, 1), (1, 0)])  40.2 us
    ppermute x29, starting transfers between devices, swap(): return lax.ppermute(value, axis, [(0, 1), (1, 0)])  33.3 us
    dynamic_update_slice x41, local copies, waits for them, and re-layouts, assemble(): full = lax.dynamic_update_slice(full, value, start)  26 us
    pallas_call x1, Pallas kernels, attend_back(): pl.pallas_call(functools.partial(attend_back_kernel, head), grid=(groups,...  23.5 us
  transfers between devices with their start and end apart: 82, of which 30 were waited for; matrix products, arithmetic and copies ran while one was open for 26% of the time, Pallas kernels for 6%

profile of v1, /device:TPU:1, one launch (start us, length us, event | category | flops | bytes accessed | tf_op | source)
XLA Modules:
  0.0 593.8 jit_solution(9947524320988641882)
XLA Ops:
  5.7 4.5 collective-permute-start
  59.8 11.0 %collective-permute-start.48 = (bf16[512,1024]{1,0:T(8,128)(2,1)}, bf16[512,1024]{1,0:T(8,128)(2,1)}, u32[]{:S(2)}, u32[]{:S(2)}) collective-permute-start(bf16[512,1024]{1,0:T(8,128)(2,1)} %param.16), channel_id=1, source_target_pairs={{4,1},{1,4},{6,3},{3,6},{12,9},{9,12},{14,11},{11,14},{20,17},{17,... | collective-permute-start | bytes 3145736 | tf_op jit(solution)/shard_map/ppermute | solution.py:348
  80.0 5.7 collective-permute-done.10
  103.2 7.1 %collective-permute-done.13 = bf16[256,256]{1,0:T(8,128)(2,1)S(1)} collective-permute-done((bf16[256,256]{1,0:T(8,128)(2,1)S(1)}, bf16[256,256]{1,0:T(8,128)(2,1)S(1)}, u32[]{:S(2)}, u32[]{:S(2)}) %collective-permute-start.13) | collective-permute-done | bytes 131104 | tf_op jit(solution)/shard_map/ppermute | solution.py:271
  122.5 10.8 %attend.1 = bf16[1024,512]{1,0:T(8,128)(2,1)S(1)} custom-call(f32[1024,1024]{1,0:T(8,128)S(1)} %fusion.28.qkv_ref, f32[1024,128]{1,0:T(8,128)S(1)} %get-tuple-element.141.cos_ref, f32[1024,128]{1,0:T(8,128)S(1)} %get-tuple-element.142.sin_ref, s32[1024,1]{1,0:T(8,128)S(1)} %copy.98.seg_col, s32[1,1024]{1,0:T(1,128)S(1)} %broadcast_select_fusion.4.seg_row, ...), custom_call_target="tpu_custom_call" | custom-call | flops 12000000000 | bytes 8000000 | tf_op jit(solution)/shard_map/attend/pallas_call | solution.py:108
  147.5 19.0 %collective-permute-done.39 = bf16[3,288,512]{2,1,0:T(8,128)(2,1)S(1)} collective-permute-done((bf16[3,288,512]{2,1,0:T(8,128)(2,1)}, bf16[3,288,512]{2,1,0:T(8,128)(2,1)S(1)}, u32[]{:S(2)}, u32[]{:S(2)}) %collective-permute-start.39) | collective-permute-done | bytes 884768 | tf_op jit(solution)/shard_map/ppermute | solution.py:271
  172.5 16.3 %collective-permute-done.41 = bf16[3,288,512]{2,1,0:T(8,128)(2,1)} collective-permute-done((bf16[3,288,512]{2,1,0:T(8,128)(2,1)S(1)}, bf16[3,288,512]{2,1,0:T(8,128)(2,1)}, u32[]{:S(2)}, u32[]{:S(2)}) %collective-permute-start.41) | collective-permute-done | bytes 884768 | tf_op jit(solution)/shard_map/ppermute | solution.py:271
  195.3 15.4 %collective-permute-done.43 = bf16[3,288,512]{2,1,0:T(8,128)(2,1)} collective-permute-done((bf16[3,288,512]{2,1,0:T(8,128)(2,1)}, bf16[3,288,512]{2,1,0:T(8,128)(2,1)}, u32[]{:S(2)}, u32[]{:S(2)}) %collective-permute-start.43) | collective-permute-done | bytes 884768 | tf_op jit(solution)/shard_map/ppermute | solution.py:271
  224.3 5.1 collective-permute-done.44
  232.4 22.6 %ffn_hidden.1 = (bf16[1152,2048]{1,0:T(8,128)(2,1)S(1)}, bf16[1152,2048]{1,0:T(8,128)(2,1)}, bf16[1152,2048]{1,0:T(8,128)(2,1)}) custom-call(bf16[3,1152,1024]{2,1,0:T(8,128)(2,1)} %constant_dynamic-update-slice_fusion.w_ref, bf16[2048,1024]{1,0:T(8,128)(2,1)S(1)} %pad_maximum_fusion.1.rows_ref, bf16[2048,1024]{1,0:T(8,128)(2,1)S(1)} %pad_maximum_fusion.2.cot_ref), custom_call_target="tpu_custom_call" | custom-call | flops 14495514624 | bytes 30000000 | tf_op jit(solution)/shard_map/ffn_hidden/pallas_call | solution.py:238
  255.0 7.8 %convolution_convert_fusion.3 = bf16[2048,1024]{1,0:T(8,128)(2,1)S(1)} fusion(bf16[1152,2048]{1,0:T(8,128)(2,1)S(1)} %get-tuple-element.18, bf16[3,1152,1024]{2,1,0:T(8,128)(2,1)} %constant_dynamic-update-slice_fusion.w_ref), kind=kOutput, calls=%fused_computation.9 | convolution fusion | flops 4833935360 | bytes 11272192 | tf_op jit(solution)/shard_map/dot_general | solution.py:19
  266.7 9.7 %fusion.7 = f32[2048,1024]{1,0:T(8,128)} fusion(bf16[1152,2048]{1,0:T(8,128)(2,1)S(1)} %copy-done.37, bf16[3,1152,1024]{2,1,0:T(8,128)(2,1)} %constant_dynamic-update-slice_fusion.w_ref), kind=kOutput, calls=%fused_computation.21 | convolution fusion | flops 4831838208 | bytes 15466496 | tf_op jit(solution)/shard_map/dot_general | solution.py:19
  276.4 9.9 %add_convert_fusion = bf16[2048,1024]{1,0:T(8,128)(2,1)S(1)} fusion(f32[2048,1024]{1,0:T(8,128)} %fusion.7, bf16[1152,2048]{1,0:T(8,128)(2,1)} %get-tuple-element.19, bf16[3,1152,1024]{2,1,0:T(8,128)(2,1)} %constant_dynamic-update-slice_fusion.w_ref), kind=kOutput, calls=%fused_computation | convolution fusion | flops 4836032512 | bytes 19660800 | tf_op jit(solution)/shard_map/dot_general | solution.py:19
  287.0 8.1 %fusion = bf16[1,1152,1024]{2,1,0:T(8,128)(2,1)S(1)} fusion(bf16[1152,2048]{1,0:T(8,128)(2,1)} %get-tuple-element.19, bf16[512,1024]{1,0:T(8,128)(2,1)S(1)} %collective-permute-done.47, bf16[512,1024]{1,0:T(8,128)(2,1)} %collective-permute-done.46, bf16[512,1024]{1,0:T(8,128)(2,1)S(1)} %collective-permute-done.45, bf16[512,1024]{1,0:T(8,128)(2,1)} %multiply_convert_fusion), kind=kOutput, calls=%fused_computation.10 | convolution fusion | flops 4849795072 | bytes 11272192 | tf_op jit(solution)/shard_map/dot_general | solution.py:19
  295.2 9.1 %fusion.1 = bf16[1,1152,1024]{2,1,0:T(8,128)(2,1)} fusion(bf16[1152,2048]{1,0:T(8,128)(2,1)} %get-tuple-element.20, bf16[512,1024]{1,0:T(8,128)(2,1)S(1)} %collective-permute-done.47, bf16[512,1024]{1,0:T(8,128)(2,1)} %collective-permute-done.46, bf16[512,1024]{1,0:T(8,128)(2,1)S(1)} %collective-permute-done.45, bf16[512,1024]{1,0:T(8,128)(2,1)} %multiply_convert_fusion), kind=kOutput, calls=%fused_computation.11 | convolution fusion | flops 4849795072 | bytes 11272192 | tf_op jit(solution)/shard_map/dot_general | solution.py:19
  306.7 7.9 %fusion.2 = bf16[1,1152,1024]{2,1,0:T(8,128)(2,1)} fusion(bf16[1152,2048]{1,0:T(8,128)(2,1)S(1)} %get-tuple-element.18, bf16[512,1024]{1,0:T(8,128)(2,1)} %collective-permute-done.51, bf16[512,1024]{1,0:T(8,128)(2,1)} %collective-permute-done.50, bf16[512,1024]{1,0:T(8,128)(2,1)} %collective-permute-done.49, bf16[512,1024]{1,0:T(8,128)(2,1)} %broadcast_select_fusion.2), kind=kOutput, calls=%fused_computation.12 | convolution fusion | flops 4849795072 | bytes 11272192 | tf_op jit(solution)/shard_map/dot_general | solution.py:19
  314.6 36.9 %collective-permute-done.58 = bf16[512,1024]{1,0:T(8,128)(2,1)S(1)} collective-permute-done((bf16[512,1024]{1,0:T(8,128)(2,1)S(1)}, bf16[512,1024]{1,0:T(8,128)(2,1)S(1)}, u32[]{:S(2)}, u32[]{:S(2)}) %collective-permute-start.58) | collective-permute-done | bytes 1048608 | tf_op jit(solution)/shard_map/ppermute | solution.py:261
  367.6 23.5 %attend_back.1 = (bf16[1024,1024]{1,0:T(8,128)(2,1)S(1)}, f32[32,128]{1,0:T(8,128)S(1)}) custom-call(f32[1024,1024]{1,0:T(8,128)} %copy-done.2, f32[1024,128]{1,0:T(8,128)S(1)} %get-tuple-element.141.cos_ref, f32[1024,128]{1,0:T(8,128)S(1)} %get-tuple-element.142.sin_ref, s32[1024,1]{1,0:T(8,128)S(1)} %copy.98.seg_col, ...), custom_call_target="tpu_custom_call" | custom-call | flops 30000001024 | bytes 10000000 | tf_op jit(solution)/shard_map/attend_back/pallas_call | solution.py:193
  404.1 40.5 %collective-permute-done.71 = bf16[512,256]{1,0:T(8,128)(2,1)S(1)} collective-permute-done((bf16[512,256]{1,0:T(8,128)(2,1)S(1)}, bf16[512,256]{1,0:T(8,128)(2,1)S(1)}, u32[]{:S(2)}, u32[]{:S(2)}) %collective-permute-start.71) | collective-permute-done | bytes 262176 | tf_op jit(solution)/shard_map/ppermute | solution.py:303
  444.9 4.8 collective-permute-done.72
  456.5 20.6 %collective-permute-done.74 = bf16[128,256]{1,0:T(8,128)(2,1)S(1)} collective-permute-done((bf16[128,256]{1,0:T(8,128)(2,1)S(1)}, bf16[128,256]{1,0:T(8,128)(2,1)S(1)}, u32[]{:S(2)}, u32[]{:S(2)}) %collective-permute-start.74) | collective-permute-done | bytes 65568 | tf_op jit(solution)/shard_map/ppermute | solution.py:303
  487.8 7.0 %collective-permute-done.64 = bf16[1024,256]{1,0:T(8,128)(2,1)} collective-permute-done((bf16[1024,256]{1,0:T(8,128)(2,1)}, bf16[1024,256]{1,0:T(8,128)(2,1)}, u32[]{:S(2)}, u32[]{:S(2)}) %collective-permute-start.64) | collective-permute-done | bytes 524320 | tf_op jit(solution)/shard_map/ppermute | solution.py:303
  496.2 10.6 %collective-permute-done.78 = bf16[3,288,512]{2,1,0:T(8,128)(2,1)S(1)} collective-permute-done((bf16[3,288,512]{2,1,0:T(8,128)(2,1)S(1)}, bf16[3,288,512]{2,1,0:T(8,128)(2,1)S(1)}, u32[]{:S(2)}, u32[]{:S(2)}) %collective-permute-start.78) | collective-permute-done | bytes 884768 | tf_op jit(solution)/shard_map/ppermute | solution.py:303
  515.0 50.1 %psum.7 = f32[2176]{0:T(1024)S(1)} all-reduce(f32[2176]{0:T(1024)S(1)} %concatenate.80), channel_id=1, replica_groups=mesh['y'=2,'x'=2,'c'=2,'z'=4] {'y','x','c','z'}, use_global_device_ids=true, to_apply=%region_8.9 | all-reduce | flops 2176 | bytes 17408 | tf_op jit(solution)/shard_map/psum | solution.py:530
  (387 shorter events, 227.3 us)
Async XLA Ops:
  5.7 83.6 %collective-permute-start = (bf16[512,1024]{1,0:T(8,128)(2,1)}, bf16[512,1024]{1,0:T(8,128)(2,1)}, u32[]{:S(2)}, u32[]{:S(2)}) collective-permute-start(bf16[512,1024]{1,0:T(8,128)(2,1)} %param.14), channel_id=1, source_target_pairs={{4,1},{1,4},{6,3},{3,6},{12,9},{9,12},{14,11},{11,14},{20,17},{17,... | collective-permute-start | bytes 3145736 | tf_op jit(solution)/shard_map/ppermute | solution.py:348
  14.6 72.5 %collective-permute-start.36 = (bf16[3,2,288,128]{3,2,1,0:T(8,128)(2,1)S(1)}, bf16[3,2,288,128]{3,2,1,0:T(8,128)(2,1)}, u32[]{:S(2)}, u32[]{:S(2)}) collective-permute-start(bf16[3,2,288,128]{3,2,1,0:T(8,128)(2,1)S(1)} %get-tuple-element.110), channel_id=1, source_target_pairs={{0,4},{4,0},{1,5},{5,1},{2,6},{6,2},{3,7},{7,3},{8,12},{12,8},{9,1... | collective-permute-start | bytes 1327112 | tf_op jit(solution)/shard_map/ppermute | solution.py:261
  59.8 84.1 %collective-permute-start.48 = (bf16[512,1024]{1,0:T(8,128)(2,1)}, bf16[512,1024]{1,0:T(8,128)(2,1)}, u32[]{:S(2)}, u32[]{:S(2)}) collective-permute-start(bf16[512,1024]{1,0:T(8,128)(2,1)} %param.16), channel_id=1, source_target_pairs={{4,1},{1,4},{6,3},{3,6},{12,9},{9,12},{14,11},{11,14},{20,17},{17,... | collective-permute-start | bytes 3145736 | tf_op jit(solution)/shard_map/ppermute | solution.py:348
  95.7 41.0 %collective-permute-start.37 = (bf16[3,288,256]{2,1,0:T(8,128)(2,1)S(1)}, bf16[3,288,256]{2,1,0:T(8,128)(2,1)}, u32[]{:S(2)}, u32[]{:S(2)}) collective-permute-start(bf16[3,288,256]{2,1,0:T(8,128)(2,1)S(1)} %get-tuple-element.107), channel_id=1, source_target_pairs={{0,8},{8,0},{1,9},{9,1},{2,10},{10,2},{3,11},{11,3},{4,12},{12,4},... | collective-permute-start | bytes 1327112 | tf_op jit(solution)/shard_map/ppermute | solution.py:261
  135.0 31.4 %collective-permute-start.35 = (bf16[512,1024]{1,0:T(8,128)(2,1)}, bf16[512,1024]{1,0:T(8,128)(2,1)}, u32[]{:S(2)}, u32[]{:S(2)}) collective-permute-start(bf16[512,1024]{1,0:T(8,128)(2,1)} %convolution_convert_fusion.8), channel_id=1, source_target_pairs={{0,4},{4,0},{1,5},{5,1},{2,6},{6,2},{3,7},{7,3},{8,12},{12,8},{9,1... | collective-permute-start | bytes 3145736 | tf_op jit(solution)/shard_map/ppermute | solution.py:261
  146.2 42.9 %collective-permute-start.50 = (bf16[512,1024]{1,0:T(8,128)(2,1)}, bf16[512,1024]{1,0:T(8,128)(2,1)}, u32[]{:S(2)}, u32[]{:S(2)}) collective-permute-start(bf16[512,1024]{1,0:T(8,128)(2,1)} %broadcast_select_fusion.2), channel_id=1, source_target_pairs={{0,8},{8,0},{1,9},{9,1},{2,10},{10,2},{3,11},{11,3},{4,12},{12,4},... | collective-permute-start | bytes 3145736 | tf_op jit(solution)/shard_map/ppermute | solution.py:261
  146.9 44.0 %collective-permute-start.49 = (bf16[512,1024]{1,0:T(8,128)(2,1)}, bf16[512,1024]{1,0:T(8,128)(2,1)}, u32[]{:S(2)}, u32[]{:S(2)}) collective-permute-start(bf16[512,1024]{1,0:T(8,128)(2,1)} %broadcast_select_fusion.2), channel_id=1, source_target_pairs={{0,4},{4,0},{1,5},{5,1},{2,6},{6,2},{3,7},{7,3},{8,12},{12,8},{9,1... | collective-permute-start | bytes 3145736 | tf_op jit(solution)/shard_map/ppermute | solution.py:261
  171.2 40.2 %collective-permute-start.46 = (bf16[512,1024]{1,0:T(8,128)(2,1)}, bf16[512,1024]{1,0:T(8,128)(2,1)}, u32[]{:S(2)}, u32[]{:S(2)}) collective-permute-start(bf16[512,1024]{1,0:T(8,128)(2,1)} %multiply_convert_fusion), channel_id=1, source_target_pairs={{0,8},{8,0},{1,9},{9,1},{2,10},{10,2},{3,11},{11,3},{4,12},{12,4},... | collective-permute-start | bytes 3145736 | tf_op jit(solution)/shard_map/ppermute | solution.py:261
  194.9 35.6 %collective-permute-start.45 = (bf16[512,1024]{1,0:T(8,128)(2,1)}, bf16[512,1024]{1,0:T(8,128)(2,1)S(1)}, u32[]{:S(2)}, u32[]{:S(2)}) collective-permute-start(bf16[512,1024]{1,0:T(8,128)(2,1)} %multiply_convert_fusion), channel_id=1, source_target_pairs={{0,4},{4,0},{1,5},{5,1},{2,6},{6,2},{3,7},{7,3},{8,12},{12,8},{9,1... | collective-permute-start | bytes 3145736 | tf_op jit(solution)/shard_map/ppermute | solution.py:261
  263.1 41.2 %collective-permute-start.53 = (bf16[512,1024]{1,0:T(8,128)(2,1)S(1)}, bf16[512,1024]{1,0:T(8,128)(2,1)S(1)}, u32[]{:S(2)}, u32[]{:S(2)}) collective-permute-start(bf16[512,1024]{1,0:T(8,128)(2,1)S(1)} %get-tuple-element.90), channel_id=1, source_target_pairs={{0,4},{4,0},{1,5},{5,1},{2,6},{6,2},{3,7},{7,3},{8,12},{12,8},{9,1... | collective-permute-start | bytes 3145736 | tf_op jit(solution)/shard_map/ppermute | solution.py:261
  266.6 85.8 %collective-permute-start.52 = (bf16[512,1024]{1,0:T(8,128)(2,1)S(1)}, bf16[512,1024]{1,0:T(8,128)(2,1)S(1)}, u32[]{:S(2)}, u32[]{:S(2)}) collective-permute-start(bf16[512,1024]{1,0:T(8,128)(2,1)S(1)} %get-tuple-element.89), channel_id=1, source_target_pairs={{0,4},{4,0},{1,5},{5,1},{2,6},{6,2},{3,7},{7,3},{8,12},{12,8},{9,1... | collective-permute-start | bytes 3145736 | tf_op jit(solution)/shard_map/ppermute | solution.py:261
  304.7 47.8 %collective-permute-start.54 = (bf16[512,1024]{1,0:T(8,128)(2,1)S(1)}, bf16[512,1024]{1,0:T(8,128)(2,1)S(1)}, u32[]{:S(2)}, u32[]{:S(2)}) collective-permute-start(bf16[512,1024]{1,0:T(8,128)(2,1)S(1)} %add_convert_fusion.4), channel_id=1, source_target_pairs={{0,8},{8,0},{1,9},{9,1},{2,10},{10,2},{3,11},{11,3},{4,12},{12,4},... | collective-permute-start | bytes 3145736 | tf_op jit(solution)/shard_map/ppermute | solution.py:261
  305.6 45.9 %collective-permute-start.58 = (bf16[512,1024]{1,0:T(8,128)(2,1)S(1)}, bf16[512,1024]{1,0:T(8,128)(2,1)S(1)}, u32[]{:S(2)}, u32[]{:S(2)}) collective-permute-start(bf16[512,1024]{1,0:T(8,128)(2,1)S(1)} %add_convert_fusion.2), channel_id=1, source_target_pairs={{0,8},{8,0},{1,9},{9,1},{2,10},{10,2},{3,11},{11,3},{4,12},{12,4},... | collective-permute-start | bytes 3145736 | tf_op jit(solution)/shard_map/ppermute | solution.py:261
  360.7 89.2 %collective-permute-start.76 = (bf16[3,1152,512]{2,1,0:T(8,128)(2,1)}, bf16[3,1152,512]{2,1,0:T(8,128)(2,1)}, u32[]{:S(2)}, u32[]{:S(2)}) collective-permute-start(bf16[3,1152,512]{2,1,0:T(8,128)(2,1)} %constant_dynamic-slice_fusion.3), channel_id=1, source_target_pairs={{0,16},{16,0},{1,17},{17,1},{2,18},{18,2},{3,19},{19,3},{4,20},{20... | collective-permute-start | bytes 10616840 | tf_op jit(solution)/shard_map/ppermute | solution.py:303
  361.3 39.5 %collective-permute-start.55 = (bf16[512,1024]{1,0:T(8,128)(2,1)S(1)}, bf16[512,1024]{1,0:T(8,128)(2,1)}, u32[]{:S(2)}, u32[]{:S(2)}) collective-permute-start(bf16[512,1024]{1,0:T(8,128)(2,1)S(1)} %get-tuple-element.95), channel_id=1, source_target_pairs={{4,1},{1,4},{6,3},{3,6},{12,9},{9,12},{14,11},{11,14},{20,17},{17,... | collective-permute-start | bytes 3145736 | tf_op jit(solution)/shard_map/ppermute | solution.py:348
  364.8 33.8 %collective-permute-start.69 = (bf16[512,256]{1,0:T(8,128)(2,1)S(1)}, bf16[512,256]{1,0:T(8,128)(2,1)S(1)}, u32[]{:S(2)}, u32[]{:S(2)}) collective-permute-start(bf16[512,256]{1,0:T(8,128)(2,1)S(1)} %get-tuple-element.99), channel_id=1, source_target_pairs={{0,8},{8,0},{1,9},{9,1},{2,10},{10,2},{3,11},{11,3},{4,12},{12,4},... | collective-permute-start | bytes 786440 | tf_op jit(solution)/shard_map/ppermute | solution.py:261
  365.5 33.9 %collective-permute-start.70 = (bf16[512,256]{1,0:T(8,128)(2,1)S(1)}, bf16[512,256]{1,0:T(8,128)(2,1)S(1)}, u32[]{:S(2)}, u32[]{:S(2)}) collective-permute-start(bf16[512,256]{1,0:T(8,128)(2,1)S(1)} %get-tuple-element.98), channel_id=1, source_target_pairs={{0,8},{8,0},{1,9},{9,1},{2,10},{10,2},{3,11},{11,3},{4,12},{12,4},... | collective-permute-start | bytes 786440 | tf_op jit(solution)/shard_map/ppermute | solution.py:261
  393.9 62.2 %collective-permute-start.62 = (bf16[1024,256]{1,0:T(8,128)(2,1)S(1)}, bf16[1024,256]{1,0:T(8,128)(2,1)S(1)}, u32[]{:S(2)}, u32[]{:S(2)}) collective-permute-start(bf16[1024,256]{1,0:T(8,128)(2,1)S(1)} %get-tuple-element.94), channel_id=1, source_target_pairs={{0,8},{8,0},{1,9},{9,1},{2,10},{10,2},{3,11},{11,3},{4,12},{12,4},... | collective-permute-start | bytes 1572872 | tf_op jit(solution)/shard_map/ppermute | solution.py:261
  398.5 57.5 %collective-permute-start.63 = (bf16[1024,256]{1,0:T(8,128)(2,1)S(1)}, bf16[1024,256]{1,0:T(8,128)(2,1)S(1)}, u32[]{:S(2)}, u32[]{:S(2)}) collective-permute-start(bf16[1024,256]{1,0:T(8,128)(2,1)S(1)} %get-tuple-element.93), channel_id=1, source_target_pairs={{0,8},{8,0},{1,9},{9,1},{2,10},{10,2},{3,11},{11,3},{4,12},{12,4},... | collective-permute-start | bytes 1572872 | tf_op jit(solution)/shard_map/ppermute | solution.py:261
  399.3 84.8 %collective-permute-start.60 = (bf16[512,1024]{1,0:T(8,128)(2,1)}, bf16[512,1024]{1,0:T(8,128)(2,1)}, u32[]{:S(2)}, u32[]{:S(2)}) collective-permute-start(bf16[512,1024]{1,0:T(8,128)(2,1)} %convolution_convert_fusion.6), channel_id=1, source_target_pairs={{0,4},{4,0},{1,5},{5,1},{2,6},{6,2},{3,7},{7,3},{8,12},{12,8},{9,1... | collective-permute-start | bytes 3145736 | tf_op jit(solution)/shard_map/ppermute | solution.py:261
  400.8 43.8 %collective-permute-start.71 = (bf16[512,256]{1,0:T(8,128)(2,1)S(1)}, bf16[512,256]{1,0:T(8,128)(2,1)S(1)}, u32[]{:S(2)}, u32[]{:S(2)}) collective-permute-start(bf16[512,256]{1,0:T(8,128)(2,1)S(1)} %fusion.34), channel_id=1, source_target_pairs={{0,16},{16,0},{1,17},{17,1},{2,18},{18,2},{3,19},{19,3},{4,20},{20... | collective-permute-start | bytes 786440 | tf_op jit(solution)/shard_map/ppermute | solution.py:303
  509.1 57.9 %collective-permute-start.79 = (bf16[3,288,512]{2,1,0:T(8,128)(2,1)}, bf16[3,288,512]{2,1,0:T(8,128)(2,1)S(1)}, u32[]{:S(2)}, u32[]{:S(2)}) collective-permute-start(bf16[3,288,512]{2,1,0:T(8,128)(2,1)} %add_convert_fusion.6), channel_id=1, source_target_pairs={{0,1},{1,2},{2,3},{3,0},{4,5},{5,6},{6,7},{7,4},{8,9},{9,10},{10,1... | collective-permute-start | bytes 2654216 | tf_op jit(solution)/shard_map/ppermute | solution.py:303
  510.4 55.4 %collective-permute-start.66 = (bf16[256,256]{1,0:T(8,128)(2,1)}, bf16[256,256]{1,0:T(8,128)(2,1)}, u32[]{:S(2)}, u32[]{:S(2)}) collective-permute-start(bf16[256,256]{1,0:T(8,128)(2,1)} %add_convert_fusion.14), channel_id=1, source_target_pairs={{0,1},{1,2},{2,3},{3,0},{4,5},{5,6},{6,7},{7,4},{8,9},{9,10},{10,1... | collective-permute-start | bytes 393224 | tf_op jit(solution)/shard_map/ppermute | solution.py:303
  511.0 74.5 %collective-permute-start.61 = (bf16[512,1024]{1,0:T(8,128)(2,1)S(1)}, bf16[512,1024]{1,0:T(8,128)(2,1)}, u32[]{:S(2)}, u32[]{:S(2)}) collective-permute-start(bf16[512,1024]{1,0:T(8,128)(2,1)S(1)} %fusion.13), channel_id=1, source_target_pairs={{4,1},{1,4},{6,3},{3,6},{12,9},{9,12},{14,11},{11,14},{20,17},{17,... | collective-permute-start | bytes 3145736 | tf_op jit(solution)/shard_map/ppermute | solution.py:348
  (96 other events, 1104.7 us)

commit v2 on v1

v2 whole, which is shorter than its diff:
```python
import functools

import jax
import jax.numpy as jnp
from jax import lax
from jax.experimental import pallas as pl
from jax.experimental.pallas import tpu as pltpu
from jax.sharding import Mesh, PartitionSpec as P

epsilon = 1e-05
theta_base = 1000000.0
bf16 = jnp.bfloat16
f32 = jnp.float32
tile = 256
span = 512


def cost(flops):
    return pl.CostEstimate(flops=flops, bytes_accessed=10**6, transcendentals=0)


def dot(left, right, left_dim, right_dim):
    return lax.dot_general(
        left, right, (((left_dim,), (right_dim,)), ((), ())), preferred_element_type=f32
    )


def group_sum(value, ones):
    high = value.astype(bf16)
    low = (value - high.astype(f32)).astype(bf16)
    return dot(high, ones, 1, 0) + dot(low, ones, 1, 0)


def ones_by_head(lanes, head):
    row = lax.broadcasted_iota(jnp.int32, (lanes, lanes), 0) // head
    col = lax.broadcasted_iota(jnp.int32, (lanes, lanes), 1) // head
    return jnp.where(row == col, 1.0, 0.0).astype(bf16)


def half_swap(value, head):
    lanes = value.shape[-1]
    lane = lax.broadcasted_iota(jnp.int32, value.shape, 1) % head
    return jnp.where(
        lane < head // 2,
        pltpu.roll(value, lanes - head // 2, 1),
        pltpu.roll(value, head // 2, 1),
    )


def head_norm(raw, ones, head):
    root = lax.rsqrt(group_sum(raw * raw, ones) * (1.0 / head) + epsilon)
    return raw * root, root


def split_block(block, head):
    lanes = 2 * head
    queries = block[:, :lanes]
    both = block[:, lanes:]
    other = pltpu.roll(both, head, 1)
    first = lax.broadcasted_iota(jnp.int32, both.shape, 1) < head
    keys = jnp.where(first, both, other)
    values = jnp.where(first, other, both)
    return queries, keys, values


def stack_heads(block, head):
    first = lax.broadcasted_iota(jnp.int32, block.shape, 1) < head
    zero = jnp.zeros_like(block)
    return jnp.concatenate([jnp.where(first, block, zero), jnp.where(first, zero, block)], axis=0)


def merge_heads(stacked, head):
    half = stacked.shape[0] // 2
    first = lax.broadcasted_iota(jnp.int32, (half, stacked.shape[1]), 1) < head
    return jnp.where(first, stacked[:half], stacked[half:])


def attend_kernel(head, qkv_ref, cos_ref, sin_ref, seg_col, seg_row, gain_ref, ctx_ref, q_s, k_s, v_s):
    length = qkv_ref.shape[0]
    lanes = 2 * head
    ones = ones_by_head(lanes, head)
    queries, keys, values = split_block(qkv_ref[...], head)
    cosine, sine = cos_ref[...], sin_ref[...]

    def rotated(raw, gain):
        hat, _ = head_norm(raw, ones, head)
        scaled = hat * gain
        return (scaled * cosine + half_swap(scaled, head) * sine).astype(bf16)

    q_s[...] = rotated(queries, gain_ref[0:1, :]) * jnp.asarray(head**-0.5, bf16)
    k_s[...] = rotated(keys, gain_ref[1:2, :])
    v_s[...] = values.astype(bf16)
    for top in range(0, length, tile):
        low, high = max(0, top - span), top + tile
        stacked = stack_heads(q_s[top:high, :], head)
        scores = dot(stacked, k_s[low:high, :], 1, 1)
        row = lax.broadcasted_iota(jnp.int32, (tile, high - low), 0) + top
        col = lax.broadcasted_iota(jnp.int32, (tile, high - low), 1) + low
        allowed = (seg_col[top:high, 0:1] == seg_row[0:1, low:high]) & (row >= col)
        allowed = jnp.concatenate([allowed, allowed], axis=0)
        exponent = jnp.where(allowed, jnp.exp(scores), 0.0)
        total = jnp.sum(exponent, axis=1, keepdims=True)
        mixed = dot(exponent.astype(bf16), v_s[low:high, :], 1, 0) / total
        ctx_ref[top:high, :] = merge_heads(mixed, head).astype(bf16)


def attend(qkv, cosine, sine, seg_col, seg_row, gains, head):
    length, width = qkv.shape
    groups = width // (4 * head)
    lanes = 2 * head
    whole = lambda shape: pl.BlockSpec(shape, lambda j: (0, 0))
    return pl.pallas_call(
        functools.partial(attend_kernel, head),
        grid=(groups,),
        in_specs=[
            pl.BlockSpec((length, 2 * lanes), lambda j: (0, j)),
            whole((length, lanes)),
            whole((length, lanes)),
            whole((length, 1)),
            whole((1, length)),
            whole((8, lanes)),
        ],
        out_specs=pl.BlockSpec((length, lanes), lambda j: (0, j)),
        out_shape=jax.ShapeDtypeStruct((length, groups * lanes), bf16),
        scratch_shapes=[pltpu.VMEM((length, lanes), bf16)] * 3,
        compiler_params=pltpu.CompilerParams(vmem_limit_bytes=40 * 2**20),
        cost_estimate=cost(6 * 10**9),
        name="attend",
    )(qkv, cosine, sine, seg_col, seg_row, gains)


def attend_back_kernel(
    head, qkv_ref, cos_ref, sin_ref, seg_col, seg_row, gain_ref, do_ref, out_ref, sums_ref,
    q_s, k_s, v_s, dk_s, dv_s, dq_s,
):
    length = qkv_ref.shape[0]
    lanes = 2 * head
    ones = ones_by_head(lanes, head)
    queries, keys, values = split_block(qkv_ref[...], head)
    cosine, sine = cos_ref[...], sin_ref[...]

    def rotated(raw, gain):
        hat, _ = head_norm(raw, ones, head)
        scaled = hat * gain
        return (scaled * cosine + half_swap(scaled, head) * sine).astype(bf16)

    scale = jnp.asarray(head**-0.5, bf16)
    q_s[...] = rotated(queries, gain_ref[0:1, :]) * scale
    k_s[...] = rotated(keys, gain_ref[1:2, :])
    v_s[...] = values.astype(bf16)
    dk_s[...] = jnp.zeros_like(dk_s)
    dv_s[...] = jnp.zeros_like(dv_s)
    for top in range(0, length, tile):
        low, high = max(0, top - span), top + tile
        stacked = stack_heads(q_s[top:high, :], head)
        grads = stack_heads(do_ref[top:high, :], head)
        near_k, near_v = k_s[low:high, :], v_s[low:high, :]
        scores = dot(near_k, stacked, 1, 1)
        col = lax.broadcasted_iota(jnp.int32, (high - low, tile), 0) + low
        row = lax.broadcasted_iota(jnp.int32, (high - low, tile), 1) + top
        allowed = (seg_col[low:high, 0:1] == seg_row[0:1, top:high]) & (row >= col)
        allowed = jnp.concatenate([allowed, allowed], axis=1)
        exponent = jnp.where(allowed, jnp.exp(scores), 0.0)
        probs = exponent * (1.0 / jnp.sum(exponent, axis=0, keepdims=True))
        grad_probs = dot(near_v, grads, 1, 1)
        weighted = probs * grad_probs
        delta = jnp.sum(weighted, axis=0, keepdims=True)
        grad_scores = (weighted - probs * delta).astype(bf16)
        dv_s[low:high, :] += dot(probs.astype(bf16), grads, 1, 0)
        dk_s[low:high, :] += dot(grad_scores, stacked, 1, 0)
        dq_s[top:high, :] = merge_heads(dot(grad_scores, near_k, 0, 0), head) * head**-0.5

    def back(raw, gain, grad):
        hat, root = head_norm(raw, ones, head)
        normed = grad * cosine - half_swap(grad, head) * sine
        gain_part = jnp.sum(normed * hat, axis=0, keepdims=True)
        scaled = normed * gain
        mean = group_sum(scaled * hat, ones) * (1.0 / head)
        return root * (scaled - hat * mean), gain_part

    grad_q, q_sum = back(queries, gain_ref[0:1, :], dq_s[...])
    folded_k = dk_s[...] + pltpu.roll(dk_s[...], head, 1)
    grad_k, k_sum = back(keys, gain_ref[1:2, :], folded_k)
    folded_v = dv_s[...] + pltpu.roll(dv_s[...], head, 1)
    first = lax.broadcasted_iota(jnp.int32, (length, lanes), 1) < head
    out_ref[:, :lanes] = grad_q.astype(bf16)
    out_ref[:, lanes:] = jnp.where(first, grad_k, folded_v).astype(bf16)
    which = lax.broadcasted_iota(jnp.int32, sums_ref.shape, 0)
    sums_ref[...] = jnp.where(which == 0, q_sum, jnp.where(which == 1, k_sum, 0.0))


def attend_back(qkv, cosine, sine, seg_col, seg_row, gains, grad_context, head):
    length, width = qkv.shape
    groups = width // (4 * head)
    lanes = 2 * head
    whole = lambda shape: pl.BlockSpec(shape, lambda j: (0, 0))
    return pl.pallas_call(
        functools.partial(attend_back_kernel, head),
        grid=(groups,),
        in_specs=[
            pl.BlockSpec((length, 2 * lanes), lambda j: (0, j)),
            whole((length, lanes)),
            whole((length, lanes)),
            whole((length, 1)),
            whole((1, length)),
            whole((8, lanes)),
            pl.BlockSpec((length, lanes), lambda j: (0, j)),
        ],
        out_specs=(
            pl.BlockSpec((length, 2 * lanes), lambda j: (0, j)),
            pl.BlockSpec((8, lanes), lambda j: (j, 0)),
        ),
        out_shape=(
            jax.ShapeDtypeStruct((length, width), bf16),
            jax.ShapeDtypeStruct((8 * groups, lanes), f32),
        ),
        scratch_shapes=[pltpu.VMEM((length, lanes), bf16)] * 3 + [pltpu.VMEM((length, lanes), f32)] * 3,
        compiler_params=pltpu.CompilerParams(vmem_limit_bytes=48 * 2**20),
        cost_estimate=cost(12 * 10**9),
        name="attend_back",
    )(qkv, cosine, sine, seg_col, seg_row, gains, grad_context)


def pull(pairs, sems, start):
    copies = [pltpu.make_async_copy(s, d, sems.at[start + i]) for i, (s, d) in enumerate(pairs)]
    for copy in copies:
        copy.start()
    return copies


def finish(copies):
    for copy in copies:
        copy.wait()


def halves(which_ref, half):
    first = pl.multiple_of(which_ref[0] * half, half)
    second = pl.multiple_of((1 - which_ref[0]) * half, half)
    return pl.ds(first, half), pl.ds(second, half)


def call_local(kernel, which, arrays, outs, out_spaces, scratch, copies, flops, name, limit=58):
    return pl.pallas_call(
        kernel,
        in_specs=[pl.BlockSpec(memory_space=pltpu.SMEM)] + [pl.BlockSpec(memory_space=pltpu.HBM)] * len(arrays),
        out_specs=[pl.BlockSpec(memory_space=space) for space in out_spaces],
        out_shape=outs,
        scratch_shapes=[*scratch, pltpu.SemaphoreType.DMA((copies,))],
        compiler_params=pltpu.CompilerParams(vmem_limit_bytes=limit * 2**20),
        cost_estimate=cost(flops),
        name=name,
    )(which, *arrays)


class Loads:
    def __init__(self, sems):
        self.sems, self.count, self.open = sems, 0, {}

    def start(self, key, *pairs):
        for source, target in pairs:
            copy = pltpu.make_async_copy(source, target, self.sems.at[self.count])
            copy.start()
            self.open.setdefault(key, []).append(copy)
            self.count += 1

    def wait(self, *keys):
        for key in keys:
            for copy in self.open.pop(key, ()):
                copy.wait()

    def close(self):
        self.wait(*list(self.open))


def load_weights(loads, key, near, far, which_ref, gate_up, down, slots):
    size, half = near[0].shape
    top = 2 * size // 3
    first, second = halves(which_ref, half)
    for i in slots:
        for piece, lanes in ((near[i], first), (far[i], second)):
            if gate_up is not None:
                loads.start((key, i), (piece.at[pl.ds(0, top)], gate_up.at[pl.ds(i * top, top), lanes]))
            if down is not None:
                rest = size - top
                loads.start((key, i), (piece.at[pl.ds(top, rest)], down.at[pl.ds(i * rest, rest), lanes]))


def hidden_step(gate_up, down, rows, cot, gu_s, hid_s, slot, columns, sub):
    both = dot(gate_up[2 * slot * sub : 2 * (slot + 1) * sub, :], rows, 1, 1)
    back = dot(down[slot * sub : (slot + 1) * sub, :], cot, 1, 1)
    gate, up = both[:sub], both[sub:]
    sig = 0.5 * jnp.tanh(0.5 * gate) + 0.5
    act = gate * sig
    base = 2 * slot * sub
    gu_s[base : base + sub, columns] = (back * up * (sig + act * (1.0 - sig))).astype(bf16)
    gu_s[base + sub : base + 2 * sub, columns] = (back * act).astype(bf16)
    hid_s[slot * sub : (slot + 1) * sub, columns] = (act * up).astype(bf16)


def weight_step(loads, which_ref, gu_s, hid_s, rows_s, cot_s, out_s, far_out, near_out, order, sub):
    half = far_out[0].shape[1]
    first, second = halves(which_ref, half)
    for side, lanes, outs in ((0, second, far_out), (1, first, near_out)):
        rows, cots = rows_s[:, lanes], cot_s[:, lanes]
        for s in order:
            out_s[side, s, : 2 * sub] = dot(gu_s[2 * s * sub : 2 * (s + 1) * sub, :], rows, 1, 0).astype(bf16)
            out_s[side, s, 2 * sub :] = dot(hid_s[s * sub : (s + 1) * sub, :], cots, 1, 0).astype(bf16)
            loads.start("out", (out_s.at[side, s], outs[s]))


def take(refs, *counts):
    at, out = 0, []
    for count in counts:
        out.append(refs[at : at + count])
        at += count
    return (*out, refs[at:])


def first_kernel(slots, quarters, order, which_ref, *refs):
    near, far, rows, cots, (gu_out, hid_out), far_out, near_out, rest = take(
        refs, slots, slots, quarters, quarters, 2, slots, slots
    )
    gate_up, down, rows_s, cot_s, gu_s, hid_s, out_s, sems = rest
    sub, count = near[0].shape[0] // 3, rows[0].shape[0]
    loads = Loads(sems)
    for q in range(max(slots, quarters)):
        if q < quarters:
            place = pl.ds(q * count, count)
            loads.start(("rows", q), (rows[q], rows_s.at[place]), (cots[q], cot_s.at[place]))
        if q < slots:
            load_weights(loads, "w", near, far, which_ref, gate_up, down, [q])
    for q in range(quarters):
        columns = slice(q * count, (q + 1) * count)
        loads.wait(("rows", q))
        for s in range(slots):
            loads.wait(("w", s))
            hidden_step(gate_up, down, rows_s[columns, :], cot_s[columns, :], gu_s, hid_s, s, columns, sub)
    loads.start("out", (gu_s, gu_out), (hid_s, hid_out))
    weight_step(loads, which_ref, gu_s, hid_s, rows_s, cot_s, out_s, far_out, near_out, order, sub)
    loads.close()


def ffn_first(which, near, far, rows, cots, order):
    slots, quarters = len(near), len(rows)
    size, half = near[0].shape
    sub, count = size // 3, rows[0].shape[0]
    tokens = quarters * count
    gu, hid = (2 * slots * sub, tokens), (slots * sub, tokens)
    out = call_local(
        functools.partial(first_kernel, slots, quarters, order),
        which,
        [*near, *far, *rows, *cots],
        [jax.ShapeDtypeStruct(v, bf16) for v in (gu, hid)]
        + [jax.ShapeDtypeStruct((size, half), bf16)] * (2 * slots),
        [pl.ANY] * (2 + 2 * slots),
        [
            pltpu.VMEM((2 * slots * sub, 2 * half), bf16),
            pltpu.VMEM((slots * sub, 2 * half), bf16),
            pltpu.VMEM((tokens, 2 * half), bf16),
            pltpu.VMEM((tokens, 2 * half), bf16),
            pltpu.VMEM(gu, bf16),
            pltpu.VMEM(hid, bf16),
            pltpu.VMEM((2, slots, size, half), bf16),
        ],
        2 * quarters + 4 * slots + 2 + 2 * slots,
        8 * slots * size * half * tokens,
        "ffn_first",
    )
    return out[0], out[1], out[2 : 2 + slots], out[2 + slots :]


def second_kernel(slots, quarters, which_ref, *refs):
    near, far, near_0, far_0, rows, cots, (gu_0,), (gu_out, hid_out), outs, rest = take(
        refs, slots, slots, slots, slots, quarters, quarters, 1, 2, quarters
    )
    gate_up, down, gate_up_0, rows_s, cot_s, gu_s, hid_s, gu_0s, out_s, sems = rest
    sub, count = near[0].shape[0] // 3, rows[0].shape[0]
    loads = Loads(sems)
    turn = [(i + quarters // 2) % quarters for i in range(quarters)]
    for i in range(max(slots, quarters)):
        if i < quarters:
            q = turn[i]
            place = pl.ds(q * count, count)
            loads.start(("rows", q), (rows[q], rows_s.at[place]), (cots[q], cot_s.at[place]))
        if i < slots:
            load_weights(loads, "w", near, far, which_ref, gate_up, down, [i])
        if i == slots - 1:
            load_weights(loads, "w0", near_0, far_0, which_ref, gate_up_0, None, range(slots))
            loads.start("g0", (gu_0, gu_0s))
    for q in turn:
        columns = slice(q * count, (q + 1) * count)
        loads.wait(("rows", q))
        for s in range(slots):
            loads.wait(("w", s))
            hidden_step(gate_up, down, rows_s[columns, :], cot_s[columns, :], gu_s, hid_s, s, columns, sub)
        loads.wait("g0", *(("w0", s) for s in range(slots)))
        total = dot(gu_0s[:, columns], gate_up_0[...], 0, 0) + dot(gu_s[:, columns], gate_up[...], 0, 0)
        out_s[q] = total.astype(bf16)
        loads.start("out", (out_s.at[q], outs[q]))
    loads.start("out", (gu_s, gu_out), (hid_s, hid_out))
    loads.close()


def ffn_second(which, near, far, rows, cots, gu_0):
    slots, quarters = len(near) // 2, len(rows)
    size, half = near[0].shape
    sub, count = size // 3, rows[0].shape[0]
    tokens = quarters * count
    gu, hid = (2 * slots * sub, tokens), (slots * sub, tokens)
    out = call_local(
        functools.partial(second_kernel, slots, quarters),
        which,
        [*near[slots:], *far[slots:], *near[:slots], *far[:slots], *rows, *cots, gu_0],
        [jax.ShapeDtypeStruct(v, bf16) for v in (gu, hid)]
        + [jax.ShapeDtypeStruct((count, 2 * half), bf16)] * quarters,
        [pl.ANY] * (2 + quarters),
        [
            pltpu.VMEM((2 * slots * sub, 2 * half), bf16),
            pltpu.VMEM((slots * sub, 2 * half), bf16),
            pltpu.VMEM((2 * slots * sub, 2 * half), bf16),
            pltpu.VMEM((tokens, 2 * half), bf16),
            pltpu.VMEM((tokens, 2 * half), bf16),
            pltpu.VMEM(gu, bf16),
            pltpu.VMEM(hid, bf16),
            pltpu.VMEM(gu, bf16),
            pltpu.VMEM((quarters, count, 2 * half), bf16),
        ],
        3 * quarters + 6 * slots + 3,
        10 * slots * size * half * tokens,
        "ffn_second",
    )
    return out[0], out[1], out[2:]


def third_kernel(slots, quarters, order, which_ref, *refs):
    near, far, rows, cots, (gu, hid, hid_0), far_out, near_out, outs, rest = take(
        refs, 2 * slots, 2 * slots, quarters, quarters, 3, slots, slots, quarters
    )
    down, rows_s, cot_s, gu_s, hid_s, hid_0s, grad_s, out_s, sems = rest
    sub, count = near[0].shape[0] // 3, rows[0].shape[0]
    loads = Loads(sems)
    for q in range(quarters):
        loads.start("rows", (rows[q], rows_s.at[pl.ds(q * count, count)]))
    loads.start("rows", (gu, gu_s))
    for q in range(quarters):
        loads.start("rows", (cots[q], cot_s.at[pl.ds(q * count, count)]))
    loads.start("rows", (hid, hid_s))
    load_weights(loads, "w", near, far, which_ref, None, down, range(2 * slots))
    loads.start("h0", (hid_0, hid_0s))
    loads.wait("rows")
    weight_step(loads, which_ref, gu_s, hid_s, rows_s, cot_s, grad_s, far_out, near_out, order, sub)
    loads.wait("h0", *(("w", s) for s in range(2 * slots)))
    for q in range(quarters):
        columns = slice(q * count, (q + 1) * count)
        total = dot(hid_0s[:, columns], down[: slots * sub, :], 0, 0)
        total = total + dot(hid_s[:, columns], down[slots * sub :, :], 0, 0)
        out_s[q] = total.astype(bf16)
        loads.start("out", (out_s.at[q], outs[q]))
    loads.close()


def ffn_third(which, near, far, rows, cots, gu, hid, hid_0, order):
    slots, quarters = len(near) // 2, len(rows)
    size, half = near[0].shape
    sub, count = size // 3, rows[0].shape[0]
    tokens = quarters * count
    out = call_local(
        functools.partial(third_kernel, slots, quarters, order),
        which,
        [*near, *far, *rows, *cots, gu, hid, hid_0],
        [jax.ShapeDtypeStruct((size, half), bf16)] * (2 * slots)
        + [jax.ShapeDtypeStruct((count, 2 * half), bf16)] * quarters,
        [pl.ANY] * (2 * slots + quarters),
        [
            pltpu.VMEM((2 * slots * sub, 2 * half), bf16),
            pltpu.VMEM((tokens, 2 * half), bf16),
            pltpu.VMEM((tokens, 2 * half), bf16),
            pltpu.VMEM((2 * slots * sub, tokens), bf16),
            pltpu.VMEM((slots * sub, tokens), bf16),
            pltpu.VMEM((slots * sub, tokens), bf16),
            pltpu.VMEM((2, slots, size, half), bf16),
            pltpu.VMEM((quarters, count, 2 * half), bf16),
        ],
        3 * quarters + 4 * slots + 3 + 2 * slots,
        6 * slots * size * half * tokens,
        "ffn_third",
    )
    return out[:slots], out[slots : 2 * slots], out[2 * slots :]


def place_kernel(count, starts_ref, *refs):
    width = refs[0].shape[1]
    sems = refs[-1]
    finish(
        pull(
            [(refs[i], refs[count].at[:, pl.ds(pl.multiple_of(starts_ref[i], width), width)]) for i in range(count)],
            sems,
            0,
        )
    )


def place_lanes(blocks, starts):
    rows, width = blocks[0].shape
    return call_local(
        functools.partial(place_kernel, len(blocks)),
        jnp.stack(starts).astype(jnp.int32),
        blocks,
        [jax.ShapeDtypeStruct((rows, len(blocks) * width), bf16)],
        [pl.ANY],
        [],
        len(blocks),
        10**9,
        "place_lanes",
        4,
    )[0]


def after(value, *earlier):
    return lax.optimization_barrier((value, *earlier))[0]


def ring(size, step=1):
    return [(i, (i + step) % size) for i in range(size)]


class Lanes:
    def __init__(self):
        self.last = {}

    def wait(self, value, lane):
        return after(value, *self.last.get(lane, ())) if lane in self.last else value

    def move(self, value, axes, pairs, lane):
        got = lax.ppermute(self.wait(value, lane), axes, pairs)
        if lane:
            self.last[lane] = (got,)
        return got

    def swap(self, value, axis):
        return self.move(value, axis, [(0, 1), (1, 0)], None if axis == "c" else axis)

    def around(self, values, size, signs, lane):
        held = [self.wait(value, lane) for value in values]
        got = [lax.ppermute(v, "z", ring(size, signs * (i + 1))) for i, v in enumerate(held)]
        self.last[lane] = tuple(got)
        return got


def by_index(index, first, second, axis):
    return jnp.where(
        index == 0,
        jnp.concatenate([first, second], axis=axis),
        jnp.concatenate([second, first], axis=axis),
    )


def lane_block(value, index, width):
    start = [0] * (value.ndim - 1) + [index * width]
    return lax.dynamic_slice(value, start, (*value.shape[:-1], width))


def plus(left, *right):
    total = left.astype(f32)
    for value in right:
        total = total + value.astype(f32)
    return total


def plane_gather(value, sizes, lanes):
    y_size, x_size = sizes[:2]
    y, x = lax.axis_index("y"), lax.axis_index("x")
    if y_size > 2:
        wide = by_index(x, value, lanes.swap(value, "x"), -1)
        wide = lax.all_gather(wide, "y", axis=0)
        return jnp.concatenate([wide[i] for i in range(y_size)], axis=-1)
    width = value.shape[1]
    far = lanes.swap(value, "y")
    blocks = [value, lanes.swap(value, "x"), far, lanes.swap(far, "x")]
    starts = [(a * x_size + b) * width for a in (y, 1 - y) for b in (x, 1 - x)]
    return place_lanes(blocks, starts)


def plane_scatter(value, sizes, pair, lanes):
    y_size, x_size = sizes[:2]
    y, x = lax.axis_index("y"), lax.axis_index("x")
    block = lambda y_at, x_at: lane_block(value, y_at * x_size + x_at, pair)
    if y_size > 2:
        per_y = [plus(block(i, x), lanes.swap(block(i, 1 - x), "x")).astype(bf16) for i in range(y_size)]
        return lax.psum_scatter(jnp.stack(per_y), "y", scatter_dimension=0, tiled=False).astype(f32)
    far = plus(block(1 - y, x), lanes.swap(block(1 - y, 1 - x), "x")).astype(bf16)
    near = lanes.swap(block(y, 1 - x), "x")
    return plus(block(y, x), near, lanes.swap(far, "y"))


def z_scatter(blocks, size, lanes):
    return plus(blocks[0], *lanes.around(blocks[1:], size, -1, "z"))


def shards(
    sizes,
    tokens,
    segments,
    cotangent,
    attn_gain,
    q_weight,
    k_weight,
    v_weight,
    query_gain,
    key_gain,
    o_weight,
    ffn_gain,
    gate_weight,
    up_weight,
    down_weight,
):
    y_size, x_size, c_size, z_size = sizes
    y, x, c, z = (lax.axis_index(name) for name in "yxcz")
    own_rows, width = tokens.shape
    part = q_weight.shape[0]
    parts = width // part
    pair, quad = c_size * part, x_size * c_size * part
    gain_part = query_gain.shape[0]
    head = gain_part * parts
    seq_count, length = segments.shape

    lanes = Lanes()

    pairs = []
    for low in range(0, z_size, 2):
        pairs += [(z_size + low, low + 1), (low + 1, z_size + low)]
    trades = (c + z) % 2 == 1

    def trade(value, lane):
        return jnp.where(trades, lanes.move(value, ("c", "z"), pairs, lane), value)

    tokens = trade(tokens, None)

    qt, kt, vt, ot = q_weight.T, k_weight.T, v_weight.T, o_weight.T
    q_rows, k_rows = qt.shape[0] // 2, kt.shape[0] // 2
    qkv_rows = q_rows + 2 * k_rows
    gain_rows = jnp.concatenate(
        [attn_gain[None], ffn_gain[None]]
        + [jnp.pad(g, (0, part - gain_part))[None] for g in (query_gain, key_gain)]
        + [jnp.zeros((12, part), bf16)],
        axis=0,
    )
    seg_rows = seq_count * length // part
    numbers = segments.astype(bf16).reshape(seg_rows, part)
    pack = jnp.concatenate(
        [v.reshape(2, -1, part) for v in (qt, kt, vt)]
        + [
            jnp.broadcast_to(gain_rows, (2, 16, part)),
            ot.reshape(2, q_rows, part),
            jnp.broadcast_to(numbers, (2, seg_rows, part)),
        ],
        axis=1,
    )
    mine = lax.dynamic_index_in_dim(pack, c, 0, keepdims=False)
    other = lax.dynamic_index_in_dim(pack, 1 - c, 0, keepdims=False)
    got = lanes.swap(other, "c")
    pack_end = qkv_rows + 16 + q_rows
    pack = by_index(c, mine[:pack_end], got[:pack_end], -1)
    other_segments = got[pack_end:].astype(jnp.int32).reshape(seq_count, length)

    sub = gate_weight.shape[1] // (x_size * c_size)
    ffn_pack = jnp.stack([after(v, other).T for v in (gate_weight, up_weight, down_weight)]).reshape(
        3, x_size, c_size, sub, part
    )
    mine = lax.dynamic_index_in_dim(ffn_pack, c, 2, keepdims=False)
    other = lax.dynamic_index_in_dim(ffn_pack, 1 - c, 2, keepdims=False)
    ffn_pack = by_index(c, mine, lanes.swap(other, "c"), -1)
    mine = lax.dynamic_index_in_dim(ffn_pack, x, 1, keepdims=False)
    other = lax.dynamic_index_in_dim(ffn_pack, 1 - x, 1, keepdims=False)
    ffn_own = by_index(x, mine, lanes.swap(other, "x"), -1).reshape(3 * sub, quad)

    qkv_own = pack[:qkv_rows]
    qkv_own = jnp.concatenate(
        [qkv_own, *lanes.around([qkv_own] * (z_size - 1), z_size, 1, "z"), pack[qkv_rows : qkv_rows + 16]],
        axis=0,
    )
    all_tokens = by_index(c, tokens, lanes.swap(tokens, "c"), 0).astype(f32)
    qkv_all = plane_gather(qkv_own, sizes, lanes)
    qkv_full = qkv_all[: z_size * qkv_rows]
    gains = qkv_all[z_size * qkv_rows :].astype(f32)
    gain_one, gain_two = gains[0:1], gains[1:2]
    gain_query, gain_key = (
        gains[i].reshape(parts, part)[:, :gain_part].reshape(1, head) for i in (2, 3)
    )
    head_gains = jnp.concatenate(
        [jnp.tile(gain_query, (1, 2)), jnp.tile(gain_key, (1, 2)), jnp.zeros((6, 2 * head), f32)], axis=0
    )

    half = width // 2
    pieces, wide = [ffn_own], []

    def over_y(piece):
        if y_size > 2:
            full = jnp.concatenate(list(lax.all_gather(piece, "y", axis=0)), axis=-1)
            wide.append((full[:, :half], full[:, half:]))
        else:
            wide.append((piece, lanes.swap(piece, "y")))

    over_y(ffn_own)
    lanes.last["more"] = lanes.last["z"]
    o_own = [pack[qkv_rows + 16 :]]
    for _ in range(1, z_size):
        o_own.append(lanes.move(o_own[-1], "z", ring(z_size), "more"))
    o_full = plane_gather(jnp.concatenate(o_own, axis=0), sizes, lanes)
    cotangent = trade(cotangent, "more")
    for _ in range(1, z_size):
        pieces.append(lanes.move(pieces[-1], "z", ring(z_size), "z"))
        over_y(pieces[-1])
    which = (y if y_size == 2 else y * 0).astype(jnp.int32).reshape(1)
    near, far = [w[0] for w in wide], [w[1] for w in wide]

    segment = lax.dynamic_index_in_dim(
        jnp.where(c == z % 2, segments, other_segments), z // 2, 0, keepdims=False
    )
    place = lax.broadcasted_iota(jnp.int32, (length,), 0) - jnp.sum(
        (segment[None, :] < segment[:, None]).astype(jnp.int32), axis=1
    )
    frequency = theta_base ** (-2.0 * jnp.arange(head // 2, dtype=f32) / head)
    angles = place.astype(f32)[:, None] * frequency
    cosine, sine = jnp.cos(angles), jnp.sin(angles)
    cosine = jnp.concatenate([cosine] * 4, axis=1)
    sine = jnp.concatenate([-sine, sine] * 2, axis=1)
    seg_col, seg_row = segment[:, None], segment[None, :]

    inputs = tokens.astype(f32)
    root_one = lax.rsqrt(jnp.mean(inputs * inputs, axis=-1, keepdims=True) + epsilon)
    hat_one = inputs * root_one
    all_root = lax.rsqrt(jnp.mean(all_tokens * all_tokens, axis=-1, keepdims=True) + epsilon)
    normed_one = (all_tokens * all_root * gain_one).astype(bf16)
    qkv = dot(after(normed_one, pieces[1], wide[0][1]), qkv_full, 1, 1)
    context = attend(qkv, cosine, sine, seg_col, seg_row, head_gains, head)

    def half_rows(value, index):
        return lax.dynamic_slice_in_dim(value, index * own_rows, own_rows, 0)

    def core_reduce(left, right, right_dim):
        sent = dot(half_rows(left, 1 - c), right, 1, right_dim).astype(bf16)
        kept = dot(half_rows(left, c), right, 1, right_dim)
        return kept + lanes.swap(sent, "c").astype(f32)

    def spread(value):
        across = lanes.swap(value, "x")
        return [value, lanes.swap(value, "c"), across, lanes.swap(across, "c")]

    cots = spread(cotangent)
    mid = inputs + core_reduce(after(context, pieces[z_size // 2], wide[1][1]), o_full, 0)
    root_two = lax.rsqrt(jnp.mean(mid * mid, axis=-1, keepdims=True) + epsilon)
    hat_two = mid * root_two
    normed_two = (hat_two * gain_two).astype(bf16)
    rows_two = spread(normed_two)

    count = z_size // 2
    slot_grads, arrived = [None] * z_size, [None] * z_size

    def turn(group):
        return sorted(range(count), key=lambda i: (group * count + i - 1) % z_size)

    def send_gradients(group, sent, kept):
        for i in turn(group):
            slot = group * count + i
            if y_size > 2:
                full = jnp.concatenate([kept[i], sent[i]], axis=1)
                full = jnp.stack([full[:, k * quad : (k + 1) * quad] for k in range(y_size)])
                arrived[slot] = lax.psum_scatter(full, "y", scatter_dimension=0, tiled=False)
                slot_grads[slot] = arrived[slot].astype(f32)
            else:
                arrived[slot] = lanes.swap(sent[i], "y")
                slot_grads[slot] = plus(kept[i], arrived[slot])

    gu_0, hid_0, sent, kept = ffn_first(which, near[:count], far[:count], rows_two, cots, turn(0))
    send_gradients(0, sent, kept)
    gu_1, hid_1, (first, second, third, fourth) = ffn_second(which, near, far, rows_two, cots, gu_0)
    third = plus(third, lanes.swap(fourth, "c")).astype(bf16)
    across = lanes.swap(third, "x")
    second = lanes.swap(second, "c")
    sent, kept, (out_first, out_second, out_third, out_fourth) = ffn_third(
        after(which, third, arrived[1]), near, far, rows_two, cots, gu_1, hid_1, hid_0, turn(1)
    )
    send_gradients(1, sent, kept)
    total = lanes.move(slot_grads[1].astype(bf16), "z", ring(z_size), "z")
    grad_normed_two = after(plus(first, second, across), total, arrived[0])


    def norm_back(grad, hat, root):
        return root * (grad - hat * jnp.mean(grad * hat, axis=-1, keepdims=True))

    gain_two_part = jnp.sum(grad_normed_two * hat_two, axis=0)
    grad_mid = cotangent.astype(f32) + norm_back(grad_normed_two * gain_two, hat_two, root_two)

    branch_own = grad_mid.astype(bf16)
    branch = by_index(c, branch_own, lanes.swap(branch_own, "c"), 0)
    grad_context = dot(branch, o_full, 1, 1).astype(bf16)
    o_grad = dot(after(context, grad_context), branch, 0, 0).astype(bf16)
    grad_qkv, head_sums = attend_back(
        qkv, cosine, sine, seg_col, seg_row, head_gains, after(grad_context, o_grad, arrived[2]), head
    )
    out_third = plus(out_third, lanes.swap(out_fourth, "c")).astype(bf16)
    out_across = lanes.swap(out_third, "x")
    output = (mid + plus(out_first, lanes.swap(out_second, "c"), out_across)).astype(bf16)
    o_part = plane_scatter(o_grad, sizes, pair, lanes).astype(bf16)
    for step in range(1, z_size - 1):
        total = plus(total, slot_grads[step + 1]).astype(bf16)
        total = lanes.move(total, "z", ring(z_size), "z")
        if step == 1:
            grad_qkv = after(grad_qkv, total, arrived[-1])
    total = plus(total, slot_grads[0])

    head_sums = jnp.sum(head_sums.reshape(-1, 8, 2 * head), axis=0)
    gain_query_part = head_sums[0, :head] + head_sums[0, head:]
    gain_key_part = head_sums[1, :head]
    qkv_grad = dot(grad_qkv, normed_one, 0, 0).astype(bf16)
    qkv_part = plane_scatter(qkv_grad, sizes, pair, lanes).astype(bf16)
    grad_normed_one = core_reduce(after(grad_qkv, qkv_grad), qkv_full, 0)

    def core_deal(value):
        kept = lane_block(value, c, part)
        sent = lanes.swap(lane_block(value, 1 - c, part), "c")
        return jnp.where(c == 0, jnp.stack([kept, sent]), jnp.stack([sent, kept]))

    wgrads = total.astype(bf16).reshape(3, sub, quad)
    kept = lane_block(wgrads, x, pair)
    sent = lanes.swap(lane_block(wgrads, 1 - x, pair), "x")
    wgrads = jnp.where(x == 0, jnp.stack([kept, sent], 1), jnp.stack([sent, kept], 1))
    kept = lane_block(wgrads, c, part)
    sent = lanes.swap(lane_block(wgrads, 1 - c, part), "c")
    wgrads = jnp.where(c == 0, jnp.stack([kept, sent], 2), jnp.stack([sent, kept], 2))
    wgrads = wgrads.reshape(3, x_size * c_size * sub, part)
    gate_wgrad, up_wgrad, down_wgrad = (wgrads[i].astype(f32).T for i in range(3))


    value = z_scatter([o_part[i * q_rows : (i + 1) * q_rows] for i in range(z_size)], z_size, lanes)
    o_wgrad = core_deal(value.astype(bf16)).astype(f32).reshape(2 * q_rows, part).T

    gain_one_part = jnp.sum(grad_normed_one * hat_one, axis=0)
    tokens_grad = (grad_mid + norm_back(grad_normed_one * gain_one, hat_one, root_one)).astype(bf16)
    spaced = [
        jnp.pad(v.reshape(parts, gain_part), ((0, 0), (0, part - gain_part))).reshape(1, width)
        for v in (gain_query_part, gain_key_part)
    ]
    gain_sums = jnp.concatenate([gain_one_part[None], gain_two_part[None]] + spaced, axis=0)
    gain_sums = plus(gain_sums, lanes.swap(gain_sums, "c")).astype(bf16)
    gain_sums = plane_scatter(jnp.pad(gain_sums, ((0, 12), (0, 0))), sizes, pair, lanes).astype(bf16)
    value = z_scatter(
        [
            jnp.concatenate([qkv_part[i * qkv_rows : (i + 1) * qkv_rows], gain_sums], axis=0)
            for i in range(z_size)
        ],
        z_size,
        lanes,
    )
    gain_sums = lane_block(value[qkv_rows:], c, part)
    qkv_grad = core_deal(value[:qkv_rows].astype(bf16)).astype(f32)
    q_wgrad = qkv_grad[:, :q_rows].reshape(-1, part).T
    k_wgrad = qkv_grad[:, q_rows : q_rows + k_rows].reshape(-1, part).T
    v_wgrad = qkv_grad[:, q_rows + k_rows :].reshape(-1, part).T
    return (
        trade(output, "more"),
        trade(tokens_grad, "more"),
        gain_sums[0],
        q_wgrad,
        k_wgrad,
        v_wgrad,
        gain_sums[2, :gain_part],
        gain_sums[3, :gain_part],
        o_wgrad,
        gain_sums[1],
        gate_wgrad,
        up_wgrad,
        down_wgrad,
    )


def solution(mesh):
    dp, tp = mesh.devices.shape
    sizes = (dp // 4, 2, 2, tp)
    fine = Mesh(mesh.devices.reshape(sizes), ("y", "x", "c", "z"))
    d = ("y", "x", "c")
    rows, weight, gain = P((*d, "z"), None), P(d, "z"), P(d)
    return jax.shard_map(
        functools.partial(shards, sizes),
        mesh=fine,
        in_specs=(rows, P(d, None), rows, gain, weight, weight, weight, gain, gain, weight, gain)
        + (weight,) * 3,
        out_specs=(rows, rows, gain, weight, weight, weight, gain, gain, weight, gain) + (weight,) * 3,
        check_vma=False,
    )
```

time: 602 us -> 460 us (0.76)
  waiting for transfers between devices: 225 us -> 163 us
  matrix products: 73.4 us -> 22.1 us
  blocking collectives: 50.1 us -> 0 us
  Pallas kernels: 56.9 us -> 104 us
  local copies, waits for them, and re-layouts: 57 us -> 29.7 us
    ppermute x82 -> x69, waiting for transfers between devices: 225 us -> 163 us  [the longest x60 140 us: move(): got = lax.ppermute(self.wait(value, lane), axes, pairs)]
    dot_general x14 -> x8, matrix products: 73.4 us -> 22.1 us  [dot(): lax.dot_general(left, right, (((left_dim,), (right_dim,)), ((), ())), pre...]
    psum x1 -> x0, blocking collectives: 50.1 us -> none  [shards(): lax.psum(jnp.concatenate([gain_one_part, gain_two_part, gain_query_part,...]
    pallas_call x1 -> x5, Pallas kernels: 22.6 us -> 70.9 us  [call_local(): pl.pallas_call(kernel, in_specs=[pl.BlockSpec(memory_space=pltpu.SMEM)] +...]
    dynamic_update_slice x41 -> x0, local copies, waits for them, and re-layouts: 26 us -> none  [assemble(): full = lax.dynamic_update_slice(full, value, start)]
    convert_element_type x16 -> x18, other arithmetic: 13.2 us -> 19.1 us  [the longest x2 4.77 us: shards(): total = plus(total, slot_grads[step + 1]).astype(bf16)]
    ppermute x82 -> x69, starting transfers between devices: 81.2 us -> 83.1 us  [the longest x60 74.5 us: move(): got = lax.ppermute(self.wait(value, lane), axes, pairs)]
  transfers between devices with their start and end apart: 82 -> 69, of which waited for: 30 -> 23; matrix products, arithmetic and copies ran while one was open for 26% -> 19% of each run, Pallas kernels for 6% -> 17%
where the time goes in v2:
time: 460 us; the launch traced here: 453 us
  waiting for transfers between devices  163 us (35%)
  Pallas kernels  104 us (23%)
  starting transfers between devices  83.1 us (18%)
  other arithmetic  49.3 us (11%)
  local copies, waits for them, and re-layouts  29.7 us (6%)
  matrix products  22.1 us (5%)
    ppermute x60, waiting for transfers between devices, move(): got = lax.ppermute(self.wait(value, lane), axes, pairs)  140 us
    ppermute x60, starting transfers between devices, move(): got = lax.ppermute(self.wait(value, lane), axes, pairs)  74.5 us
    pallas_call x5, Pallas kernels, call_local(): pl.pallas_call(kernel, in_specs=[pl.BlockSpec(memory_space=pltpu.SMEM)] +...  70.9 us
    pallas_call x1, Pallas kernels, attend_back(): pl.pallas_call(functools.partial(attend_back_kernel, head), grid=(groups,...  22.7 us
    ppermute x9, waiting for transfers between devices, around(): lax.ppermute(v, 'z', ring(size, signs * (i + 1)))  22.4 us
    dot_general x8, matrix products, dot(): lax.dot_general(left, right, (((left_dim,), (right_dim,)), ((), ())), pre...  22.1 us
    unnamed x98, local copies, waits for them, and re-layouts  10.8 us
    pallas_call x1, Pallas kernels, attend(): pl.pallas_call(functools.partial(attend_kernel, head), grid=(groups,), in...  10.6 us
  transfers between devices with their start and end apart: 69, of which 23 were waited for; matrix products, arithmetic and copies ran while one was open for 19% of the time, Pallas kernels for 17%

profile of v2, /device:TPU:1, one launch (start us, length us, event | category | flops | bytes accessed | tf_op | source)
XLA Modules:
  0.0 452.9 jit_solution(7967554554147592132)
XLA Ops:
  10.1 4.6 %collective-permute-start = (bf16[512,1024]{1,0:T(8,128)(2,1)}, bf16[512,1024]{1,0:T(8,128)(2,1)}, u32[]{:S(2)}, u32[]{:S(2)}) collective-permute-start(bf16[512,1024]{1,0:T(8,128)(2,1)} %param.14), channel_id=1, source_target_pairs={{4,1},{1,4},{6,3},{3,6},{12,9},{9,12},{14,11},{11,14},{20,17},{17,... | collective-permute-start | bytes 3145736 | tf_op jit(solution)/shard_map/ppermute | solution.py:535
  19.0 16.1 %collective-permute-done.3 = bf16[256,256]{1,0:T(8,128)(2,1)S(1)} collective-permute-done((bf16[256,256]{1,0:T(8,128)(2,1)S(1)}, bf16[256,256]{1,0:T(8,128)(2,1)S(1)}, u32[]{:S(2)}, u32[]{:S(2)}) %collective-permute-start.3) | collective-permute-done | bytes 131104 | tf_op jit(solution)/shard_map/ppermute | solution.py:545
  38.7 5.1 %collective-permute-done.7 = bf16[3,288,256]{2,1,0:T(8,128)(2,1)S(1)} collective-permute-done((bf16[3,288,256]{2,1,0:T(8,128)(2,1)S(1)}, bf16[3,288,256]{2,1,0:T(8,128)(2,1)S(1)}, u32[]{:S(2)}, u32[]{:S(2)}) %collective-permute-start.7) | collective-permute-done | bytes 442400 | tf_op jit(solution)/shard_map/ppermute | solution.py:535
  45.0 5.3 %collective-permute-start.14 = (bf16[128,256]{1,0:T(8,128)(2,1)S(1)}, bf16[128,256]{1,0:T(8,128)(2,1)S(1)}, u32[]{:S(2)}, u32[]{:S(2)}) collective-permute-start(bf16[128,256]{1,0:T(8,128)(2,1)S(1)} %slice.165), channel_id=1, source_target_pairs={{0,1},{1,2},{2,3},{3,0},{4,5},{5,6},{6,7},{7,4},{8,9},{9,10},{10,1... | collective-permute-start | bytes 196616 | tf_op jit(solution)/shard_map/ppermute | solution.py:535
  60.0 3.8 collective-permute-start.1
  66.1 9.1 %collective-permute-done.15 = bf16[128,256]{1,0:T(8,128)(2,1)S(1)} collective-permute-done((bf16[128,256]{1,0:T(8,128)(2,1)S(1)}, bf16[128,256]{1,0:T(8,128)(2,1)S(1)}, u32[]{:S(2)}, u32[]{:S(2)}) %collective-permute-start.15) | collective-permute-done | bytes 65568 | tf_op jit(solution)/shard_map/ppermute | solution.py:535
  80.2 3.7 collective-permute-start.26
  99.7 10.6 %attend.1 = bf16[1024,512]{1,0:T(8,128)(2,1)S(1)} custom-call(f32[1024,1024]{1,0:T(8,128)S(1)} %fusion.17.qkv_ref, f32[1024,128]{1,0:T(8,128)S(1)} %copy-done.6, f32[1024,128]{1,0:T(8,128)S(1)} %copy-done.4, s32[1024,1]{1,0:T(8,128)S(1)} %copy-done.8, s32[1,1024]{1,0:T(1,128)S(1)} %broadcast_select_fusion.4.seg_row, f32[8,128]{1,0:T(8,128)S(1)} %maximum_maximum_fusion.gain_ref), custom_call_target="tpu_custom_call" | custom-call | flops 6000000000 | bytes 1000000 | tf_op jit(solution)/shard_map/attend/pallas_call | solution.py:112
  125.1 21.3 %collective-permute-done.27.refs_10_.refs_14_ = bf16[512,1024]{1,0:T(8,128)(2,1)} collective-permute-done((bf16[512,1024]{1,0:T(8,128)(2,1)}, bf16[512,1024]{1,0:T(8,128)(2,1)}, u32[]{:S(2)}, u32[]{:S(2)}) %collective-permute-start.27) | collective-permute-done | bytes 1048608 | tf_op jit(solution)/shard_map/ppermute | solution.py:535
  147.5 23.6 %collective-permute-done.28.refs_6_.refs_10_ = bf16[512,1024]{1,0:T(8,128)(2,1)S(1)} collective-permute-done((bf16[512,1024]{1,0:T(8,128)(2,1)S(1)}, bf16[512,1024]{1,0:T(8,128)(2,1)S(1)}, u32[]{:S(2)}, u32[]{:S(2)}) %collective-permute-start.28) | collective-permute-done | bytes 1048608 | tf_op jit(solution)/shard_map/ppermute | solution.py:535
  172.4 21.0 %collective-permute-done.23.refs_2_.refs_6_ = bf16[864,512]{1,0:T(8,128)(2,1)S(1)} collective-permute-done((bf16[864,512]{1,0:T(8,128)(2,1)}, bf16[864,512]{1,0:T(8,128)(2,1)S(1)}, u32[]{:S(2)}, u32[]{:S(2)}) %collective-permute-start.23) | collective-permute-done | bytes 884768 | tf_op jit(solution)/shard_map/ppermute | solution.py:535
  196.5 20.4 %ffn_first.1 = (bf16[1152,2048]{1,0:T(8,128)(2,1)}, bf16[576,2048]{1,0:T(8,128)(2,1)}, bf16[864,512]{1,0:T(8,128)(2,1)}, bf16[864,512]{1,0:T(8,128)(2,1)}, bf16[...) custom-call(s32[1]{0:T(128)} %bitcast.34.which_ref, bf16[864,512]{1,0:T(8,128)(2,1)} %maximum_select_fusion.3.refs_0_.refs_4_, ...), custom_call_target="tpu_custom_call" | custom-call | flops 14495514624 | bytes 1000000 | tf_op jit(solution)/shard_map/ffn_first/pallas_call | solution.py:243
  216.8 27.0 %ffn_second.1 = (bf16[1152,2048]{1,0:T(8,128)(2,1)}, bf16[576,2048]{1,0:T(8,128)(2,1)}, bf16[512,1024]{1,0:T(8,128)(2,1)}, bf16[512,1024]{1,0:T(8,128)(2,1)}, bf...) custom-call(s32[1]{0:T(128)} %bitcast.34.which_ref, bf16[864,512]{1,0:T(8,128)(2,1)} %collective-permute-done.13.refs_0_.refs_2_, ...), custom_call_target="tpu_custom_call" | custom-call | flops 18119393280 | bytes 1000000 | tf_op jit(solution)/shard_map/ffn_second/pallas_call | solution.py:243
  250.5 16.2 %collective-permute-done.33 = bf16[864,512]{1,0:T(8,128)(2,1)S(1)} collective-permute-done((bf16[864,512]{1,0:T(8,128)(2,1)}, bf16[864,512]{1,0:T(8,128)(2,1)S(1)}, u32[]{:S(2)}, u32[]{:S(2)}) %collective-permute-start.33) | collective-permute-done | bytes 884768 | tf_op jit(solution)/shard_map/ppermute | solution.py:535
  268.9 20.9 %ffn_third.1 = (bf16[864,512]{1,0:T(8,128)(2,1)}, bf16[864,512]{1,0:T(8,128)(2,1)}, bf16[864,512]{1,0:T(8,128)(2,1)}, bf16[864,512]{1,0:T(8,128)(2,1)}, bf16[512...) custom-call(s32[1]{0:T(128)} %bitcast.34.which_ref, ...), custom_call_target="tpu_custom_call" | custom-call | flops 10871635968 | bytes 1000000 | tf_op jit(solution)/shard_map/ffn_third/pallas_call | solution.py:243
  300.8 11.6 %collective-permute-done.43 = bf16[864,512]{1,0:T(8,128)(2,1)} collective-permute-done((bf16[864,512]{1,0:T(8,128)(2,1)}, bf16[864,512]{1,0:T(8,128)(2,1)}, u32[]{:S(2)}, u32[]{:S(2)}) %collective-permute-start.43) | collective-permute-done | bytes 884768 | tf_op jit(solution)/shard_map/ppermute | solution.py:535
  326.5 22.7 %attend_back.1 = (bf16[1024,1024]{1,0:T(8,128)(2,1)S(1)}, f32[32,128]{1,0:T(8,128)S(1)}) custom-call(f32[1024,1024]{1,0:T(8,128)} %copy-done.12, f32[1024,128]{1,0:T(8,128)S(1)} %copy-done.7, f32[1024,128]{1,0:T(8,128)S(1)} %copy-done.5, s32[1024,1]{1,0:T(8,128)S(1)} %copy-done.9, s32[1,1024]{1,0:T(1,128)S(1)} %broadcast_select_fusion.4.seg_row, ...), custom_call_target="tpu_custom_call" | custom-call | flops 12000000000 | bytes 1000000 | tf_op jit(solution)/shard_map/attend_back/pallas_call | solution.py:197
  365.0 6.4 %collective-permute-done.50 = bf16[1024,256]{1,0:T(8,128)(2,1)S(1)} collective-permute-done((bf16[1024,256]{1,0:T(8,128)(2,1)S(1)}, bf16[1024,256]{1,0:T(8,128)(2,1)S(1)}, u32[]{:S(2)}, u32[]{:S(2)}) %collective-permute-start.50) | collective-permute-done | bytes 524320 | tf_op jit(solution)/shard_map/ppermute | solution.py:535
  372.4 5.1 %collective-permute-done.55 = bf16[864,512]{1,0:T(8,128)(2,1)S(1)} collective-permute-done((bf16[864,512]{1,0:T(8,128)(2,1)S(1)}, bf16[864,512]{1,0:T(8,128)(2,1)S(1)}, u32[]{:S(2)}, u32[]{:S(2)}) %collective-permute-start.55) | collective-permute-done | bytes 884768 | tf_op jit(solution)/shard_map/ppermute | solution.py:535
  384.5 4.1 collective-permute-start.67
  390.3 3.7 fusion.11
  398.8 6.0 %collective-permute-start.38 = (bf16[512,1024]{1,0:T(8,128)(2,1)S(1)}, bf16[512,1024]{1,0:T(8,128)(2,1)}, u32[]{:S(2)}, u32[]{:S(2)}) collective-permute-start(bf16[512,1024]{1,0:T(8,128)(2,1)S(1)} %get-tuple-element.129), channel_id=1, source_target_pairs={{4,1},{1,4},{6,3},{3,6},{12,9},{9,12},{14,11},{11,14},{20,17},{17,... | collective-permute-start | bytes 3145736 | tf_op jit(solution)/shard_map/ppermute | solution.py:535
  415.1 5.8 %collective-permute-start.68 = (bf16[3,2,288,128]{3,2,1,0:T(8,128)(2,1)S(1)}, bf16[3,2,288,128]{3,2,1,0:T(8,128)(2,1)S(1)}, u32[]{:S(2)}, u32[]{:S(2)}) collective-permute-start(bf16[3,2,288,128]{3,2,1,0:T(8,128)(2,1)S(1)} %get-tuple-element.239), channel_id=1, source_target_pairs={{0,4},{4,0},{1,5},{5,1},{2,6},{6,2},{3,7},{7,3},{8,12},{12,8},{9,1... | collective-permute-start | bytes 1327112 | tf_op jit(solution)/shard_map/ppermute | solution.py:535
  442.2 8.2 %collective-permute-done.47 = bf16[512,1024]{1,0:T(8,128)(2,1)} collective-permute-done((bf16[512,1024]{1,0:T(8,128)(2,1)S(1)}, bf16[512,1024]{1,0:T(8,128)(2,1)}, u32[]{:S(2)}, u32[]{:S(2)}) %collective-permute-start.47) | collective-permute-done | bytes 1048608 | tf_op jit(solution)/shard_map/ppermute | solution.py:535
  (341 shorter events, 168.6 us)
Async XLA Ops:
  9.6 25.6 %collective-permute-start.6 = (bf16[3,2,288,128]{3,2,1,0:T(8,128)(2,1)S(1)}, bf16[3,2,288,128]{3,2,1,0:T(8,128)(2,1)S(1)}, u32[]{:S(2)}, u32[]{:S(2)}) collective-permute-start(bf16[3,2,288,128]{3,2,1,0:T(8,128)(2,1)S(1)} %get-tuple-element.245), channel_id=1, source_target_pairs={{0,4},{4,0},{1,5},{5,1},{2,6},{6,2},{3,7},{7,3},{8,12},{12,8},{9,1... | collective-permute-start | bytes 1327112 | tf_op jit(solution)/shard_map/ppermute | solution.py:535
  10.1 47.4 %collective-permute-start = (bf16[512,1024]{1,0:T(8,128)(2,1)}, bf16[512,1024]{1,0:T(8,128)(2,1)}, u32[]{:S(2)}, u32[]{:S(2)}) collective-permute-start(bf16[512,1024]{1,0:T(8,128)(2,1)} %param.14), channel_id=1, source_target_pairs={{4,1},{1,4},{6,3},{3,6},{12,9},{9,12},{14,11},{11,14},{20,17},{17,... | collective-permute-start | bytes 3145736 | tf_op jit(solution)/shard_map/ppermute | solution.py:535
  51.4 33.4 %collective-permute-start.12 = (bf16[864,512]{1,0:T(8,128)(2,1)}, bf16[864,512]{1,0:T(8,128)(2,1)}, u32[]{:S(2)}, u32[]{:S(2)}) collective-permute-start(bf16[864,512]{1,0:T(8,128)(2,1)} %maximum_select_fusion.3.refs_0_.refs_4_), channel_id=1, source_target_pairs={{0,16},{16,0},{1,17},{17,1},{2,18},{18,2},{3,19},{19,3},{4,20},{20... | collective-permute-start | bytes 2654216 | tf_op jit(solution)/shard_map/ppermute | solution.py:535
  52.6 32.7 %collective-permute-start.11 = (bf16[864,512]{1,0:T(8,128)(2,1)}, bf16[864,512]{1,0:T(8,128)(2,1)}, u32[]{:S(2)}, u32[]{:S(2)}) collective-permute-start(bf16[864,512]{1,0:T(8,128)(2,1)} %maximum_select_fusion.3.refs_0_.refs_4_), channel_id=1, source_target_pairs={{0,1},{1,2},{2,3},{3,0},{4,5},{5,6},{6,7},{7,4},{8,9},{9,10},{10,1... | collective-permute-start | bytes 2654216 | tf_op jit(solution)/shard_map/ppermute | solution.py:535
  57.2 28.6 %collective-permute-start.10 = (bf16[1040,256]{1,0:T(8,128)(2,1)S(1)}, bf16[1040,256]{1,0:T(8,128)(2,1)S(1)}, u32[]{:S(2)}, u32[]{:S(2)}) collective-permute-start(bf16[1040,256]{1,0:T(8,128)(2,1)S(1)} %collective-permute-done.9.refs_2_), channel_id=1, source_target_pairs={{0,8},{8,0},{1,9},{9,1},{2,10},{10,2},{3,11},{11,3},{4,12},{12,4},... | collective-permute-start | bytes 1597448 | tf_op jit(solution)/shard_map/ppermute | solution.py:535
  60.0 31.3 %collective-permute-start.1 = (bf16[512,1024]{1,0:T(8,128)(2,1)}, bf16[512,1024]{1,0:T(8,128)(2,1)}, u32[]{:S(2)}, u32[]{:S(2)}) collective-permute-start(bf16[512,1024]{1,0:T(8,128)(2,1)} %get-tuple-element.228), channel_id=1, source_target_pairs={{0,4},{4,0},{1,5},{5,1},{2,6},{6,2},{3,7},{7,3},{8,12},{12,8},{9,1... | collective-permute-start | bytes 3145736 | tf_op jit(solution)/shard_map/ppermute | solution.py:535
  80.2 39.4 %collective-permute-start.26 = (bf16[512,1024]{1,0:T(8,128)(2,1)}, bf16[512,1024]{1,0:T(8,128)(2,1)}, u32[]{:S(2)}, u32[]{:S(2)}) collective-permute-start(bf16[512,1024]{1,0:T(8,128)(2,1)} %param.16), channel_id=1, source_target_pairs={{4,1},{1,4},{6,3},{3,6},{12,9},{9,12},{14,11},{11,14},{20,17},{17,... | collective-permute-start | bytes 3145736 | tf_op jit(solution)/shard_map/ppermute | solution.py:535
  85.4 29.5 %collective-permute-start.13 = (bf16[864,512]{1,0:T(8,128)(2,1)}, bf16[864,512]{1,0:T(8,128)(2,1)}, u32[]{:S(2)}, u32[]{:S(2)}) collective-permute-start(bf16[864,512]{1,0:T(8,128)(2,1)} %collective-permute-done.11.refs_1_.refs_5_), channel_id=1, source_target_pairs={{0,1},{1,2},{2,3},{3,0},{4,5},{5,6},{6,7},{7,4},{8,9},{9,10},{10,1... | collective-permute-start | bytes 2654216 | tf_op jit(solution)/shard_map/ppermute | solution.py:535
  146.4 24.8 %collective-permute-start.28 = (bf16[512,1024]{1,0:T(8,128)(2,1)S(1)}, bf16[512,1024]{1,0:T(8,128)(2,1)S(1)}, u32[]{:S(2)}, u32[]{:S(2)}) collective-permute-start(bf16[512,1024]{1,0:T(8,128)(2,1)S(1)} %multiply_convert_fusion.refs_4_.refs_8_), channel_id=1, source_target_pairs={{0,8},{8,0},{1,9},{9,1},{2,10},{10,2},{3,11},{11,3},{4,12},{12,4},... | collective-permute-start | bytes 3145736 | tf_op jit(solution)/shard_map/ppermute | solution.py:535
  146.5 25.4 %collective-permute-start.22 = (bf16[864,512]{1,0:T(8,128)(2,1)}, bf16[864,512]{1,0:T(8,128)(2,1)}, u32[]{:S(2)}, u32[]{:S(2)}) collective-permute-start(bf16[864,512]{1,0:T(8,128)(2,1)} %collective-permute-done.13.refs_0_.refs_2_), channel_id=1, source_target_pairs={{0,1},{1,2},{2,3},{3,0},{4,5},{5,6},{6,7},{7,4},{8,9},{9,10},{10,1... | collective-permute-start | bytes 2654216 | tf_op jit(solution)/shard_map/ppermute | solution.py:535
  146.7 47.1 %collective-permute-start.30 = (bf16[512,1024]{1,0:T(8,128)(2,1)}, bf16[512,1024]{1,0:T(8,128)(2,1)S(1)}, u32[]{:S(2)}, u32[]{:S(2)}) collective-permute-start(bf16[512,1024]{1,0:T(8,128)(2,1)} %broadcast_select_fusion.2.refs_8_.refs_12_), channel_id=1, source_target_pairs={{0,4},{4,0},{1,5},{5,1},{2,6},{6,2},{3,7},{7,3},{8,12},{12,8},{9,1... | collective-permute-start | bytes 3145736 | tf_op jit(solution)/shard_map/ppermute | solution.py:535
  147.0 46.8 %collective-permute-start.31 = (bf16[512,1024]{1,0:T(8,128)(2,1)}, bf16[512,1024]{1,0:T(8,128)(2,1)S(1)}, u32[]{:S(2)}, u32[]{:S(2)}) collective-permute-start(bf16[512,1024]{1,0:T(8,128)(2,1)} %collective-permute-done.27.refs_10_.refs_14_), channel_id=1, source_target_pairs={{0,4},{4,0},{1,5},{5,1},{2,6},{6,2},{3,7},{7,3},{8,12},{12,8},{9,1... | collective-permute-start | bytes 3145736 | tf_op jit(solution)/shard_map/ppermute | solution.py:535
  147.3 46.5 %collective-permute-start.25 = (bf16[512,1024]{1,0:T(8,128)(2,1)S(1)}, bf16[512,1024]{1,0:T(8,128)(2,1)S(1)}, u32[]{:S(2)}, u32[]{:S(2)}) collective-permute-start(bf16[512,1024]{1,0:T(8,128)(2,1)S(1)} %multiply_convert_fusion.refs_4_.refs_8_), channel_id=1, source_target_pairs={{0,4},{4,0},{1,5},{5,1},{2,6},{6,2},{3,7},{7,3},{8,12},{12,8},{9,1... | collective-permute-start | bytes 3145736 | tf_op jit(solution)/shard_map/ppermute | solution.py:535
  246.2 45.2 %collective-permute-start.39 = (bf16[512,1024]{1,0:T(8,128)(2,1)}, bf16[512,1024]{1,0:T(8,128)(2,1)}, u32[]{:S(2)}, u32[]{:S(2)}) collective-permute-start(bf16[512,1024]{1,0:T(8,128)(2,1)} %get-tuple-element.131), channel_id=1, source_target_pairs={{0,4},{4,0},{1,5},{5,1},{2,6},{6,2},{3,7},{7,3},{8,12},{12,8},{9,1... | collective-permute-start | bytes 3145736 | tf_op jit(solution)/shard_map/ppermute | solution.py:535
  250.2 41.1 %collective-permute-start.36 = (bf16[512,1024]{1,0:T(8,128)(2,1)}, bf16[512,1024]{1,0:T(8,128)(2,1)}, u32[]{:S(2)}, u32[]{:S(2)}) collective-permute-start(bf16[512,1024]{1,0:T(8,128)(2,1)} %add_convert_fusion.2), channel_id=1, source_target_pairs={{0,8},{8,0},{1,9},{9,1},{2,10},{10,2},{3,11},{11,3},{4,12},{12,4},... | collective-permute-start | bytes 3145736 | tf_op jit(solution)/shard_map/ppermute | solution.py:535
  268.9 24.9 %collective-permute-start.40 = (bf16[864,512]{1,0:T(8,128)(2,1)}, bf16[864,512]{1,0:T(8,128)(2,1)}, u32[]{:S(2)}, u32[]{:S(2)}) collective-permute-start(bf16[864,512]{1,0:T(8,128)(2,1)} %add_convert_fusion.6), channel_id=1, source_target_pairs={{0,1},{1,2},{2,3},{3,0},{4,5},{5,6},{6,7},{7,4},{8,9},{9,10},{10,1... | collective-permute-start | bytes 2654216 | tf_op jit(solution)/shard_map/ppermute | solution.py:535
  298.3 97.2 %collective-permute-start.34 = (bf16[512,1024]{1,0:T(8,128)(2,1)}, bf16[512,1024]{1,0:T(8,128)(2,1)}, u32[]{:S(2)}, u32[]{:S(2)}) collective-permute-start(bf16[512,1024]{1,0:T(8,128)(2,1)} %get-tuple-element.124), channel_id=1, source_target_pairs={{0,4},{4,0},{1,5},{5,1},{2,6},{6,2},{3,7},{7,3},{8,12},{12,8},{9,1... | collective-permute-start | bytes 3145736 | tf_op jit(solution)/shard_map/ppermute | solution.py:535
  300.5 24.7 %collective-permute-start.37 = (bf16[512,1024]{1,0:T(8,128)(2,1)S(1)}, bf16[512,1024]{1,0:T(8,128)(2,1)S(1)}, u32[]{:S(2)}, u32[]{:S(2)}) collective-permute-start(bf16[512,1024]{1,0:T(8,128)(2,1)S(1)} %add_convert_fusion.1), channel_id=1, source_target_pairs={{0,8},{8,0},{1,9},{9,1},{2,10},{10,2},{3,11},{11,3},{4,12},{12,4},... | collective-permute-start | bytes 3145736 | tf_op jit(solution)/shard_map/ppermute | solution.py:535
  315.1 38.0 %collective-permute-start.45 = (bf16[864,512]{1,0:T(8,128)(2,1)}, bf16[864,512]{1,0:T(8,128)(2,1)}, u32[]{:S(2)}, u32[]{:S(2)}) collective-permute-start(bf16[864,512]{1,0:T(8,128)(2,1)} %get-tuple-element.145), channel_id=1, source_target_pairs={{0,16},{16,0},{1,17},{17,1},{2,18},{18,2},{3,19},{19,3},{4,20},{20... | collective-permute-start | bytes 2654216 | tf_op jit(solution)/shard_map/ppermute | solution.py:535
  315.6 37.6 %collective-permute-start.44 = (bf16[864,512]{1,0:T(8,128)(2,1)}, bf16[864,512]{1,0:T(8,128)(2,1)}, u32[]{:S(2)}, u32[]{:S(2)}) collective-permute-start(bf16[864,512]{1,0:T(8,128)(2,1)} %add_convert_fusion.5), channel_id=1, source_target_pairs={{0,1},{1,2},{2,3},{3,0},{4,5},{5,6},{6,7},{7,4},{8,9},{9,10},{10,1... | collective-permute-start | bytes 2654216 | tf_op jit(solution)/shard_map/ppermute | solution.py:535
  326.2 24.6 %collective-permute-start.48 = (bf16[512,256]{1,0:T(8,128)(2,1)}, bf16[512,256]{1,0:T(8,128)(2,1)}, u32[]{:S(2)}, u32[]{:S(2)}) collective-permute-start(bf16[512,256]{1,0:T(8,128)(2,1)} %get-tuple-element.149), channel_id=1, source_target_pairs={{0,8},{8,0},{1,9},{9,1},{2,10},{10,2},{3,11},{11,3},{4,12},{12,4},... | collective-permute-start | bytes 786440 | tf_op jit(solution)/shard_map/ppermute | solution.py:535
  362.5 27.8 %collective-permute-start.46 = (bf16[512,1024]{1,0:T(8,128)(2,1)}, bf16[512,1024]{1,0:T(8,128)(2,1)}, u32[]{:S(2)}, u32[]{:S(2)}) collective-permute-start(bf16[512,1024]{1,0:T(8,128)(2,1)} %fusion.21), channel_id=1, source_target_pairs={{0,4},{4,0},{1,5},{5,1},{2,6},{6,2},{3,7},{7,3},{8,12},{12,8},{9,1... | collective-permute-start | bytes 3145736 | tf_op jit(solution)/shard_map/ppermute | solution.py:535
  380.6 26.1 %collective-permute-start.53 = (bf16[1024,256]{1,0:T(8,128)(2,1)}, bf16[1024,256]{1,0:T(8,128)(2,1)S(1)}, u32[]{:S(2)}, u32[]{:S(2)}) collective-permute-start(bf16[1024,256]{1,0:T(8,128)(2,1)} %add_convert_fusion.8), channel_id=1, source_target_pairs={{0,16},{16,0},{1,17},{17,1},{2,18},{18,2},{3,19},{19,3},{4,20},{20... | collective-permute-start | bytes 1572872 | tf_op jit(solution)/shard_map/ppermute | solution.py:535
  398.8 35.4 %collective-permute-start.38 = (bf16[512,1024]{1,0:T(8,128)(2,1)S(1)}, bf16[512,1024]{1,0:T(8,128)(2,1)}, u32[]{:S(2)}, u32[]{:S(2)}) collective-permute-start(bf16[512,1024]{1,0:T(8,128)(2,1)S(1)} %get-tuple-element.129), channel_id=1, source_target_pairs={{4,1},{1,4},{6,3},{3,6},{12,9},{9,12},{14,11},{11,14},{20,17},{17,... | collective-permute-start | bytes 3145736 | tf_op jit(solution)/shard_map/ppermute | solution.py:535
  (88 other events, 1031.9 us)

commit v3 on v2

--- a/solution.py
+++ b/solution.py
@@ -16,7 +16,7 @@
 
 
 def cost(flops):
-    return pl.CostEstimate(flops=flops, bytes_accessed=10**6, transcendentals=0)
+    return pl.CostEstimate(flops=flops // 1000, bytes_accessed=10**5, transcendentals=0)
 
 
 def dot(left, right, left_dim, right_dim):
@@ -104,16 +104,15 @@
         ctx_ref[top:high, :] = merge_heads(mixed, head).astype(bf16)
 
 
-def attend(qkv, cosine, sine, seg_col, seg_row, gains, head):
-    length, width = qkv.shape
-    groups = width // (4 * head)
+def attend(qkv, cosine, sine, seg_col, seg_row, gains, head, first, groups):
+    length = qkv.shape[0]
     lanes = 2 * head
     whole = lambda shape: pl.BlockSpec(shape, lambda j: (0, 0))
     return pl.pallas_call(
         functools.partial(attend_kernel, head),
         grid=(groups,),
         in_specs=[
-            pl.BlockSpec((length, 2 * lanes), lambda j: (0, j)),
+            pl.BlockSpec((length, 2 * lanes), lambda j: (0, j + first)),
             whole((length, lanes)),
             whole((length, lanes)),
             whole((length, 1)),
@@ -123,7 +122,7 @@
         out_specs=pl.BlockSpec((length, lanes), lambda j: (0, j)),
         out_shape=jax.ShapeDtypeStruct((length, groups * lanes), bf16),
         scratch_shapes=[pltpu.VMEM((length, lanes), bf16)] * 3,
-        compiler_params=pltpu.CompilerParams(vmem_limit_bytes=40 * 2**20),
+        compiler_params=pltpu.CompilerParams(vmem_limit_bytes=24 * 2**20),
         cost_estimate=cost(6 * 10**9),
         name="attend",
     )(qkv, cosine, sine, seg_col, seg_row, gains)
@@ -189,33 +188,32 @@
     sums_ref[...] = jnp.where(which == 0, q_sum, jnp.where(which == 1, k_sum, 0.0))
 
 
-def attend_back(qkv, cosine, sine, seg_col, seg_row, gains, grad_context, head):
-    length, width = qkv.shape
-    groups = width // (4 * head)
+def attend_back(qkv, cosine, sine, seg_col, seg_row, gains, grad_context, head, first, groups):
+    length = qkv.shape[0]
     lanes = 2 * head
     whole = lambda shape: pl.BlockSpec(shape, lambda j: (0, 0))
     return pl.pallas_call(
         functools.partial(attend_back_kernel, head),
         grid=(groups,),
         in_specs=[
-            pl.BlockSpec((length, 2 * lanes), lambda j: (0, j)),
+            pl.BlockSpec((length, 2 * lanes), lambda j: (0, j + first)),
             whole((length, lanes)),
             whole((length, lanes)),
             whole((length, 1)),
             whole((1, length)),
             whole((8, lanes)),
-            pl.BlockSpec((length, lanes), lambda j: (0, j)),
+            pl.BlockSpec((length, lanes), lambda j: (0, j + first)),
         ],
         out_specs=(
             pl.BlockSpec((length, 2 * lanes), lambda j: (0, j)),
             pl.BlockSpec((8, lanes), lambda j: (j, 0)),
         ),
         out_shape=(
-            jax.ShapeDtypeStruct((length, width), bf16),
+            jax.ShapeDtypeStruct((length, groups * 2 * lanes), bf16),
             jax.ShapeDtypeStruct((8 * groups, lanes), f32),
         ),
         scratch_shapes=[pltpu.VMEM((length, lanes), bf16)] * 3 + [pltpu.VMEM((length, lanes), f32)] * 3,
-        compiler_params=pltpu.CompilerParams(vmem_limit_bytes=48 * 2**20),
+        compiler_params=pltpu.CompilerParams(vmem_limit_bytes=58 * 2**20),
         cost_estimate=cost(12 * 10**9),
         name="attend_back",
     )(qkv, cosine, sine, seg_col, seg_row, gains, grad_context)
@@ -272,17 +270,22 @@
         self.wait(*list(self.open))
 
 
-def load_weights(loads, key, near, far, which_ref, gate_up, down, slots):
+def load_gate_up(loads, key, near, far, which_ref, target, slots):
     size, half = near[0].shape
     top = 2 * size // 3
-    first, second = halves(which_ref, half)
-    for i in slots:
-        for piece, lanes in ((near[i], first), (far[i], second)):
-            if gate_up is not None:
-                loads.start((key, i), (piece.at[pl.ds(0, top)], gate_up.at[pl.ds(i * top, top), lanes]))
-            if down is not None:
-                rest = size - top
-                loads.start((key, i), (piece.at[pl.ds(top, rest)], down.at[pl.ds(i * rest, rest), lanes]))
+    for at, i in enumerate(slots):
+        for pieces, lanes in zip((near, far), halves(which_ref, half)):
+            loads.start((key, at), (pieces[i].at[pl.ds(0, top)], target.at[pl.ds(at * top, top), lanes]))
+
+
+def load_down(loads, key, near, far, which_ref, target, slots):
+    size, half = near[0].shape
+    rest = size // 3
+    for at, i in enumerate(slots):
+        for pieces, lanes in zip((near, far), halves(which_ref, half)):
+            loads.start(
+                (key, at), (pieces[i].at[pl.ds(size - rest, rest)], target.at[pl.ds(at * rest, rest), lanes])
+            )
 
 
 def hidden_step(gate_up, down, rows, cot, gu_s, hid_s, slot, columns, sub):
@@ -298,14 +301,15 @@
 
 
 def weight_step(loads, which_ref, gu_s, hid_s, rows_s, cot_s, out_s, far_out, near_out, order, sub):
-    half = far_out[0].shape[1]
+    size, half = 3 * sub, rows_s.shape[1] // 2
     first, second = halves(which_ref, half)
     for side, lanes, outs in ((0, second, far_out), (1, first, near_out)):
         rows, cots = rows_s[:, lanes], cot_s[:, lanes]
-        for s in order:
+        for at, s in enumerate(order):
             out_s[side, s, : 2 * sub] = dot(gu_s[2 * s * sub : 2 * (s + 1) * sub, :], rows, 1, 0).astype(bf16)
             out_s[side, s, 2 * sub :] = dot(hid_s[s * sub : (s + 1) * sub, :], cots, 1, 0).astype(bf16)
-            loads.start("out", (out_s.at[side, s], outs[s]))
+            target = outs[s] if len(outs) > 1 else outs[0].at[pl.ds(at * size, size)]
+            loads.start("out", (out_s.at[side, s], target))
 
 
 def take(refs, *counts):
@@ -318,7 +322,7 @@
 
 def first_kernel(slots, quarters, order, which_ref, *refs):
     near, far, rows, cots, (gu_out, hid_out), far_out, near_out, rest = take(
-        refs, slots, slots, quarters, quarters, 2, slots, slots
+        refs, slots, slots, quarters, quarters, 2, 1, 1
     )
     gate_up, down, rows_s, cot_s, gu_s, hid_s, out_s, sems = rest
     sub, count = near[0].shape[0] // 3, rows[0].shape[0]
@@ -327,8 +331,9 @@
         if q < quarters:
             place = pl.ds(q * count, count)
             loads.start(("rows", q), (rows[q], rows_s.at[place]), (cots[q], cot_s.at[place]))
-        if q < slots:
-            load_weights(loads, "w", near, far, which_ref, gate_up, down, [q])
+        if q == 0:
+            load_gate_up(loads, "w", near, far, which_ref, gate_up, range(slots))
+            load_down(loads, "w", near, far, which_ref, down, range(slots))
     for q in range(quarters):
         columns = slice(q * count, (q + 1) * count)
         loads.wait(("rows", q))
@@ -351,8 +356,8 @@
         which,
         [*near, *far, *rows, *cots],
         [jax.ShapeDtypeStruct(v, bf16) for v in (gu, hid)]
-        + [jax.ShapeDtypeStruct((size, half), bf16)] * (2 * slots),
-        [pl.ANY] * (2 + 2 * slots),
+        + [jax.ShapeDtypeStruct((slots * size, half), bf16)] * 2,
+        [pl.ANY] * 4,
         [
             pltpu.VMEM((2 * slots * sub, 2 * half), bf16),
             pltpu.VMEM((slots * sub, 2 * half), bf16),
@@ -366,38 +371,37 @@
         8 * slots * size * half * tokens,
         "ffn_first",
     )
-    return out[0], out[1], out[2 : 2 + slots], out[2 + slots :]
+    return out
 
 
 def second_kernel(slots, quarters, which_ref, *refs):
-    near, far, near_0, far_0, rows, cots, (gu_0,), (gu_out, hid_out), outs, rest = take(
-        refs, slots, slots, slots, slots, quarters, quarters, 1, 2, quarters
+    near, far, rows, cots, (gu_0,), (gu_out, hid_out), outs, rest = take(
+        refs, 2 * slots, 2 * slots, quarters, quarters, 1, 2, quarters
     )
     gate_up, down, gate_up_0, rows_s, cot_s, gu_s, hid_s, gu_0s, out_s, sems = rest
     sub, count = near[0].shape[0] // 3, rows[0].shape[0]
     loads = Loads(sems)
-    turn = [(i + quarters // 2) % quarters for i in range(quarters)]
-    for i in range(max(slots, quarters)):
-        if i < quarters:
-            q = turn[i]
-            place = pl.ds(q * count, count)
-            loads.start(("rows", q), (rows[q], rows_s.at[place]), (cots[q], cot_s.at[place]))
-        if i < slots:
-            load_weights(loads, "w", near, far, which_ref, gate_up, down, [i])
-        if i == slots - 1:
-            load_weights(loads, "w0", near_0, far_0, which_ref, gate_up_0, None, range(slots))
-            loads.start("g0", (gu_0, gu_0s))
-    for q in turn:
+    for q in range(quarters):
+        place = pl.ds(q * count, count)
+        loads.start(("rows", q), (rows[q], rows_s.at[place]), (cots[q], cot_s.at[place]))
+        if q == 0:
+            load_gate_up(loads, "w", near, far, which_ref, gate_up, range(slots, 2 * slots))
+            load_down(loads, "w", near, far, which_ref, down, range(slots, 2 * slots))
+    load_gate_up(loads, "w0", near, far, which_ref, gate_up_0, range(slots))
+    loads.start("g0", (gu_0, gu_0s))
+    for q in range(quarters):
         columns = slice(q * count, (q + 1) * count)
         loads.wait(("rows", q))
         for s in range(slots):
             loads.wait(("w", s))
             hidden_step(gate_up, down, rows_s[columns, :], cot_s[columns, :], gu_s, hid_s, s, columns, sub)
-        loads.wait("g0", *(("w0", s) for s in range(slots)))
+    loads.start("out", (gu_s, gu_out), (hid_s, hid_out))
+    loads.wait("g0", *(("w0", s) for s in range(slots)))
+    for q in range(quarters):
+        columns = slice(q * count, (q + 1) * count)
         total = dot(gu_0s[:, columns], gate_up_0[...], 0, 0) + dot(gu_s[:, columns], gate_up[...], 0, 0)
         out_s[q] = total.astype(bf16)
         loads.start("out", (out_s.at[q], outs[q]))
-    loads.start("out", (gu_s, gu_out), (hid_s, hid_out))
     loads.close()
 
 
@@ -410,7 +414,7 @@
     out = call_local(
         functools.partial(second_kernel, slots, quarters),
         which,
-        [*near[slots:], *far[slots:], *near[:slots], *far[:slots], *rows, *cots, gu_0],
+        [*near, *far, *rows, *cots, gu_0],
         [jax.ShapeDtypeStruct(v, bf16) for v in (gu, hid)]
         + [jax.ShapeDtypeStruct((count, 2 * half), bf16)] * quarters,
         [pl.ANY] * (2 + quarters),
@@ -437,30 +441,28 @@
         refs, 2 * slots, 2 * slots, quarters, quarters, 3, slots, slots, quarters
     )
     down, rows_s, cot_s, gu_s, hid_s, hid_0s, grad_s, out_s, sems = rest
-    sub, count = near[0].shape[0] // 3, rows[0].shape[0]
+    sub, count = far_out[0].shape[0] // 3, rows[0].shape[0]
     loads = Loads(sems)
-    for q in range(quarters):
-        loads.start("rows", (rows[q], rows_s.at[pl.ds(q * count, count)]))
+    load_down(loads, "w", near, far, which_ref, down, range(2 * slots))
+    loads.start("h", (hid_0, hid_0s), (hid, hid_s))
     loads.start("rows", (gu, gu_s))
     for q in range(quarters):
-        loads.start("rows", (cots[q], cot_s.at[pl.ds(q * count, count)]))
-    loads.start("rows", (hid, hid_s))
-    load_weights(loads, "w", near, far, which_ref, None, down, range(2 * slots))
-    loads.start("h0", (hid_0, hid_0s))
-    loads.wait("rows")
-    weight_step(loads, which_ref, gu_s, hid_s, rows_s, cot_s, grad_s, far_out, near_out, order, sub)
-    loads.wait("h0", *(("w", s) for s in range(2 * slots)))
+        place = pl.ds(q * count, count)
+        loads.start("rows", (rows[q], rows_s.at[place]), (cots[q], cot_s.at[place]))
+    loads.wait("h", *(("w", s) for s in range(2 * slots)))
     for q in range(quarters):
         columns = slice(q * count, (q + 1) * count)
         total = dot(hid_0s[:, columns], down[: slots * sub, :], 0, 0)
         total = total + dot(hid_s[:, columns], down[slots * sub :, :], 0, 0)
         out_s[q] = total.astype(bf16)
         loads.start("out", (out_s.at[q], outs[q]))
+    loads.wait("rows")
+    weight_step(loads, which_ref, gu_s, hid_s, rows_s, cot_s, grad_s, far_out, near_out, order, sub)
     loads.close()
 
 
 def ffn_third(which, near, far, rows, cots, gu, hid, hid_0, order):
-    slots, quarters = len(near) // 2, len(rows)
+    slots, quarters = len(order), len(rows)
     size, half = near[0].shape
     sub, count = size // 3, rows[0].shape[0]
     tokens = quarters * count
@@ -488,32 +490,98 @@
     return out[:slots], out[slots : 2 * slots], out[2 * slots :]
 
 
-def place_kernel(count, starts_ref, *refs):
+def qkv_grads_kernel(groups, spaced, starts_ref, grads_0, grads_1, rows, weights, extra_ref, gain_ref, sums_0, sums_1, *refs):
+    outs, rest = refs[:4], refs[4:]
+    grad_s, rows_s, weight_s, extra_s, gain_s, sums_s, out_s, sems = rest
+    size = (grads_0.shape[1] + grads_1.shape[1]) // groups
+    width = outs[0].shape[1]
+    more = extra_ref.shape[0]
+    cut = grads_0.shape[1]
+    loads = Loads(sems)
+    loads.start("a", (grads_0, grad_s.at[:, pl.ds(0, cut)]), (grads_1, grad_s.at[:, pl.ds(cut, grads_1.shape[1])]))
+    loads.start("a", (rows, rows_s))
+    loads.start("b", (weights.at[pl.ds(0, groups * size)], weight_s), (extra_ref, extra_s), (gain_ref, gain_s))
+    loads.start("b", (sums_0, sums_s.at[pl.ds(0, sums_0.shape[0])]))
+    loads.start("b", (sums_1, sums_s.at[pl.ds(sums_0.shape[0], sums_1.shape[0])]))
+    loads.wait("a")
+    for i in range(4):
+        lanes = pl.ds(pl.multiple_of(starts_ref[i], width), width)
+        block = dot(grad_s[...], rows_s[:, lanes], 0, 0)
+        if i == 0:
+            loads.wait("b")
+        gain_row = jnp.sum(block * weight_s[:, lanes].astype(f32), axis=0, keepdims=True)
+        gain_row = gain_row / gain_s[0:1, lanes]
+        row = lax.broadcasted_iota(jnp.int32, (more, width), 0)
+        extra = jnp.where(row == 0, gain_row, extra_s[:, lanes])
+        if not spaced:
+            sums = sums_s[0:8, :]
+            for g in range(1, groups):
+                sums = sums + sums_s[8 * g : 8 * (g + 1), :]
+            head = sums.shape[1] // 2
+            query = sums[0:1, :] + pltpu.roll(sums[0:1, :], head, 1)
+            lane = lax.broadcasted_iota(jnp.int32, query.shape, 1)
+            both = jnp.where(lane < head, query, pltpu.roll(sums[1:2, :], head, 1))
+            both = jnp.concatenate([both] * (width // (2 * head)), axis=1)
+            extra = jnp.where(row == 2, both, extra)
+        extra = extra.astype(bf16)
+        for g in range(groups):
+            base = g * (size + more)
+            out_s[i, base : base + size, :] = block[g * size : (g + 1) * size, :].astype(bf16)
+            out_s[i, base + size : base + size + more, :] = extra
+        loads.start("out", (out_s.at[i], outs[i]))
+    loads.close()
+
+
+def qkv_grads(starts, grads, rows, weights, extra, gains, sums, groups, spaced):
+    count, width = rows.shape
+    columns, more = grads[0].shape[1] + grads[1].shape[1], extra.shape[0]
+    block = (columns + groups * more, width // 4)
+    return call_local(
+        functools.partial(qkv_grads_kernel, groups, spaced),
+        jnp.stack(starts).astype(jnp.int32),
+        [*grads, rows, weights, extra, gains, *sums],
+        [jax.ShapeDtypeStruct(block, bf16)] * 4,
+        [pl.ANY] * 4,
+        [
+            pltpu.VMEM((count, columns), bf16),
+            pltpu.VMEM((count, width), bf16),
+            pltpu.VMEM((columns, width), bf16),
+            pltpu.VMEM((more, width), f32),
+            pltpu.VMEM(gains.shape, f32),
+            pltpu.VMEM((8 * groups, sums[0].shape[1]), f32),
+            pltpu.VMEM((4, *block), bf16),
+        ],
+        12,
+        10**9,
+        "qkv_grads",
+    )
+
+
+def place_kernel(count, parts, starts_ref, *refs):
     width = refs[0].shape[1]
-    sems = refs[-1]
-    finish(
-        pull(
-            [(refs[i], refs[count].at[:, pl.ds(pl.multiple_of(starts_ref[i], width), width)]) for i in range(count)],
-            sems,
-            0,
-        )
-    )
-
-
-def place_lanes(blocks, starts):
-    rows, width = blocks[0].shape
+    loads = Loads(refs[-1])
+    for i in range(count):
+        lanes = pl.ds(pl.multiple_of(starts_ref[i], width), width)
+        for low, rows, out, place in parts:
+            target = refs[count + out].at[pl.ds(place, rows), lanes]
+            loads.start("a", (refs[i].at[pl.ds(low, rows)], target))
+    loads.close()
+
+
+def place_lanes(blocks, starts, parts, sizes):
+    width = len(blocks) * blocks[0].shape[1]
     return call_local(
-        functools.partial(place_kernel, len(blocks)),
+        functools.partial(place_kernel, len(blocks), parts),
         jnp.stack(starts).astype(jnp.int32),
         blocks,
-        [jax.ShapeDtypeStruct((rows, len(blocks) * width), bf16)],
-        [pl.ANY],
+        [jax.ShapeDtypeStruct((rows, width), bf16) for rows in sizes],
+        [pl.ANY] * len(sizes),
         [],
-        len(blocks),
+        len(blocks) * len(parts),
         10**9,
         "place_lanes",
         4,
-    )[0]
+    )
 
 
 def after(value, *earlier):
@@ -567,18 +635,22 @@
     return total
 
 
-def plane_gather(value, sizes, lanes):
+def plane_gather(value, sizes, lanes, parts, heights):
     y_size, x_size = sizes[:2]
     y, x = lax.axis_index("y"), lax.axis_index("x")
     if y_size > 2:
         wide = by_index(x, value, lanes.swap(value, "x"), -1)
         wide = lax.all_gather(wide, "y", axis=0)
-        return jnp.concatenate([wide[i] for i in range(y_size)], axis=-1)
+        wide = jnp.concatenate([wide[i] for i in range(y_size)], axis=-1)
+        return [
+            jnp.concatenate([wide[low : low + rows] for low, rows, to, _ in parts if to == out], axis=0)
+            for out in range(len(heights))
+        ]
     width = value.shape[1]
     far = lanes.swap(value, "y")
     blocks = [value, lanes.swap(value, "x"), far, lanes.swap(far, "x")]
     starts = [(a * x_size + b) * width for a in (y, 1 - y) for b in (x, 1 - x)]
-    return place_lanes(blocks, starts)
+    return place_lanes(blocks, starts, parts, heights)
 
 
 def plane_scatter(value, sizes, pair, lanes):
@@ -639,50 +711,54 @@
     qt, kt, vt, ot = q_weight.T, k_weight.T, v_weight.T, o_weight.T
     q_rows, k_rows = qt.shape[0] // 2, kt.shape[0] // 2
     qkv_rows = q_rows + 2 * k_rows
+    qkv_pack = jnp.concatenate([v.reshape(2, -1, part) for v in (qt, kt, vt, ot)], axis=1)
+    qkv_pack = qkv_pack.reshape(-1, part)
+    qkv_slots = [qkv_pack, *lanes.around([qkv_pack] * (z_size - 1), z_size, 1, "z")]
+
+    sub = gate_weight.shape[1] // (x_size * c_size)
+    ffn_pack = jnp.stack([v.T for v in (gate_weight, up_weight, down_weight)]).reshape(
+        3, x_size, c_size, sub, part
+    )
+    mine = lax.dynamic_index_in_dim(ffn_pack, x, 1, keepdims=False)
+    other = lax.dynamic_index_in_dim(ffn_pack, 1 - x, 1, keepdims=False)
+    ffn_pack = by_index(x, mine, lanes.swap(other, "x"), -1)
+    mine = lax.dynamic_index_in_dim(ffn_pack, c, 1, keepdims=False)
+    other = lax.dynamic_index_in_dim(ffn_pack, 1 - c, 1, keepdims=False)
+    ffn_ready = other
+    other = lanes.swap(other, "c")
+    ffn_own = jnp.concatenate(
+        [
+            by_index(c, mine[..., i * part : (i + 1) * part], other[..., i * part : (i + 1) * part], -1)
+            for i in range(x_size)
+        ],
+        axis=-1,
+    ).reshape(3 * sub, quad)
+
     gain_rows = jnp.concatenate(
         [attn_gain[None], ffn_gain[None]]
         + [jnp.pad(g, (0, part - gain_part))[None] for g in (query_gain, key_gain)]
         + [jnp.zeros((12, part), bf16)],
         axis=0,
     )
-    seg_rows = seq_count * length // part
-    numbers = segments.astype(bf16).reshape(seg_rows, part)
-    pack = jnp.concatenate(
-        [v.reshape(2, -1, part) for v in (qt, kt, vt)]
-        + [
-            jnp.broadcast_to(gain_rows, (2, 16, part)),
-            ot.reshape(2, q_rows, part),
-            jnp.broadcast_to(numbers, (2, seg_rows, part)),
-        ],
-        axis=1,
-    )
-    mine = lax.dynamic_index_in_dim(pack, c, 0, keepdims=False)
-    other = lax.dynamic_index_in_dim(pack, 1 - c, 0, keepdims=False)
-    got = lanes.swap(other, "c")
-    pack_end = qkv_rows + 16 + q_rows
-    pack = by_index(c, mine[:pack_end], got[:pack_end], -1)
-    other_segments = got[pack_end:].astype(jnp.int32).reshape(seq_count, length)
-
-    sub = gate_weight.shape[1] // (x_size * c_size)
-    ffn_pack = jnp.stack([after(v, other).T for v in (gate_weight, up_weight, down_weight)]).reshape(
-        3, x_size, c_size, sub, part
-    )
-    mine = lax.dynamic_index_in_dim(ffn_pack, c, 2, keepdims=False)
-    other = lax.dynamic_index_in_dim(ffn_pack, 1 - c, 2, keepdims=False)
-    ffn_pack = by_index(c, mine, lanes.swap(other, "c"), -1)
-    mine = lax.dynamic_index_in_dim(ffn_pack, x, 1, keepdims=False)
-    other = lax.dynamic_index_in_dim(ffn_pack, 1 - x, 1, keepdims=False)
-    ffn_own = by_index(x, mine, lanes.swap(other, "x"), -1).reshape(3 * sub, quad)
-
-    qkv_own = pack[:qkv_rows]
-    qkv_own = jnp.concatenate(
-        [qkv_own, *lanes.around([qkv_own] * (z_size - 1), z_size, 1, "z"), pack[qkv_rows : qkv_rows + 16]],
-        axis=0,
-    )
+    numbers = segments.astype(bf16).reshape(-1, part)
+    slot_rows = qkv_rows + q_rows
+
+    def rows_of(core):
+        return [lax.dynamic_slice_in_dim(v, core * slot_rows, slot_rows, 0) for v in qkv_slots]
+
+    height = z_size * slot_rows + 16
+    got = jnp.concatenate([*rows_of(1 - c), gain_rows, numbers], axis=0)
+    got = lanes.swap(after(got, ffn_ready), "c")
+    own = by_index(c, jnp.concatenate([*rows_of(c), gain_rows], axis=0), got[:height], -1)
+    other_segments = got[height:].astype(jnp.int32).reshape(seq_count, length)
+
     all_tokens = by_index(c, tokens, lanes.swap(tokens, "c"), 0).astype(f32)
-    qkv_all = plane_gather(qkv_own, sizes, lanes)
-    qkv_full = qkv_all[: z_size * qkv_rows]
-    gains = qkv_all[z_size * qkv_rows :].astype(f32)
+    gathered = [(i * slot_rows, qkv_rows, 0, i * qkv_rows) for i in range(z_size)]
+    gathered += [(i * slot_rows + qkv_rows, q_rows, 2, i * q_rows) for i in range(z_size)]
+    gathered += [(z_size * slot_rows, 16, 1, 0)]
+    heights = (z_size * qkv_rows, 16, z_size * q_rows)
+    qkv_full, gains, o_full = plane_gather(own, sizes, lanes, gathered, heights)
+    gains = gains.astype(f32)
     gain_one, gain_two = gains[0:1], gains[1:2]
     gain_query, gain_key = (
         gains[i].reshape(parts, part)[:, :gain_part].reshape(1, head) for i in (2, 3)
@@ -702,17 +778,12 @@
             wide.append((piece, lanes.swap(piece, "y")))
 
     over_y(ffn_own)
-    lanes.last["more"] = lanes.last["z"]
-    o_own = [pack[qkv_rows + 16 :]]
-    for _ in range(1, z_size):
-        o_own.append(lanes.move(o_own[-1], "z", ring(z_size), "more"))
-    o_full = plane_gather(jnp.concatenate(o_own, axis=0), sizes, lanes)
-    cotangent = trade(cotangent, "more")
     for _ in range(1, z_size):
         pieces.append(lanes.move(pieces[-1], "z", ring(z_size), "z"))
         over_y(pieces[-1])
+    near, far = [w[0] for w in wide], [w[1] for w in wide]
+    cotangent = trade(cotangent, None)
     which = (y if y_size == 2 else y * 0).astype(jnp.int32).reshape(1)
-    near, far = [w[0] for w in wide], [w[1] for w in wide]
 
     segment = lax.dynamic_index_in_dim(
         jnp.where(c == z % 2, segments, other_segments), z // 2, 0, keepdims=False
@@ -732,8 +803,13 @@
     hat_one = inputs * root_one
     all_root = lax.rsqrt(jnp.mean(all_tokens * all_tokens, axis=-1, keepdims=True) + epsilon)
     normed_one = (all_tokens * all_root * gain_one).astype(bf16)
-    qkv = dot(after(normed_one, pieces[1], wide[0][1]), qkv_full, 1, 1)
-    context = attend(qkv, cosine, sine, seg_col, seg_row, head_gains, head)
+    normed_one = after(normed_one, pieces[1])
+    qkv = dot(normed_one, qkv_full, 1, 1)
+    qkv = after(qkv, cotangent)
+    tables = (cosine, sine, seg_col, seg_row, head_gains, head)
+    context = attend(qkv, *tables, 0, z_size // 2)
+    qkv = after(qkv, context, pieces[z_size // 2], far[0])
+    context = jnp.concatenate([context, attend(qkv, *tables, z_size // 2, z_size - z_size // 2)], axis=1)
 
     def half_rows(value, index):
         return lax.dynamic_slice_in_dim(value, index * own_rows, own_rows, 0)
@@ -743,16 +819,17 @@
         kept = dot(half_rows(left, c), right, 1, right_dim)
         return kept + lanes.swap(sent, "c").astype(f32)
 
-    def spread(value):
+    def spread(value, *earlier):
         across = lanes.swap(value, "x")
-        return [value, lanes.swap(value, "c"), across, lanes.swap(across, "c")]
+        over = lanes.swap(after(across, *earlier) if earlier else across, "c")
+        return [value, lanes.swap(value, "c"), across, over]
 
     cots = spread(cotangent)
-    mid = inputs + core_reduce(after(context, pieces[z_size // 2], wide[1][1]), o_full, 0)
+    mid = inputs + core_reduce(after(context, cots[2], far[1]), o_full, 0)
     root_two = lax.rsqrt(jnp.mean(mid * mid, axis=-1, keepdims=True) + epsilon)
     hat_two = mid * root_two
     normed_two = (hat_two * gain_two).astype(bf16)
-    rows_two = spread(normed_two)
+    rows_two = spread(normed_two, far[-2])
 
     count = z_size // 2
     slot_grads, arrived = [None] * z_size, [None] * z_size
@@ -760,30 +837,32 @@
     def turn(group):
         return sorted(range(count), key=lambda i: (group * count + i - 1) % z_size)
 
-    def send_gradients(group, sent, kept):
-        for i in turn(group):
-            slot = group * count + i
-            if y_size > 2:
-                full = jnp.concatenate([kept[i], sent[i]], axis=1)
-                full = jnp.stack([full[:, k * quad : (k + 1) * quad] for k in range(y_size)])
-                arrived[slot] = lax.psum_scatter(full, "y", scatter_dimension=0, tiled=False)
-                slot_grads[slot] = arrived[slot].astype(f32)
-            else:
-                arrived[slot] = lanes.swap(sent[i], "y")
-                slot_grads[slot] = plus(kept[i], arrived[slot])
+    def send_gradients(sent, kept):
+        if y_size > 2:
+            full = jnp.concatenate([kept, sent], axis=1)
+            full = jnp.stack([full[:, k * quad : (k + 1) * quad] for k in range(y_size)])
+            got = lax.psum_scatter(full, "y", scatter_dimension=0, tiled=False)
+            return got, got.astype(f32)
+        got = lanes.swap(sent, "y")
+        return got, plus(kept, got)
 
     gu_0, hid_0, sent, kept = ffn_first(which, near[:count], far[:count], rows_two, cots, turn(0))
-    send_gradients(0, sent, kept)
+    arrived[1], value = send_gradients(sent, kept)
+    for i, slot in enumerate(turn(0)):
+        slot_grads[slot] = value[i * 3 * sub : (i + 1) * 3 * sub]
     gu_1, hid_1, (first, second, third, fourth) = ffn_second(which, near, far, rows_two, cots, gu_0)
     third = plus(third, lanes.swap(fourth, "c")).astype(bf16)
     across = lanes.swap(third, "x")
     second = lanes.swap(second, "c")
     sent, kept, (out_first, out_second, out_third, out_fourth) = ffn_third(
-        after(which, third, arrived[1]), near, far, rows_two, cots, gu_1, hid_1, hid_0, turn(1)
-    )
-    send_gradients(1, sent, kept)
-    total = lanes.move(slot_grads[1].astype(bf16), "z", ring(z_size), "z")
-    grad_normed_two = after(plus(first, second, across), total, arrived[0])
+        after(which, third), near, far, rows_two, cots, gu_1, hid_1, hid_0, turn(1)
+    )
+    for i in turn(1):
+        lanes.last.pop("y", None)
+        arrived[count + i], slot_grads[count + i] = send_gradients(sent[i], kept[i])
+    ring_first = slot_grads[1].astype(bf16)
+    total = lanes.move(ring_first, "z", ring(z_size), "z")
+    grad_normed_two = after(plus(first, second, across), out_first)
 
 
     def norm_back(grad, hat, root):
@@ -796,33 +875,78 @@
     branch = by_index(c, branch_own, lanes.swap(branch_own, "c"), 0)
     grad_context = dot(branch, o_full, 1, 1).astype(bf16)
     o_grad = dot(after(context, grad_context), branch, 0, 0).astype(bf16)
-    grad_qkv, head_sums = attend_back(
-        qkv, cosine, sine, seg_col, seg_row, head_gains, after(grad_context, o_grad, arrived[2]), head
-    )
+    grad_context = after(grad_context, o_grad, ring_first)
+    grad_first, sums_first = attend_back(qkv, *tables[:-1], grad_context, head, 0, z_size // 2)
+    if y_size > 2:
+        o_part = plane_scatter(o_grad, sizes, pair, lanes).astype(bf16)
+        o_far = o_part
+    else:
+        block = lambda a, b: lane_block(o_grad, a * x_size + b, pair)
+        o_far = lanes.move(block(1 - y, 1 - x), "x", [(0, 1), (1, 0)], None)
+        o_near = lanes.move(block(y, 1 - x), "x", [(0, 1), (1, 0)], None)
+        o_far = plus(block(1 - y, x), after(o_far, grad_first)).astype(bf16)
+        o_part = plus(block(y, x), o_near)
+    total = plus(after(total, grad_first), slot_grads[2]).astype(bf16)
+    grad_last, sums_last = attend_back(
+        qkv, *tables[:-1], after(grad_context, total, o_far), head, z_size // 2, z_size - z_size // 2
+    )
+    if y_size == 2:
+        o_far = lanes.move(o_far, "y", [(0, 1), (1, 0)], None)
+        o_part = plus(o_part, after(o_far, grad_last)).astype(bf16)
+    total = lanes.move(total, "z", ring(z_size), "z")
     out_third = plus(out_third, lanes.swap(out_fourth, "c")).astype(bf16)
-    out_across = lanes.swap(out_third, "x")
-    output = (mid + plus(out_first, lanes.swap(out_second, "c"), out_across)).astype(bf16)
-    o_part = plane_scatter(o_grad, sizes, pair, lanes).astype(bf16)
-    for step in range(1, z_size - 1):
-        total = plus(total, slot_grads[step + 1]).astype(bf16)
+    out_third = after(out_third, grad_normed_two)
+    out_across = lanes.move(out_third, "x", [(0, 1), (1, 0)], None)
+    output = mid + plus(out_first, lanes.swap(out_second, "c"), after(out_across, grad_first))
+    output = output.astype(bf16)
+    grad_last = after(grad_last, o_part, arrived[-1])
+    for step in range(2, z_size - 1):
+        total = plus(after(total, grad_last), slot_grads[step + 1]).astype(bf16)
+        grad_last = after(grad_last, total)
         total = lanes.move(total, "z", ring(z_size), "z")
-        if step == 1:
-            grad_qkv = after(grad_qkv, total, arrived[-1])
-    total = plus(total, slot_grads[0])
-
-    head_sums = jnp.sum(head_sums.reshape(-1, 8, 2 * head), axis=0)
-    gain_query_part = head_sums[0, :head] + head_sums[0, head:]
-    gain_key_part = head_sums[1, :head]
-    qkv_grad = dot(grad_qkv, normed_one, 0, 0).astype(bf16)
-    qkv_part = plane_scatter(qkv_grad, sizes, pair, lanes).astype(bf16)
-    grad_normed_one = core_reduce(after(grad_qkv, qkv_grad), qkv_full, 0)
+    total_last = plus(total, slot_grads[0])
+    extra = [jnp.zeros((1, width), f32), gain_two_part[None], jnp.zeros((14, width), f32)]
+    spaced = part < 2 * head
+    if spaced:
+        sums = jnp.sum(jnp.concatenate([sums_first, sums_last]).reshape(-1, 8, 2 * head), axis=0)
+        extra[2:] = [
+            jnp.pad(v.reshape(parts, gain_part), ((0, 0), (0, part - gain_part))).reshape(1, width)
+            for v in (sums[0, :head] + sums[0, head:], sums[1, :head])
+        ] + [jnp.zeros((12, width), f32)]
+    extra = jnp.concatenate(extra, axis=0)
+    if y_size > 2:
+        starts = [which[0] + i * (width // 4) for i in range(4)]
+    else:
+        starts = [(a * x_size + b) * pair for a, b in ((1 - y, 1 - x), (y, 1 - x), (1 - y, x), (y, x))]
+    blocks = qkv_grads(
+        starts, (grad_first, grad_last), normed_one, qkv_full, extra, gain_one, (sums_first, sums_last), z_size, spaced
+    )
+    if y_size > 2:
+        qkv_part = plane_scatter(jnp.concatenate(blocks, axis=1), sizes, pair, lanes).astype(bf16)
+    else:
+        far_got = lanes.move(blocks[0], "x", [(0, 1), (1, 0)], None)
+        near_got = lanes.move(after(blocks[1], far_got), "x", [(0, 1), (1, 0)], None)
+        lanes.last["x"] = (near_got,)
+        far_sum = plus(blocks[2], far_got).astype(bf16)
+        qkv_part = plus(blocks[3], near_got, lanes.swap(far_sum, "y")).astype(bf16)
+    output = trade(output, None)
+    grad_first = after(grad_first, blocks[3])
+    cut = grad_first.shape[1]
+
+    def two_terms(index):
+        return dot(half_rows(grad_first, index), qkv_full[:cut], 1, 0) + dot(
+            half_rows(grad_last, index), qkv_full[cut:], 1, 0
+        )
+
+    sent = two_terms(1 - c).astype(bf16)
+    grad_normed_one = two_terms(c) + lanes.swap(sent, "c").astype(f32)
 
     def core_deal(value):
         kept = lane_block(value, c, part)
         sent = lanes.swap(lane_block(value, 1 - c, part), "c")
         return jnp.where(c == 0, jnp.stack([kept, sent]), jnp.stack([sent, kept]))
 
-    wgrads = total.astype(bf16).reshape(3, sub, quad)
+    wgrads = total_last.astype(bf16).reshape(3, sub, quad)
     kept = lane_block(wgrads, x, pair)
     sent = lanes.swap(lane_block(wgrads, 1 - x, pair), "x")
     wgrads = jnp.where(x == 0, jnp.stack([kept, sent], 1), jnp.stack([sent, kept], 1))
@@ -833,40 +957,45 @@
     gate_wgrad, up_wgrad, down_wgrad = (wgrads[i].astype(f32).T for i in range(3))
 
 
-    value = z_scatter([o_part[i * q_rows : (i + 1) * q_rows] for i in range(z_size)], z_size, lanes)
-    o_wgrad = core_deal(value.astype(bf16)).astype(f32).reshape(2 * q_rows, part).T
-
-    gain_one_part = jnp.sum(grad_normed_one * hat_one, axis=0)
     tokens_grad = (grad_mid + norm_back(grad_normed_one * gain_one, hat_one, root_one)).astype(bf16)
-    spaced = [
-        jnp.pad(v.reshape(parts, gain_part), ((0, 0), (0, part - gain_part))).reshape(1, width)
-        for v in (gain_query_part, gain_key_part)
-    ]
-    gain_sums = jnp.concatenate([gain_one_part[None], gain_two_part[None]] + spaced, axis=0)
-    gain_sums = plus(gain_sums, lanes.swap(gain_sums, "c")).astype(bf16)
-    gain_sums = plane_scatter(jnp.pad(gain_sums, ((0, 12), (0, 0))), sizes, pair, lanes).astype(bf16)
+    rows = qkv_rows + 16
+    lanes.last.pop("z", None)
     value = z_scatter(
         [
-            jnp.concatenate([qkv_part[i * qkv_rows : (i + 1) * qkv_rows], gain_sums], axis=0)
+            jnp.concatenate(
+                [qkv_part[i * rows : (i + 1) * rows], o_part[i * q_rows : (i + 1) * q_rows]], axis=0
+            )
             for i in range(z_size)
         ],
         z_size,
         lanes,
     )
-    gain_sums = lane_block(value[qkv_rows:], c, part)
-    qkv_grad = core_deal(value[:qkv_rows].astype(bf16)).astype(f32)
+    value = after(value.astype(bf16), output)
+    kept = lane_block(value, c, part)
+    sent = lanes.swap(lane_block(value, 1 - c, part), "c")
+    gain_sums = plus(kept[qkv_rows:rows], sent[qkv_rows:rows])
+    qkv_grad = jnp.where(c == 0, jnp.stack([kept, sent]), jnp.stack([sent, kept])).astype(f32)
+    o_wgrad = qkv_grad[:, rows:].reshape(2 * q_rows, part).T
+    qkv_grad = qkv_grad[:, :qkv_rows]
     q_wgrad = qkv_grad[:, :q_rows].reshape(-1, part).T
     k_wgrad = qkv_grad[:, q_rows : q_rows + k_rows].reshape(-1, part).T
     v_wgrad = qkv_grad[:, q_rows + k_rows :].reshape(-1, part).T
+    if spaced:
+        gain_query_sum, gain_key_sum = gain_sums[2, :gain_part], gain_sums[3, :gain_part]
+    else:
+        mine = ((y * x_size + x) * c_size + c) * gain_part
+        gain_query_sum, gain_key_sum = (
+            lax.dynamic_slice(gain_sums[2], (mine + at,), (gain_part,)) for at in (0, head)
+        )
     return (
-        trade(output, "more"),
-        trade(tokens_grad, "more"),
+        output,
+        trade(tokens_grad, None),
         gain_sums[0],
         q_wgrad,
         k_wgrad,
         v_wgrad,
-        gain_sums[2, :gain_part],
-        gain_sums[3, :gain_part],
+        gain_query_sum,
+        gain_key_sum,
         o_wgrad,
         gain_sums[1],
         gate_wgrad,

time: 460 us -> 386 us (0.84)
  waiting for transfers between devices: 163 us -> 102 us
  starting transfers between devices: 83.1 us -> 64.3 us
  Pallas kernels: 104 us -> 110 us
  local copies, waits for them, and re-layouts: 29.7 us -> 35 us
    ppermute x60 -> x48, waiting for transfers between devices: 140 us -> 102 us  [move(): got = lax.ppermute(self.wait(value, lane), axes, pairs)]
    ppermute x9 -> x6, waiting for transfers between devices: 22.4 us -> 0.02 us  [around(): lax.ppermute(v, 'z', ring(size, signs * (i + 1)))]
    ppermute x60 -> x48, starting transfers between devices: 74.5 us -> 55.4 us  [move(): got = lax.ppermute(self.wait(value, lane), axes, pairs)]
    unnamed x98 -> x130, local copies, waits for them, and re-layouts: 10.8 us -> 21.8 us
    convert_element_type x15 -> x10, other arithmetic: 11.9 us -> 6.5 us  [the longest x1 2.98 us: shards(): total = plus(after(total, grad_first), slot_grads[2]).astype(bf16)]
    dot_general x8 -> x9, matrix products: 22.1 us -> 18.3 us  [dot(): lax.dot_general(left, right, (((left_dim,), (right_dim,)), ((), ())), pre...]
    pallas_call x1 -> x2, Pallas kernels: 22.7 us -> 26.4 us  [attend_back(): pl.pallas_call(functools.partial(attend_back_kernel, head), grid=(groups,...]
    pallas_call x1 -> x2, Pallas kernels: 10.6 us -> 10.8 us  [attend(): pl.pallas_call(functools.partial(attend_kernel, head), grid=(groups,), in...]
  transfers between devices with their start and end apart: 69 -> 54, of which waited for: 23 -> 19; matrix products, arithmetic and copies ran while one was open for 19% -> 19% of each run, Pallas kernels for 17% -> 23%
where the time goes in v3:
time: 386 us; the launch traced here: 379 us
  Pallas kernels  110 us (28%)
  waiting for transfers between devices  102 us (26%)
  starting transfers between devices  64.3 us (17%)
  other arithmetic  46.4 us (12%)
  local copies, waits for them, and re-layouts  35 us (9%)
  matrix products  18.3 us (5%)
    ppermute x48, waiting for transfers between devices, move(): got = lax.ppermute(self.wait(value, lane), axes, pairs)  102 us
    pallas_call x5, Pallas kernels, call_local(): pl.pallas_call(kernel, in_specs=[pl.BlockSpec(memory_space=pltpu.SMEM)] +...  73.2 us
    ppermute x48, starting transfers between devices, move(): got = lax.ppermute(self.wait(value, lane), axes, pairs)  55.4 us
    pallas_call x2, Pallas kernels, attend_back(): pl.pallas_call(functools.partial(attend_back_kernel, head), grid=(groups,...  26.4 us
    unnamed x130, local copies, waits for them, and re-layouts  21.8 us
    dot_general x9, matrix products, dot(): lax.dot_general(left, right, (((left_dim,), (right_dim,)), ((), ())), pre...  18.3 us
    pallas_call x2, Pallas kernels, attend(): pl.pallas_call(functools.partial(attend_kernel, head), grid=(groups,), in...  10.8 us
    ppermute x6, starting transfers between devices, around(): lax.ppermute(v, 'z', ring(size, signs * (i + 1)))  8.98 us
  transfers between devices with their start and end apart: 54, of which 19 were waited for; matrix products, arithmetic and copies ran while one was open for 19% of the time, Pallas kernels for 23%

profile of v3, /device:TPU:1, one launch (start us, length us, event | category | flops | bytes accessed | tf_op | source)
XLA Modules:
  0.0 379.0 jit_solution(10495103966475464359)
XLA Ops:
  9.9 3.7 collective-permute-start
  17.8 6.1 %collective-permute-start.12 = (bf16[512,1024]{1,0:T(8,128)(2,1)}, bf16[512,1024]{1,0:T(8,128)(2,1)}, u32[]{:S(2)}, u32[]{:S(2)}) collective-permute-start(bf16[512,1024]{1,0:T(8,128)(2,1)} %param.16), channel_id=1, source_target_pairs={{4,1},{1,4},{6,3},{3,6},{12,9},{9,12},{14,11},{11,14},{20,17},{17,... | collective-permute-start | bytes 3145736 | tf_op jit(solution)/shard_map/ppermute | solution.py:603
  24.3 4.2 %collective-permute-done.5 = bf16[3,2,288,128]{3,2,1,0:T(8,128)(2,1)S(1)} collective-permute-done((bf16[3,2,288,128]{3,2,1,0:T(8,128)(2,1)S(1)}, bf16[3,2,288,128]{3,2,1,0:T(8,128)(2,1)S(1)}, u32[]{:S(2)}, u32[]{:S(2)}) %collective-permute-start.5) | collective-permute-done | bytes 442400 | tf_op jit(solution)/shard_map/ppermute | solution.py:603
  45.3 6.6 %collective-permute-done.7.refs_1_ = bf16[1552,256]{1,0:T(8,128)(2,1)S(1)} collective-permute-done((bf16[1552,256]{1,0:T(8,128)(2,1)S(1)}, bf16[1552,256]{1,0:T(8,128)(2,1)S(1)}, u32[]{:S(2)}, u32[]{:S(2)}) %collective-permute-start.7) | collective-permute-done | bytes 794656 | tf_op jit(solution)/shard_map/ppermute | solution.py:603
  58.2 8.1 %collective-permute-done.11.refs_1_ = bf16[864,512]{1,0:T(8,128)(2,1)} collective-permute-done((bf16[864,512]{1,0:T(8,128)(2,1)}, bf16[864,512]{1,0:T(8,128)(2,1)}, u32[]{:S(2)}, u32[]{:S(2)}) %collective-permute-start.11) | collective-permute-done | bytes 884768 | tf_op jit(solution)/shard_map/ppermute | solution.py:603
  79.8 4.5 %fusion.46.qkv_ref = f32[1024,1024]{1,0:T(8,128)} fusion(bf16[1024,1024]{1,0:T(8,128)(2,1)S(1)} %fusion.2.rows, bf16[1024,1024]{1,0:T(8,128)(2,1)S(1)} %get-tuple-element.88.weights), kind=kOutput, calls=%fused_computation.145 | convolution fusion | flops 2147483648 | bytes 8388608 | tf_op jit(solution)/shard_map/dot_general | solution.py:23
  88.0 5.4 %attend.2 = bf16[1024,256]{1,0:T(8,128)(2,1)S(1)} custom-call(f32[1024,1024]{1,0:T(8,128)S(1)} %copy-done, f32[1024,128]{1,0:T(8,128)S(1)} %pad_maximum_fusion.3.cos_ref, f32[1024,128]{1,0:T(8,128)S(1)} %pad_maximum_fusion.4.sin_ref, s32[1024,1]{1,0:T(8,128)S(1)} %copy-done.5, s32[1,1024]{1,0:T(1,128)S(1)} %broadcast_select_fusion.4.seg_row, ...), custom_call_target="tpu_custom_call" | custom-call | flops 6000000 | bytes 100000 | tf_op jit(solution)/shard_map/attend/pallas_call | solution.py:111
  93.4 5.4 %attend.3 = bf16[1024,256]{1,0:T(8,128)(2,1)S(1)} custom-call(f32[1024,1024]{1,0:T(8,128)S(1)} %copy-done, f32[1024,128]{1,0:T(8,128)S(1)} %pad_maximum_fusion.3.cos_ref, f32[1024,128]{1,0:T(8,128)S(1)} %pad_maximum_fusion.4.sin_ref, s32[1024,1]{1,0:T(8,128)S(1)} %copy-done.5, s32[1,1024]{1,0:T(1,128)S(1)} %broadcast_select_fusion.4.seg_row, ...), custom_call_target="tpu_custom_call" | custom-call | flops 6000000 | bytes 100000 | tf_op jit(solution)/shard_map/attend/pallas_call | solution.py:111
  115.0 18.1 %collective-permute-done.19.refs_6_ = bf16[864,512]{1,0:T(8,128)(2,1)} collective-permute-done((bf16[864,512]{1,0:T(8,128)(2,1)}, bf16[864,512]{1,0:T(8,128)(2,1)}, u32[]{:S(2)}, u32[]{:S(2)}) %collective-permute-start.19) | collective-permute-done | bytes 884768 | tf_op jit(solution)/shard_map/ppermute | solution.py:603
  141.4 20.6 %ffn_first.1 = (bf16[1152,2048]{1,0:T(8,128)(2,1)}, bf16[576,2048]{1,0:T(8,128)(2,1)}, bf16[1728,512]{1,0:T(8,128)(2,1)}, bf16[1728,512]{1,0:T(8,128)(2,1)}) custom-call(s32[1]{0:T(128)} %bitcast.36.which_ref, bf16[864,512]{1,0:T(8,128)(2,1)} %pad_maximum_fusion.2.refs_0_, bf16[864,512]{1,0:T(8,128)(2,1)} %collective-permute-done.11.refs_1_, ...), custom_call_target="tpu_custom_call" | custom-call | flops 14495514 | bytes 100000 | tf_op jit(solution)/shard_map/ffn_first/pallas_call | solution.py:241
  162.0 24.4 %ffn_second.1 = (bf16[1152,2048]{1,0:T(8,128)(2,1)}, bf16[576,2048]{1,0:T(8,128)(2,1)}, bf16[512,1024]{1,0:T(8,128)(2,1)}, bf16[512,1024]{1,0:T(8,128)(2,1)}, bf...) custom-call(s32[1]{0:T(128)} %bitcast.36.which_ref, bf16[864,512]{1,0:T(8,128)(2,1)} %pad_maximum_fusion.2.refs_0_, ...), custom_call_target="tpu_custom_call" | custom-call | flops 18119392 | bytes 100000 | tf_op jit(solution)/shard_map/ffn_second/pallas_call | solution.py:241
  194.5 18.7 %ffn_third.1 = (bf16[864,512]{1,0:T(8,128)(2,1)}, bf16[864,512]{1,0:T(8,128)(2,1)}, bf16[864,512]{1,0:T(8,128)(2,1)}, bf16[864,512]{1,0:T(8,128)(2,1)}, bf16[512...) custom-call(s32[1]{0:T(128)} %bitcast.36.which_ref, ...), custom_call_target="tpu_custom_call" | custom-call | flops 10871635 | bytes 100000 | tf_op jit(solution)/shard_map/ffn_third/pallas_call | solution.py:241
  225.5 7.5 %collective-permute-done.33 = bf16[1728,512]{1,0:T(8,128)(2,1)} collective-permute-done((bf16[1728,512]{1,0:T(8,128)(2,1)}, bf16[1728,512]{1,0:T(8,128)(2,1)}, u32[]{:S(2)}, u32[]{:S(2)}) %collective-permute-start.33) | collective-permute-done | bytes 1769504 | tf_op jit(solution)/shard_map/ppermute | solution.py:603
  241.5 13.2 %attend_back.2 = (bf16[1024,512]{1,0:T(8,128)(2,1)}, f32[16,128]{1,0:T(8,128)}) custom-call(f32[1024,1024]{1,0:T(8,128)} %fusion.46.qkv_ref, f32[1024,128]{1,0:T(8,128)} %copy-done.3, f32[1024,128]{1,0:T(8,128)} %copy-done.4, s32[1024,1]{1,0:T(8,128)} %copy.84.seg_col, s32[1,1024]{1,0:T(1,128)} %copy-done.16, f32[8,128]{1,0:T(8,128)} %copy-done.17, ...), custom_call_target="tpu_custom_call" | custom-call | flops 12000000 | bytes 100000 | tf_op jit(solution)/shard_map/attend_back/pallas_call | solution.py:195
  261.4 3.9 %collective-permute-done.37 = bf16[512,256]{1,0:T(8,128)(2,1)S(1)} collective-permute-done((bf16[512,256]{1,0:T(8,128)(2,1)S(1)}, bf16[512,256]{1,0:T(8,128)(2,1)S(1)}, u32[]{:S(2)}, u32[]{:S(2)}) %collective-permute-start.37) | collective-permute-done | bytes 262176 | tf_op jit(solution)/shard_map/ppermute | solution.py:603
  268.1 6.6 %collective-permute-start.27 = (bf16[512,1024]{1,0:T(8,128)(2,1)}, bf16[512,1024]{1,0:T(8,128)(2,1)}, u32[]{:S(2)}, u32[]{:S(2)}) collective-permute-start(bf16[512,1024]{1,0:T(8,128)(2,1)} %get-tuple-element.110), channel_id=1, source_target_pairs={{0,4},{4,0},{1,5},{5,1},{2,6},{6,2},{3,7},{7,3},{8,12},{12,8},{9,1... | collective-permute-start | bytes 3145736 | tf_op jit(solution)/shard_map/ppermute | solution.py:603
  274.6 13.2 %attend_back.3 = (bf16[1024,512]{1,0:T(8,128)(2,1)}, f32[16,128]{1,0:T(8,128)}) custom-call(f32[1024,1024]{1,0:T(8,128)} %fusion.46.qkv_ref, f32[1024,128]{1,0:T(8,128)} %copy-done.3, f32[1024,128]{1,0:T(8,128)} %copy-done.4, s32[1024,1]{1,0:T(8,128)} %copy.84.seg_col, s32[1,1024]{1,0:T(1,128)} %copy-done.16, f32[8,128]{1,0:T(8,128)} %copy-done.17, ...), custom_call_target="tpu_custom_call" | custom-call | flops 12000000 | bytes 100000 | tf_op jit(solution)/shard_map/attend_back/pallas_call | solution.py:195
  292.9 8.2 %qkv_grads.1 = (bf16[1088,256]{1,0:T(8,128)(2,1)}, bf16[1088,256]{1,0:T(8,128)(2,1)}, bf16[1088,256]{1,0:T(8,128)(2,1)}, bf16[1088,256]{1,0:T(8,128)(2,1)}) custom-call(s32[4]{0:T(128)} %pad_add_fusion.1.starts_ref, bf16[1024,512]{1,0:T(8,128)(2,1)} %get-tuple-element.142.grads_0, bf16[1024,512]{1,0:T(8,128)(2,1)} %get-tuple-element.138.grads_1, ...), custom_call_target="tpu_custom_call" | custom-call | flops 1000000 | bytes 100000 | tf_op jit(solution)/shard_map/qkv_grads/pallas_call | solution.py:241
  303.8 11.5 %collective-permute-done.44 = bf16[1088,256]{1,0:T(8,128)(2,1)S(1)} collective-permute-done((bf16[1088,256]{1,0:T(8,128)(2,1)}, bf16[1088,256]{1,0:T(8,128)(2,1)S(1)}, u32[]{:S(2)}, u32[]{:S(2)}) %collective-permute-start.44) | collective-permute-done | bytes 557088 | tf_op jit(solution)/shard_map/ppermute | solution.py:603
  315.8 8.0 %collective-permute-done.51 = bf16[864,512]{1,0:T(8,128)(2,1)S(1)} collective-permute-done((bf16[864,512]{1,0:T(8,128)(2,1)S(1)}, bf16[864,512]{1,0:T(8,128)(2,1)S(1)}, u32[]{:S(2)}, u32[]{:S(2)}) %collective-permute-start.51) | collective-permute-done | bytes 884768 | tf_op jit(solution)/shard_map/ppermute | solution.py:603
  332.3 5.3 %collective-permute-done.52 = bf16[3,288,256]{2,1,0:T(8,128)(2,1)S(1)} collective-permute-done((bf16[3,288,256]{2,1,0:T(8,128)(2,1)S(1)}, bf16[3,288,256]{2,1,0:T(8,128)(2,1)S(1)}, u32[]{:S(2)}, u32[]{:S(2)}) %collective-permute-start.52) | collective-permute-done | bytes 442400 | tf_op jit(solution)/shard_map/ppermute | solution.py:603
  346.6 3.6 collective-permute-start.43
  355.5 5.3 %collective-permute-done.34 = bf16[512,1024]{1,0:T(8,128)(2,1)} collective-permute-done((bf16[512,1024]{1,0:T(8,128)(2,1)S(1)}, bf16[512,1024]{1,0:T(8,128)(2,1)}, u32[]{:S(2)}, u32[]{:S(2)}) %collective-permute-start.34) | collective-permute-done | bytes 1048608 | tf_op jit(solution)/shard_map/ppermute | solution.py:603
  363.2 8.8 %collective-permute-done.43 = bf16[512,1024]{1,0:T(8,128)(2,1)} collective-permute-done((bf16[512,1024]{1,0:T(8,128)(2,1)S(1)}, bf16[512,1024]{1,0:T(8,128)(2,1)}, u32[]{:S(2)}, u32[]{:S(2)}) %collective-permute-start.43) | collective-permute-done | bytes 1048608 | tf_op jit(solution)/shard_map/ppermute | solution.py:603
  (335 shorter events, 155.7 us)
Async XLA Ops:
  9.9 28.4 %collective-permute-start = (bf16[512,1024]{1,0:T(8,128)(2,1)}, bf16[512,1024]{1,0:T(8,128)(2,1)}, u32[]{:S(2)}, u32[]{:S(2)}) collective-permute-start(bf16[512,1024]{1,0:T(8,128)(2,1)} %param.14), channel_id=1, source_target_pairs={{4,1},{1,4},{6,3},{3,6},{12,9},{9,12},{14,11},{11,14},{20,17},{17,... | collective-permute-start | bytes 3145736 | tf_op jit(solution)/shard_map/ppermute | solution.py:603
  17.8 37.7 %collective-permute-start.12 = (bf16[512,1024]{1,0:T(8,128)(2,1)}, bf16[512,1024]{1,0:T(8,128)(2,1)}, u32[]{:S(2)}, u32[]{:S(2)}) collective-permute-start(bf16[512,1024]{1,0:T(8,128)(2,1)} %param.16), channel_id=1, source_target_pairs={{4,1},{1,4},{6,3},{3,6},{12,9},{9,12},{14,11},{11,14},{20,17},{17,... | collective-permute-start | bytes 3145736 | tf_op jit(solution)/shard_map/ppermute | solution.py:603
  41.0 25.6 %collective-permute-start.1 = (bf16[512,1024]{1,0:T(8,128)(2,1)}, bf16[512,1024]{1,0:T(8,128)(2,1)}, u32[]{:S(2)}, u32[]{:S(2)}) collective-permute-start(bf16[512,1024]{1,0:T(8,128)(2,1)} %get-tuple-element.193), channel_id=1, source_target_pairs={{0,4},{4,0},{1,5},{5,1},{2,6},{6,2},{3,7},{7,3},{8,12},{12,8},{9,1... | collective-permute-start | bytes 3145736 | tf_op jit(solution)/shard_map/ppermute | solution.py:603
  42.9 23.4 %collective-permute-start.11 = (bf16[864,512]{1,0:T(8,128)(2,1)}, bf16[864,512]{1,0:T(8,128)(2,1)}, u32[]{:S(2)}, u32[]{:S(2)}) collective-permute-start(bf16[864,512]{1,0:T(8,128)(2,1)} %pad_maximum_fusion.2.refs_0_), channel_id=1, source_target_pairs={{0,1},{1,2},{2,3},{3,0},{4,5},{5,6},{6,7},{7,4},{8,9},{9,10},{10,1... | collective-permute-start | bytes 2654216 | tf_op jit(solution)/shard_map/ppermute | solution.py:603
  66.3 27.1 %collective-permute-start.13 = (bf16[864,512]{1,0:T(8,128)(2,1)}, bf16[864,512]{1,0:T(8,128)(2,1)}, u32[]{:S(2)}, u32[]{:S(2)}) collective-permute-start(bf16[864,512]{1,0:T(8,128)(2,1)} %collective-permute-done.11.refs_1_), channel_id=1, source_target_pairs={{0,1},{1,2},{2,3},{3,0},{4,5},{5,6},{6,7},{7,4},{8,9},{9,10},{10,1... | collective-permute-start | bytes 2654216 | tf_op jit(solution)/shard_map/ppermute | solution.py:603
  71.5 27.5 %collective-permute-start.15 = (bf16[512,1024]{1,0:T(8,128)(2,1)}, bf16[512,1024]{1,0:T(8,128)(2,1)}, u32[]{:S(2)}, u32[]{:S(2)}) collective-permute-start(bf16[512,1024]{1,0:T(8,128)(2,1)} %broadcast_select_fusion.2.refs_8_.refs_12_), channel_id=1, source_target_pairs={{0,8},{8,0},{1,9},{9,1},{2,10},{10,2},{3,11},{11,3},{4,12},{12,4},... | collective-permute-start | bytes 3145736 | tf_op jit(solution)/shard_map/ppermute | solution.py:603
  111.9 24.5 %collective-permute-start.22 = (bf16[512,1024]{1,0:T(8,128)(2,1)S(1)}, bf16[512,1024]{1,0:T(8,128)(2,1)S(1)}, u32[]{:S(2)}, u32[]{:S(2)}) collective-permute-start(bf16[512,1024]{1,0:T(8,128)(2,1)S(1)} %multiply_convert_fusion.refs_4_.refs_8_), channel_id=1, source_target_pairs={{0,8},{8,0},{1,9},{9,1},{2,10},{10,2},{3,11},{11,3},{4,12},{12,4},... | collective-permute-start | bytes 3145736 | tf_op jit(solution)/shard_map/ppermute | solution.py:603
  113.5 24.1 %collective-permute-start.18 = (bf16[864,512]{1,0:T(8,128)(2,1)}, bf16[864,512]{1,0:T(8,128)(2,1)}, u32[]{:S(2)}, u32[]{:S(2)}) collective-permute-start(bf16[864,512]{1,0:T(8,128)(2,1)} %collective-permute-done.13.refs_2_), channel_id=1, source_target_pairs={{0,1},{1,2},{2,3},{3,0},{4,5},{5,6},{6,7},{7,4},{8,9},{9,10},{10,1... | collective-permute-start | bytes 2654216 | tf_op jit(solution)/shard_map/ppermute | solution.py:603
  113.9 24.9 %collective-permute-start.24 = (bf16[512,1024]{1,0:T(8,128)(2,1)}, bf16[512,1024]{1,0:T(8,128)(2,1)S(1)}, u32[]{:S(2)}, u32[]{:S(2)}) collective-permute-start(bf16[512,1024]{1,0:T(8,128)(2,1)} %broadcast_select_fusion.2.refs_8_.refs_12_), channel_id=1, source_target_pairs={{0,4},{4,0},{1,5},{5,1},{2,6},{6,2},{3,7},{7,3},{8,12},{12,8},{9,1... | collective-permute-start | bytes 3145736 | tf_op jit(solution)/shard_map/ppermute | solution.py:603
  114.9 23.9 %collective-permute-start.25 = (bf16[512,1024]{1,0:T(8,128)(2,1)}, bf16[512,1024]{1,0:T(8,128)(2,1)S(1)}, u32[]{:S(2)}, u32[]{:S(2)}) collective-permute-start(bf16[512,1024]{1,0:T(8,128)(2,1)} %collective-permute-done.15.refs_10_.refs_14_), channel_id=1, source_target_pairs={{0,4},{4,0},{1,5},{5,1},{2,6},{6,2},{3,7},{7,3},{8,12},{12,8},{9,1... | collective-permute-start | bytes 3145736 | tf_op jit(solution)/shard_map/ppermute | solution.py:603
  137.6 24.4 %collective-permute-start.20 = (bf16[864,512]{1,0:T(8,128)(2,1)}, bf16[864,512]{1,0:T(8,128)(2,1)}, u32[]{:S(2)}, u32[]{:S(2)}) collective-permute-start(bf16[864,512]{1,0:T(8,128)(2,1)} %collective-permute-done.18.refs_3_), channel_id=1, source_target_pairs={{0,16},{16,0},{1,17},{17,1},{2,18},{18,2},{3,19},{19,3},{4,20},{20... | collective-permute-start | bytes 2654216 | tf_op jit(solution)/shard_map/ppermute | solution.py:603
  186.8 27.5 %collective-permute-start.29 = (bf16[512,1024]{1,0:T(8,128)(2,1)}, bf16[512,1024]{1,0:T(8,128)(2,1)}, u32[]{:S(2)}, u32[]{:S(2)}) collective-permute-start(bf16[512,1024]{1,0:T(8,128)(2,1)} %get-tuple-element.114), channel_id=1, source_target_pairs={{0,4},{4,0},{1,5},{5,1},{2,6},{6,2},{3,7},{7,3},{8,12},{12,8},{9,1... | collective-permute-start | bytes 3145736 | tf_op jit(solution)/shard_map/ppermute | solution.py:603
  191.9 24.7 %collective-permute-start.30 = (bf16[512,1024]{1,0:T(8,128)(2,1)}, bf16[512,1024]{1,0:T(8,128)(2,1)}, u32[]{:S(2)}, u32[]{:S(2)}) collective-permute-start(bf16[512,1024]{1,0:T(8,128)(2,1)} %add_convert_fusion.3), channel_id=1, source_target_pairs={{0,8},{8,0},{1,9},{9,1},{2,10},{10,2},{3,11},{11,3},{4,12},{12,4},... | collective-permute-start | bytes 3145736 | tf_op jit(solution)/shard_map/ppermute | solution.py:603
  193.2 39.8 %collective-permute-start.33 = (bf16[1728,512]{1,0:T(8,128)(2,1)}, bf16[1728,512]{1,0:T(8,128)(2,1)}, u32[]{:S(2)}, u32[]{:S(2)}) collective-permute-start(bf16[1728,512]{1,0:T(8,128)(2,1)} %get-tuple-element.121), channel_id=1, source_target_pairs={{0,16},{16,0},{1,17},{17,1},{2,18},{18,2},{3,19},{19,3},{4,20},{20... | collective-permute-start | bytes 5308424 | tf_op jit(solution)/shard_map/ppermute | solution.py:603
  213.3 22.9 %collective-permute-start.28 = (bf16[512,1024]{1,0:T(8,128)(2,1)}, bf16[512,1024]{1,0:T(8,128)(2,1)S(1)}, u32[]{:S(2)}, u32[]{:S(2)}) collective-permute-start(bf16[512,1024]{1,0:T(8,128)(2,1)} %get-tuple-element.112), channel_id=1, source_target_pairs={{0,4},{4,0},{1,5},{5,1},{2,6},{6,2},{3,7},{7,3},{8,12},{12,8},{9,1... | collective-permute-start | bytes 3145736 | tf_op jit(solution)/shard_map/ppermute | solution.py:603
  224.0 34.2 %collective-permute-start.36 = (bf16[864,512]{1,0:T(8,128)(2,1)}, bf16[864,512]{1,0:T(8,128)(2,1)}, u32[]{:S(2)}, u32[]{:S(2)}) collective-permute-start(bf16[864,512]{1,0:T(8,128)(2,1)} %get-tuple-element.128), channel_id=1, source_target_pairs={{0,16},{16,0},{1,17},{17,1},{2,18},{18,2},{3,19},{19,3},{4,20},{20... | collective-permute-start | bytes 2654216 | tf_op jit(solution)/shard_map/ppermute | solution.py:603
  225.1 62.9 %collective-permute-start.40 = (bf16[864,512]{1,0:T(8,128)(2,1)}, bf16[864,512]{1,0:T(8,128)(2,1)}, u32[]{:S(2)}, u32[]{:S(2)}) collective-permute-start(bf16[864,512]{1,0:T(8,128)(2,1)} %get-tuple-element.133), channel_id=1, source_target_pairs={{0,16},{16,0},{1,17},{17,1},{2,18},{18,2},{3,19},{19,3},{4,20},{20... | collective-permute-start | bytes 2654216 | tf_op jit(solution)/shard_map/ppermute | solution.py:603
  237.5 30.5 %collective-permute-start.31 = (bf16[512,1024]{1,0:T(8,128)(2,1)S(1)}, bf16[512,1024]{1,0:T(8,128)(2,1)S(1)}, u32[]{:S(2)}, u32[]{:S(2)}) collective-permute-start(bf16[512,1024]{1,0:T(8,128)(2,1)S(1)} %add_convert_fusion.2), channel_id=1, source_target_pairs={{0,8},{8,0},{1,9},{9,1},{2,10},{10,2},{3,11},{11,3},{4,12},{12,4},... | collective-permute-start | bytes 3145736 | tf_op jit(solution)/shard_map/ppermute | solution.py:603
  257.0 30.8 %collective-permute-start.38 = (bf16[512,256]{1,0:T(8,128)(2,1)S(1)}, bf16[512,256]{1,0:T(8,128)(2,1)S(1)}, u32[]{:S(2)}, u32[]{:S(2)}) collective-permute-start(bf16[512,256]{1,0:T(8,128)(2,1)S(1)} %get-tuple-element.196), channel_id=1, source_target_pairs={{0,8},{8,0},{1,9},{9,1},{2,10},{10,2},{3,11},{11,3},{4,12},{12,4},... | collective-permute-start | bytes 786440 | tf_op jit(solution)/shard_map/ppermute | solution.py:603
  261.2 27.4 %collective-permute-start.41 = (bf16[864,512]{1,0:T(8,128)(2,1)}, bf16[864,512]{1,0:T(8,128)(2,1)}, u32[]{:S(2)}, u32[]{:S(2)}) collective-permute-start(bf16[864,512]{1,0:T(8,128)(2,1)} %add_convert_fusion.5), channel_id=1, source_target_pairs={{0,1},{1,2},{2,3},{3,0},{4,5},{5,6},{6,7},{7,4},{8,9},{9,10},{10,1... | collective-permute-start | bytes 2654216 | tf_op jit(solution)/shard_map/ppermute | solution.py:603
  268.1 73.2 %collective-permute-start.27 = (bf16[512,1024]{1,0:T(8,128)(2,1)}, bf16[512,1024]{1,0:T(8,128)(2,1)}, u32[]{:S(2)}, u32[]{:S(2)}) collective-permute-start(bf16[512,1024]{1,0:T(8,128)(2,1)} %get-tuple-element.110), channel_id=1, source_target_pairs={{0,4},{4,0},{1,5},{5,1},{2,6},{6,2},{3,7},{7,3},{8,12},{12,8},{9,1... | collective-permute-start | bytes 3145736 | tf_op jit(solution)/shard_map/ppermute | solution.py:603
  301.3 22.6 %collective-permute-start.51 = (bf16[864,512]{1,0:T(8,128)(2,1)S(1)}, bf16[864,512]{1,0:T(8,128)(2,1)S(1)}, u32[]{:S(2)}, u32[]{:S(2)}) collective-permute-start(bf16[864,512]{1,0:T(8,128)(2,1)S(1)} %add_convert_fusion.4), channel_id=1, source_target_pairs={{0,1},{1,2},{2,3},{3,0},{4,5},{5,6},{6,7},{7,4},{8,9},{9,10},{10,1... | collective-permute-start | bytes 2654216 | tf_op jit(solution)/shard_map/ppermute | solution.py:603
  302.4 21.9 %collective-permute-start.42 = (bf16[512,1024]{1,0:T(8,128)(2,1)S(1)}, bf16[512,1024]{1,0:T(8,128)(2,1)S(1)}, u32[]{:S(2)}, u32[]{:S(2)}) collective-permute-start(bf16[512,1024]{1,0:T(8,128)(2,1)S(1)} %add_convert_fusion), channel_id=1, source_target_pairs={{0,4},{4,0},{1,5},{5,1},{2,6},{6,2},{3,7},{7,3},{8,12},{12,8},{9,1... | collective-permute-start | bytes 3145736 | tf_op jit(solution)/shard_map/ppermute | solution.py:603
  346.6 25.5 %collective-permute-start.43 = (bf16[512,1024]{1,0:T(8,128)(2,1)S(1)}, bf16[512,1024]{1,0:T(8,128)(2,1)}, u32[]{:S(2)}, u32[]{:S(2)}) collective-permute-start(bf16[512,1024]{1,0:T(8,128)(2,1)S(1)} %get-tuple-element.194), channel_id=1, source_target_pairs={{4,1},{1,4},{6,3},{3,6},{12,9},{9,12},{14,11},{11,14},{20,17},{17,... | collective-permute-start | bytes 3145736 | tf_op jit(solution)/shard_map/ppermute | solution.py:603
  (91 other events, 1162.1 us)

commit v4 on v3

--- a/solution.py
+++ b/solution.py
@@ -79,7 +79,7 @@
     length = qkv_ref.shape[0]
     lanes = 2 * head
     ones = ones_by_head(lanes, head)
-    queries, keys, values = split_block(qkv_ref[...], head)
+    queries, keys, values = split_block(qkv_ref[...].astype(f32), head)
     cosine, sine = cos_ref[...], sin_ref[...]
 
     def rotated(raw, gain):
@@ -135,7 +135,7 @@
     length = qkv_ref.shape[0]
     lanes = 2 * head
     ones = ones_by_head(lanes, head)
-    queries, keys, values = split_block(qkv_ref[...], head)
+    queries, keys, values = split_block(qkv_ref[...].astype(f32), head)
     cosine, sine = cos_ref[...], sin_ref[...]
 
     def rotated(raw, gain):
@@ -804,7 +804,7 @@
     all_root = lax.rsqrt(jnp.mean(all_tokens * all_tokens, axis=-1, keepdims=True) + epsilon)
     normed_one = (all_tokens * all_root * gain_one).astype(bf16)
     normed_one = after(normed_one, pieces[1])
-    qkv = dot(normed_one, qkv_full, 1, 1)
+    qkv = dot(normed_one, qkv_full, 1, 1).astype(bf16)
     qkv = after(qkv, cotangent)
     tables = (cosine, sine, seg_col, seg_row, head_gains, head)
     context = attend(qkv, *tables, 0, z_size // 2)
@@ -877,6 +877,11 @@
     o_grad = dot(after(context, grad_context), branch, 0, 0).astype(bf16)
     grad_context = after(grad_context, o_grad, ring_first)
     grad_first, sums_first = attend_back(qkv, *tables[:-1], grad_context, head, 0, z_size // 2)
+    out_third = plus(out_third, lanes.swap(out_fourth, "c")).astype(bf16)
+    out_third = after(out_third, grad_normed_two)
+    out_across = lanes.move(out_third, "x", [(0, 1), (1, 0)], None)
+    output = mid + plus(out_first, lanes.swap(out_second, "c"), after(out_across, grad_first))
+    output = output.astype(bf16)
     if y_size > 2:
         o_part = plane_scatter(o_grad, sizes, pair, lanes).astype(bf16)
         o_far = o_part
@@ -884,7 +889,7 @@
         block = lambda a, b: lane_block(o_grad, a * x_size + b, pair)
         o_far = lanes.move(block(1 - y, 1 - x), "x", [(0, 1), (1, 0)], None)
         o_near = lanes.move(block(y, 1 - x), "x", [(0, 1), (1, 0)], None)
-        o_far = plus(block(1 - y, x), after(o_far, grad_first)).astype(bf16)
+        o_far = plus(block(1 - y, x), after(o_far, grad_first, output)).astype(bf16)
         o_part = plus(block(y, x), o_near)
     total = plus(after(total, grad_first), slot_grads[2]).astype(bf16)
     grad_last, sums_last = attend_back(
@@ -894,11 +899,7 @@
         o_far = lanes.move(o_far, "y", [(0, 1), (1, 0)], None)
         o_part = plus(o_part, after(o_far, grad_last)).astype(bf16)
     total = lanes.move(total, "z", ring(z_size), "z")
-    out_third = plus(out_third, lanes.swap(out_fourth, "c")).astype(bf16)
-    out_third = after(out_third, grad_normed_two)
-    out_across = lanes.move(out_third, "x", [(0, 1), (1, 0)], None)
-    output = mid + plus(out_first, lanes.swap(out_second, "c"), after(out_across, grad_first))
-    output = output.astype(bf16)
+    output_got = lanes.move(after(output, total), ("c", "z"), pairs, None)
     grad_last = after(grad_last, o_part, arrived[-1])
     for step in range(2, z_size - 1):
         total = plus(after(total, grad_last), slot_grads[step + 1]).astype(bf16)
@@ -921,15 +922,8 @@
     blocks = qkv_grads(
         starts, (grad_first, grad_last), normed_one, qkv_full, extra, gain_one, (sums_first, sums_last), z_size, spaced
     )
-    if y_size > 2:
-        qkv_part = plane_scatter(jnp.concatenate(blocks, axis=1), sizes, pair, lanes).astype(bf16)
-    else:
+    if y_size == 2:
         far_got = lanes.move(blocks[0], "x", [(0, 1), (1, 0)], None)
-        near_got = lanes.move(after(blocks[1], far_got), "x", [(0, 1), (1, 0)], None)
-        lanes.last["x"] = (near_got,)
-        far_sum = plus(blocks[2], far_got).astype(bf16)
-        qkv_part = plus(blocks[3], near_got, lanes.swap(far_sum, "y")).astype(bf16)
-    output = trade(output, None)
     grad_first = after(grad_first, blocks[3])
     cut = grad_first.shape[1]
 
@@ -940,6 +934,16 @@
 
     sent = two_terms(1 - c).astype(bf16)
     grad_normed_one = two_terms(c) + lanes.swap(sent, "c").astype(f32)
+    tokens_grad = (grad_mid + norm_back(grad_normed_one * gain_one, hat_one, root_one)).astype(bf16)
+    tokens_got = lanes.move(tokens_grad, ("c", "z"), pairs, None)
+    if y_size > 2:
+        qkv_part = plane_scatter(jnp.concatenate(blocks, axis=1), sizes, pair, lanes).astype(bf16)
+    else:
+        near_got = lanes.move(after(blocks[1], far_got), "x", [(0, 1), (1, 0)], None)
+        lanes.last["x"] = (near_got,)
+        far_sum = plus(blocks[2], far_got).astype(bf16)
+        y_got = after(lanes.swap(far_sum, "y"), output_got, tokens_grad)
+        qkv_part = plus(blocks[3], near_got, y_got).astype(bf16)
 
     def core_deal(value):
         kept = lane_block(value, c, part)
@@ -949,15 +953,15 @@
     wgrads = total_last.astype(bf16).reshape(3, sub, quad)
     kept = lane_block(wgrads, x, pair)
     sent = lanes.swap(lane_block(wgrads, 1 - x, pair), "x")
+    dealt = sent
     wgrads = jnp.where(x == 0, jnp.stack([kept, sent], 1), jnp.stack([sent, kept], 1))
     kept = lane_block(wgrads, c, part)
     sent = lanes.swap(lane_block(wgrads, 1 - c, part), "c")
     wgrads = jnp.where(c == 0, jnp.stack([kept, sent], 2), jnp.stack([sent, kept], 2))
     wgrads = wgrads.reshape(3, x_size * c_size * sub, part)
-    gate_wgrad, up_wgrad, down_wgrad = (wgrads[i].astype(f32).T for i in range(3))
-
-
-    tokens_grad = (grad_mid + norm_back(grad_normed_one * gain_one, hat_one, root_one)).astype(bf16)
+    last_grads = wgrads
+
+
     rows = qkv_rows + 16
     lanes.last.pop("z", None)
     value = z_scatter(
@@ -970,13 +974,15 @@
         z_size,
         lanes,
     )
-    value = after(value.astype(bf16), output)
+    value = after(value.astype(bf16), dealt)
     kept = lane_block(value, c, part)
     sent = lanes.swap(lane_block(value, 1 - c, part), "c")
     gain_sums = plus(kept[qkv_rows:rows], sent[qkv_rows:rows])
     qkv_grad = jnp.where(c == 0, jnp.stack([kept, sent]), jnp.stack([sent, kept])).astype(f32)
     o_wgrad = qkv_grad[:, rows:].reshape(2 * q_rows, part).T
     qkv_grad = qkv_grad[:, :qkv_rows]
+    last_grads = after(last_grads, sent)
+    gate_wgrad, up_wgrad, down_wgrad = (last_grads[i].astype(f32).T for i in range(3))
     q_wgrad = qkv_grad[:, :q_rows].reshape(-1, part).T
     k_wgrad = qkv_grad[:, q_rows : q_rows + k_rows].reshape(-1, part).T
     v_wgrad = qkv_grad[:, q_rows + k_rows :].reshape(-1, part).T
@@ -988,8 +994,8 @@
             lax.dynamic_slice(gain_sums[2], (mine + at,), (gain_part,)) for at in (0, head)
         )
     return (
-        output,
-        trade(tokens_grad, None),
+        jnp.where(trades, output_got, output),
+        jnp.where(trades, tokens_got, tokens_grad),
         gain_sums[0],
         q_wgrad,
         k_wgrad,

time: 386 us -> 375 us (0.972)
  waiting for transfers between devices: 102 us -> 90.8 us
  local copies, waits for them, and re-layouts: 35 us -> 29.4 us
    ppermute x48, waiting for transfers between devices: 102 us -> 68.6 us  [move(): got = lax.ppermute(self.wait(value, lane), axes, pairs)]
    ppermute x6, waiting for transfers between devices: 0.02 us -> 22.2 us  [around(): lax.ppermute(v, 'z', ring(size, signs * (i + 1)))]
    unnamed x130 -> x122, local copies, waits for them, and re-layouts: 21.8 us -> 17.1 us
    select_n x3 -> x1, other arithmetic: 7.04 us -> 2.32 us  [trade(): return jnp.where(trades, lanes.move(value, ('c', 'z'), pairs, lane), value)]
  transfers between devices with their start and end apart: 54 -> 54, of which waited for: 19 -> 20; matrix products, arithmetic and copies ran while one was open for 19% -> 20% of each run, Pallas kernels for 23% -> 23%
where the time goes in v4:
time: 375 us; the launch traced here: 368 us
  Pallas kernels  111 us (30%)
  waiting for transfers between devices  90.8 us (24%)
  starting transfers between devices  67 us (18%)
  other arithmetic  49.6 us (13%)
  local copies, waits for them, and re-layouts  29.4 us (8%)
  matrix products  18 us (5%)
    pallas_call x5, Pallas kernels, call_local(): pl.pallas_call(kernel, in_specs=[pl.BlockSpec(memory_space=pltpu.SMEM)] +...  73.2 us
    ppermute x48, waiting for transfers between devices, move(): got = lax.ppermute(self.wait(value, lane), axes, pairs)  68.6 us
    ppermute x48, starting transfers between devices, move(): got = lax.ppermute(self.wait(value, lane), axes, pairs)  57.3 us
    pallas_call x2, Pallas kernels, attend_back(): pl.pallas_call(functools.partial(attend_back_kernel, head), grid=(groups,...  26.2 us
    ppermute x6, waiting for transfers between devices, around(): lax.ppermute(v, 'z', ring(size, signs * (i + 1)))  22.2 us
    dot_general x9, matrix products, dot(): lax.dot_general(left, right, (((left_dim,), (right_dim,)), ((), ())), pre...  18 us
    unnamed x122, local copies, waits for them, and re-layouts  17.1 us
    pallas_call x2, Pallas kernels, attend(): pl.pallas_call(functools.partial(attend_kernel, head), grid=(groups,), in...  11.1 us
  transfers between devices with their start and end apart: 54, of which 20 were waited for; matrix products, arithmetic and copies ran while one was open for 20% of the time, Pallas kernels for 23%

profile of v4, /device:TPU:1, one launch (start us, length us, event | category | flops | bytes accessed | tf_op | source)
XLA Modules:
  0.0 367.6 jit_solution(2896489660210688244)
XLA Ops:
  4.4 4.2 %collective-permute-start.4 = (bf16[768,128]{1,0:T(8,128)(2,1)S(1)}, bf16[768,128]{1,0:T(8,128)(2,1)S(1)}, u32[]{:S(2)}, u32[]{:S(2)}) collective-permute-start(bf16[768,128]{1,0:T(8,128)(2,1)S(1)} %bitcast.112), channel_id=1, source_target_pairs={{0,3},{1,0},{2,1},{3,2},{4,7},{5,4},{6,5},{7,6},{8,11},{9,8},{10,9... | collective-permute-start | bytes 589832 | tf_op jit(solution)/shard_map/ppermute | solution.py:613
  13.1 5.8 %collective-permute-start = (bf16[512,1024]{1,0:T(8,128)(2,1)}, bf16[512,1024]{1,0:T(8,128)(2,1)}, u32[]{:S(2)}, u32[]{:S(2)}) collective-permute-start(bf16[512,1024]{1,0:T(8,128)(2,1)} %param.14), channel_id=1, source_target_pairs={{4,1},{1,4},{6,3},{3,6},{12,9},{9,12},{14,11},{11,14},{20,17},{17,... | collective-permute-start | bytes 3145736 | tf_op jit(solution)/shard_map/ppermute | solution.py:603
  21.0 3.9 %collective-permute-done.3 = bf16[768,128]{1,0:T(8,128)(2,1)S(1)} collective-permute-done((bf16[768,128]{1,0:T(8,128)(2,1)S(1)}, bf16[768,128]{1,0:T(8,128)(2,1)S(1)}, u32[]{:S(2)}, u32[]{:S(2)}) %collective-permute-start.3) | collective-permute-done | bytes 196640 | tf_op jit(solution)/shard_map/ppermute | solution.py:613
  43.6 5.1 %collective-permute-done.8.refs_2_ = bf16[1552,256]{1,0:T(8,128)(2,1)S(1)} collective-permute-done((bf16[1552,256]{1,0:T(8,128)(2,1)S(1)}, bf16[1552,256]{1,0:T(8,128)(2,1)S(1)}, u32[]{:S(2)}, u32[]{:S(2)}) %collective-permute-start.8) | collective-permute-done | bytes 794656 | tf_op jit(solution)/shard_map/ppermute | solution.py:603
  53.2 14.2 %collective-permute-done.12 = bf16[512,1024]{1,0:T(8,128)(2,1)} collective-permute-done((bf16[512,1024]{1,0:T(8,128)(2,1)}, bf16[512,1024]{1,0:T(8,128)(2,1)}, u32[]{:S(2)}, u32[]{:S(2)}) %collective-permute-start.12) | collective-permute-done | bytes 1048608 | tf_op jit(solution)/shard_map/ppermute | solution.py:603
  79.9 4.3 %fusion.2.rows = bf16[1024,1024]{1,0:T(8,128)(2,1)} fusion(f32[1024]{0:T(1024)S(1)} %bitcast.133, f32[1024]{0:T(1024)S(1)} %add_rsqrt_fusion, bf16[512,1024]{1,0:T(8,128)(2,1)} %get-tuple-element.199, bf16[512,1024]{1,0:T(8,128)(2,1)} %collective-permute-done.1, pred[]{:T(512)S(6)} %eq.12), kind=kLoop, calls=%fused_computation.4 | loop fusion | flops 13631488 | bytes 4202497 | tf_op jit(solution)/shard_map/convert_element_type | solution.py:805
  84.8 4.0 %convolution_convert_fusion.qkv_ref = bf16[1024,1024]{1,0:T(8,128)(2,1)S(1)} fusion(bf16[1024,1024]{1,0:T(8,128)(2,1)} %fusion.2.rows, bf16[1024,1024]{1,0:T(8,128)(2,1)S(1)} %get-tuple-element.91.weights), kind=kOutput, calls=%fused_computation.31 | convolution fusion | flops 2148532224 | bytes 6291456 | tf_op jit(solution)/shard_map/dot_general | solution.py:23
  88.9 5.5 %attend.2 = bf16[1024,256]{1,0:T(8,128)(2,1)S(1)} custom-call(bf16[1024,1024]{1,0:T(8,128)(2,1)S(1)} %convolution_convert_fusion.qkv_ref, f32[1024,128]{1,0:T(8,128)S(1)} %pad_maximum_fusion.3.cos_ref, f32[1024,128]{1,0:T(8,128)S(1)} %pad_maximum_fusion.4.sin_ref, s32[1024,1]{1,0:T(8,128)S(1)} %copy-done.5, s32[1,1024]{1,0:T(1,128)S(1)} %broadcast_select_fusion.4.seg_row, ...), custom_call_target="tpu_custom_call" | custom-call | flops 6000000 | bytes 100000 | tf_op jit(solution)/shard_map/attend/pallas_call | solution.py:111
  94.5 5.6 %attend.3 = bf16[1024,256]{1,0:T(8,128)(2,1)S(1)} custom-call(bf16[1024,1024]{1,0:T(8,128)(2,1)S(1)} %convolution_convert_fusion.qkv_ref, f32[1024,128]{1,0:T(8,128)S(1)} %pad_maximum_fusion.3.cos_ref, f32[1024,128]{1,0:T(8,128)S(1)} %pad_maximum_fusion.4.sin_ref, s32[1024,1]{1,0:T(8,128)S(1)} %copy-done.5, s32[1,1024]{1,0:T(1,128)S(1)} %broadcast_select_fusion.4.seg_row, ...), custom_call_target="tpu_custom_call" | custom-call | flops 6000000 | bytes 100000 | tf_op jit(solution)/shard_map/attend/pallas_call | solution.py:111
  100.2 5.4 %collective-permute-done.16.refs_3_.refs_5_ = bf16[864,512]{1,0:T(8,128)(2,1)} collective-permute-done((bf16[864,512]{1,0:T(8,128)(2,1)}, bf16[864,512]{1,0:T(8,128)(2,1)}, u32[]{:S(2)}, u32[]{:S(2)}) %collective-permute-start.16) | collective-permute-done | bytes 884768 | tf_op jit(solution)/shard_map/ppermute | solution.py:603
  117.6 19.2 %collective-permute-done.19.refs_6_ = bf16[864,512]{1,0:T(8,128)(2,1)} collective-permute-done((bf16[864,512]{1,0:T(8,128)(2,1)}, bf16[864,512]{1,0:T(8,128)(2,1)}, u32[]{:S(2)}, u32[]{:S(2)}) %collective-permute-start.19) | collective-permute-done | bytes 884768 | tf_op jit(solution)/shard_map/ppermute | solution.py:603
  144.5 20.5 %ffn_first.1 = (bf16[1152,2048]{1,0:T(8,128)(2,1)}, bf16[576,2048]{1,0:T(8,128)(2,1)}, bf16[1728,512]{1,0:T(8,128)(2,1)}, bf16[1728,512]{1,0:T(8,128)(2,1)}) custom-call(s32[1]{0:T(128)} %bitcast.36.which_ref, bf16[864,512]{1,0:T(8,128)(2,1)} %pad_maximum_fusion.2.refs_0_, bf16[864,512]{1,0:T(8,128)(2,1)} %collective-permute-done.11.refs_1_, ...), custom_call_target="tpu_custom_call" | custom-call | flops 14495514 | bytes 100000 | tf_op jit(solution)/shard_map/ffn_first/pallas_call | solution.py:241
  165.0 24.4 %ffn_second.1 = (bf16[1152,2048]{1,0:T(8,128)(2,1)}, bf16[576,2048]{1,0:T(8,128)(2,1)}, bf16[512,1024]{1,0:T(8,128)(2,1)}, bf16[512,1024]{1,0:T(8,128)(2,1)}, bf...) custom-call(s32[1]{0:T(128)} %bitcast.36.which_ref, bf16[864,512]{1,0:T(8,128)(2,1)} %pad_maximum_fusion.2.refs_0_, ...), custom_call_target="tpu_custom_call" | custom-call | flops 18119392 | bytes 100000 | tf_op jit(solution)/shard_map/ffn_second/pallas_call | solution.py:241
  197.2 18.7 %ffn_third.1 = (bf16[864,512]{1,0:T(8,128)(2,1)}, bf16[864,512]{1,0:T(8,128)(2,1)}, bf16[864,512]{1,0:T(8,128)(2,1)}, bf16[864,512]{1,0:T(8,128)(2,1)}, bf16[512...) custom-call(s32[1]{0:T(128)} %bitcast.36.which_ref, ...), custom_call_target="tpu_custom_call" | custom-call | flops 10871635 | bytes 100000 | tf_op jit(solution)/shard_map/ffn_third/pallas_call | solution.py:241
  216.9 3.4 collective-permute-done.30
  231.0 5.8 %collective-permute-done.33 = bf16[1728,512]{1,0:T(8,128)(2,1)} collective-permute-done((bf16[1728,512]{1,0:T(8,128)(2,1)}, bf16[1728,512]{1,0:T(8,128)(2,1)}, u32[]{:S(2)}, u32[]{:S(2)}) %collective-permute-start.33) | collective-permute-done | bytes 1769504 | tf_op jit(solution)/shard_map/ppermute | solution.py:603
  245.5 13.1 %attend_back.2 = (bf16[1024,512]{1,0:T(8,128)(2,1)}, f32[16,128]{1,0:T(8,128)}) custom-call(bf16[1024,1024]{1,0:T(8,128)(2,1)} %copy-done, f32[1024,128]{1,0:T(8,128)} %copy-done.3, f32[1024,128]{1,0:T(8,128)} %copy-done.4, s32[1024,1]{1,0:T(8,128)} %copy.82.seg_col, s32[1,1024]{1,0:T(1,128)} %copy-done.16, f32[8,128]{1,0:T(8,128)} %copy-done.17, ...), custom_call_target="tpu_custom_call" | custom-call | flops 12000000 | bytes 100000 | tf_op jit(solution)/shard_map/attend_back/pallas_call | solution.py:195
  271.1 13.1 %attend_back.3 = (bf16[1024,512]{1,0:T(8,128)(2,1)}, f32[16,128]{1,0:T(8,128)}) custom-call(bf16[1024,1024]{1,0:T(8,128)(2,1)} %copy-done, f32[1024,128]{1,0:T(8,128)} %copy-done.3, f32[1024,128]{1,0:T(8,128)} %copy-done.4, s32[1024,1]{1,0:T(8,128)} %copy.82.seg_col, s32[1,1024]{1,0:T(1,128)} %copy-done.16, f32[8,128]{1,0:T(8,128)} %copy-done.17, ...), custom_call_target="tpu_custom_call" | custom-call | flops 12000000 | bytes 100000 | tf_op jit(solution)/shard_map/attend_back/pallas_call | solution.py:195
  289.8 8.2 %qkv_grads.1 = (bf16[1088,256]{1,0:T(8,128)(2,1)}, bf16[1088,256]{1,0:T(8,128)(2,1)}, bf16[1088,256]{1,0:T(8,128)(2,1)}, bf16[1088,256]{1,0:T(8,128)(2,1)}) custom-call(s32[4]{0:T(128)} %pad_add_fusion.1.starts_ref, bf16[1024,512]{1,0:T(8,128)(2,1)} %get-tuple-element.146.grads_0, bf16[1024,512]{1,0:T(8,128)(2,1)} %get-tuple-element.142.grads_1, ...), custom_call_target="tpu_custom_call" | custom-call | flops 1000000 | bytes 100000 | tf_op jit(solution)/shard_map/qkv_grads/pallas_call | solution.py:241
  299.1 5.4 %collective-permute-start.42 = (bf16[512,1024]{1,0:T(8,128)(2,1)S(1)}, bf16[512,1024]{1,0:T(8,128)(2,1)S(1)}, u32[]{:S(2)}, u32[]{:S(2)}) collective-permute-start(bf16[512,1024]{1,0:T(8,128)(2,1)S(1)} %add_convert_fusion), channel_id=1, source_target_pairs={{0,4},{4,0},{1,5},{5,1},{2,6},{6,2},{3,7},{7,3},{8,12},{12,8},{9,1... | collective-permute-start | bytes 3145736 | tf_op jit(solution)/shard_map/ppermute | solution.py:603
  316.9 10.9 %collective-permute-start.43 = (bf16[512,1024]{1,0:T(8,128)(2,1)S(1)}, bf16[512,1024]{1,0:T(8,128)(2,1)}, u32[]{:S(2)}, u32[]{:S(2)}) collective-permute-start(bf16[512,1024]{1,0:T(8,128)(2,1)S(1)} %fusion.9), channel_id=1, source_target_pairs={{4,1},{1,4},{6,3},{3,6},{12,9},{9,12},{14,11},{11,14},{20,17},{17,... | collective-permute-start | bytes 3145736 | tf_op jit(solution)/shard_map/ppermute | solution.py:603
  328.4 3.4 collective-permute-start.48
  334.4 13.9 %collective-permute-done.47 = bf16[400,256]{1,0:T(8,128)(2,1)S(1)} collective-permute-done((bf16[400,256]{1,0:T(8,128)(2,1)S(1)}, bf16[400,256]{1,0:T(8,128)(2,1)S(1)}, u32[]{:S(2)}, u32[]{:S(2)}) %collective-permute-start.47) | collective-permute-done | bytes 204832 | tf_op jit(solution)/shard_map/ppermute | solution.py:613
  352.9 3.5 collective-permute-start.52
  (325 shorter events, 143.7 us)
Async XLA Ops:
  13.1 24.0 %collective-permute-start = (bf16[512,1024]{1,0:T(8,128)(2,1)}, bf16[512,1024]{1,0:T(8,128)(2,1)}, u32[]{:S(2)}, u32[]{:S(2)}) collective-permute-start(bf16[512,1024]{1,0:T(8,128)(2,1)} %param.14), channel_id=1, source_target_pairs={{4,1},{1,4},{6,3},{3,6},{12,9},{9,12},{14,11},{11,14},{20,17},{17,... | collective-permute-start | bytes 3145736 | tf_op jit(solution)/shard_map/ppermute | solution.py:603
  19.0 48.3 %collective-permute-start.12 = (bf16[512,1024]{1,0:T(8,128)(2,1)}, bf16[512,1024]{1,0:T(8,128)(2,1)}, u32[]{:S(2)}, u32[]{:S(2)}) collective-permute-start(bf16[512,1024]{1,0:T(8,128)(2,1)} %param.16), channel_id=1, source_target_pairs={{4,1},{1,4},{6,3},{3,6},{12,9},{9,12},{14,11},{11,14},{20,17},{17,... | collective-permute-start | bytes 3145736 | tf_op jit(solution)/shard_map/ppermute | solution.py:603
  39.7 31.5 %collective-permute-start.1 = (bf16[512,1024]{1,0:T(8,128)(2,1)}, bf16[512,1024]{1,0:T(8,128)(2,1)}, u32[]{:S(2)}, u32[]{:S(2)}) collective-permute-start(bf16[512,1024]{1,0:T(8,128)(2,1)} %get-tuple-element.199), channel_id=1, source_target_pairs={{0,4},{4,0},{1,5},{5,1},{2,6},{6,2},{3,7},{7,3},{8,12},{12,8},{9,1... | collective-permute-start | bytes 3145736 | tf_op jit(solution)/shard_map/ppermute | solution.py:603
  40.7 30.3 %collective-permute-start.11 = (bf16[864,512]{1,0:T(8,128)(2,1)}, bf16[864,512]{1,0:T(8,128)(2,1)}, u32[]{:S(2)}, u32[]{:S(2)}) collective-permute-start(bf16[864,512]{1,0:T(8,128)(2,1)} %pad_maximum_fusion.2.refs_0_), channel_id=1, source_target_pairs={{0,1},{1,2},{2,3},{3,0},{4,5},{5,6},{6,7},{7,4},{8,9},{9,10},{10,1... | collective-permute-start | bytes 2654216 | tf_op jit(solution)/shard_map/ppermute | solution.py:603
  50.5 23.8 %collective-permute-start.9 = (bf16[1552,256]{1,0:T(8,128)(2,1)S(1)}, bf16[1552,256]{1,0:T(8,128)(2,1)S(1)}, u32[]{:S(2)}, u32[]{:S(2)}) collective-permute-start(bf16[1552,256]{1,0:T(8,128)(2,1)S(1)} %collective-permute-done.8.refs_2_), channel_id=1, source_target_pairs={{0,8},{8,0},{1,9},{9,1},{2,10},{10,2},{3,11},{11,3},{4,12},{12,4},... | collective-permute-start | bytes 2383880 | tf_op jit(solution)/shard_map/ppermute | solution.py:603
  71.0 23.5 %collective-permute-start.13 = (bf16[864,512]{1,0:T(8,128)(2,1)}, bf16[864,512]{1,0:T(8,128)(2,1)}, u32[]{:S(2)}, u32[]{:S(2)}) collective-permute-start(bf16[864,512]{1,0:T(8,128)(2,1)} %collective-permute-done.11.refs_1_), channel_id=1, source_target_pairs={{0,1},{1,2},{2,3},{3,0},{4,5},{5,6},{6,7},{7,4},{8,9},{9,10},{10,1... | collective-permute-start | bytes 2654216 | tf_op jit(solution)/shard_map/ppermute | solution.py:603
  75.1 30.5 %collective-permute-start.15 = (bf16[512,1024]{1,0:T(8,128)(2,1)}, bf16[512,1024]{1,0:T(8,128)(2,1)}, u32[]{:S(2)}, u32[]{:S(2)}) collective-permute-start(bf16[512,1024]{1,0:T(8,128)(2,1)} %broadcast_select_fusion.2.refs_8_.refs_12_), channel_id=1, source_target_pairs={{0,8},{8,0},{1,9},{9,1},{2,10},{10,2},{3,11},{11,3},{4,12},{12,4},... | collective-permute-start | bytes 3145736 | tf_op jit(solution)/shard_map/ppermute | solution.py:603
  115.5 24.5 %collective-permute-start.22 = (bf16[512,1024]{1,0:T(8,128)(2,1)S(1)}, bf16[512,1024]{1,0:T(8,128)(2,1)S(1)}, u32[]{:S(2)}, u32[]{:S(2)}) collective-permute-start(bf16[512,1024]{1,0:T(8,128)(2,1)S(1)} %multiply_convert_fusion.refs_4_.refs_8_), channel_id=1, source_target_pairs={{0,8},{8,0},{1,9},{9,1},{2,10},{10,2},{3,11},{11,3},{4,12},{12,4},... | collective-permute-start | bytes 3145736 | tf_op jit(solution)/shard_map/ppermute | solution.py:603
  116.1 25.1 %collective-permute-start.18 = (bf16[864,512]{1,0:T(8,128)(2,1)}, bf16[864,512]{1,0:T(8,128)(2,1)}, u32[]{:S(2)}, u32[]{:S(2)}) collective-permute-start(bf16[864,512]{1,0:T(8,128)(2,1)} %collective-permute-done.13.refs_2_), channel_id=1, source_target_pairs={{0,1},{1,2},{2,3},{3,0},{4,5},{5,6},{6,7},{7,4},{8,9},{9,10},{10,1... | collective-permute-start | bytes 2654216 | tf_op jit(solution)/shard_map/ppermute | solution.py:603
  116.5 24.9 %collective-permute-start.24 = (bf16[512,1024]{1,0:T(8,128)(2,1)}, bf16[512,1024]{1,0:T(8,128)(2,1)S(1)}, u32[]{:S(2)}, u32[]{:S(2)}) collective-permute-start(bf16[512,1024]{1,0:T(8,128)(2,1)} %broadcast_select_fusion.2.refs_8_.refs_12_), channel_id=1, source_target_pairs={{0,4},{4,0},{1,5},{5,1},{2,6},{6,2},{3,7},{7,3},{8,12},{12,8},{9,1... | collective-permute-start | bytes 3145736 | tf_op jit(solution)/shard_map/ppermute | solution.py:603
  117.5 23.9 %collective-permute-start.25 = (bf16[512,1024]{1,0:T(8,128)(2,1)}, bf16[512,1024]{1,0:T(8,128)(2,1)S(1)}, u32[]{:S(2)}, u32[]{:S(2)}) collective-permute-start(bf16[512,1024]{1,0:T(8,128)(2,1)} %collective-permute-done.15.refs_10_.refs_14_), channel_id=1, source_target_pairs={{0,4},{4,0},{1,5},{5,1},{2,6},{6,2},{3,7},{7,3},{8,12},{12,8},{9,1... | collective-permute-start | bytes 3145736 | tf_op jit(solution)/shard_map/ppermute | solution.py:603
  141.2 23.8 %collective-permute-start.20 = (bf16[864,512]{1,0:T(8,128)(2,1)}, bf16[864,512]{1,0:T(8,128)(2,1)}, u32[]{:S(2)}, u32[]{:S(2)}) collective-permute-start(bf16[864,512]{1,0:T(8,128)(2,1)} %collective-permute-done.18.refs_3_), channel_id=1, source_target_pairs={{0,16},{16,0},{1,17},{17,1},{2,18},{18,2},{3,19},{19,3},{4,20},{20... | collective-permute-start | bytes 2654216 | tf_op jit(solution)/shard_map/ppermute | solution.py:603
  189.9 27.0 %collective-permute-start.29 = (bf16[512,1024]{1,0:T(8,128)(2,1)}, bf16[512,1024]{1,0:T(8,128)(2,1)}, u32[]{:S(2)}, u32[]{:S(2)}) collective-permute-start(bf16[512,1024]{1,0:T(8,128)(2,1)} %get-tuple-element.117), channel_id=1, source_target_pairs={{0,4},{4,0},{1,5},{5,1},{2,6},{6,2},{3,7},{7,3},{8,12},{12,8},{9,1... | collective-permute-start | bytes 3145736 | tf_op jit(solution)/shard_map/ppermute | solution.py:603
  195.7 24.7 %collective-permute-start.30 = (bf16[512,1024]{1,0:T(8,128)(2,1)}, bf16[512,1024]{1,0:T(8,128)(2,1)}, u32[]{:S(2)}, u32[]{:S(2)}) collective-permute-start(bf16[512,1024]{1,0:T(8,128)(2,1)} %add_convert_fusion.3), channel_id=1, source_target_pairs={{0,8},{8,0},{1,9},{9,1},{2,10},{10,2},{3,11},{11,3},{4,12},{12,4},... | collective-permute-start | bytes 3145736 | tf_op jit(solution)/shard_map/ppermute | solution.py:603
  196.9 39.8 %collective-permute-start.33 = (bf16[1728,512]{1,0:T(8,128)(2,1)}, bf16[1728,512]{1,0:T(8,128)(2,1)}, u32[]{:S(2)}, u32[]{:S(2)}) collective-permute-start(bf16[1728,512]{1,0:T(8,128)(2,1)} %get-tuple-element.124), channel_id=1, source_target_pairs={{0,16},{16,0},{1,17},{17,1},{2,18},{18,2},{3,19},{19,3},{4,20},{20... | collective-permute-start | bytes 5308424 | tf_op jit(solution)/shard_map/ppermute | solution.py:603
  228.1 38.6 %collective-permute-start.27 = (bf16[512,1024]{1,0:T(8,128)(2,1)}, bf16[512,1024]{1,0:T(8,128)(2,1)}, u32[]{:S(2)}, u32[]{:S(2)}) collective-permute-start(bf16[512,1024]{1,0:T(8,128)(2,1)} %get-tuple-element.113), channel_id=1, source_target_pairs={{0,4},{4,0},{1,5},{5,1},{2,6},{6,2},{3,7},{7,3},{8,12},{12,8},{9,1... | collective-permute-start | bytes 3145736 | tf_op jit(solution)/shard_map/ppermute | solution.py:603
  228.1 35.3 %collective-permute-start.35 = (bf16[864,512]{1,0:T(8,128)(2,1)}, bf16[864,512]{1,0:T(8,128)(2,1)}, u32[]{:S(2)}, u32[]{:S(2)}) collective-permute-start(bf16[864,512]{1,0:T(8,128)(2,1)} %get-tuple-element.131), channel_id=1, source_target_pairs={{0,16},{16,0},{1,17},{17,1},{2,18},{18,2},{3,19},{19,3},{4,20},{20... | collective-permute-start | bytes 2654216 | tf_op jit(solution)/shard_map/ppermute | solution.py:603
  228.3 56.0 %collective-permute-start.41 = (bf16[864,512]{1,0:T(8,128)(2,1)}, bf16[864,512]{1,0:T(8,128)(2,1)}, u32[]{:S(2)}, u32[]{:S(2)}) collective-permute-start(bf16[864,512]{1,0:T(8,128)(2,1)} %get-tuple-element.138), channel_id=1, source_target_pairs={{0,16},{16,0},{1,17},{17,1},{2,18},{18,2},{3,19},{19,3},{4,20},{20... | collective-permute-start | bytes 2654216 | tf_op jit(solution)/shard_map/ppermute | solution.py:603
  236.7 22.3 %collective-permute-start.31 = (bf16[512,1024]{1,0:T(8,128)(2,1)}, bf16[512,1024]{1,0:T(8,128)(2,1)}, u32[]{:S(2)}, u32[]{:S(2)}) collective-permute-start(bf16[512,1024]{1,0:T(8,128)(2,1)} %add_convert_fusion.2), channel_id=1, source_target_pairs={{0,8},{8,0},{1,9},{9,1},{2,10},{10,2},{3,11},{11,3},{4,12},{12,4},... | collective-permute-start | bytes 3145736 | tf_op jit(solution)/shard_map/ppermute | solution.py:603
  287.6 22.3 %collective-permute-start.50 = (bf16[864,512]{1,0:T(8,128)(2,1)S(1)}, bf16[864,512]{1,0:T(8,128)(2,1)}, u32[]{:S(2)}, u32[]{:S(2)}) collective-permute-start(bf16[864,512]{1,0:T(8,128)(2,1)S(1)} %add_convert_fusion.4), channel_id=1, source_target_pairs={{0,1},{1,2},{2,3},{3,0},{4,5},{5,6},{6,7},{7,4},{8,9},{9,10},{10,1... | collective-permute-start | bytes 2654216 | tf_op jit(solution)/shard_map/ppermute | solution.py:603
  305.2 22.8 %collective-permute-start.37 = (bf16[512,1024]{1,0:T(8,128)(2,1)S(1)}, bf16[512,1024]{1,0:T(8,128)(2,1)S(1)}, u32[]{:S(2)}, u32[]{:S(2)}) collective-permute-start(bf16[512,1024]{1,0:T(8,128)(2,1)S(1)} %copy-done.33), channel_id=1, source_target_pairs={{4,1},{1,4},{6,3},{3,6},{12,9},{9,12},{14,11},{11,14},{20,17},{17,... | collective-permute-start | bytes 3145736 | tf_op jit(solution)/shard_map/ppermute | solution.py:603
  316.9 47.9 %collective-permute-start.43 = (bf16[512,1024]{1,0:T(8,128)(2,1)S(1)}, bf16[512,1024]{1,0:T(8,128)(2,1)}, u32[]{:S(2)}, u32[]{:S(2)}) collective-permute-start(bf16[512,1024]{1,0:T(8,128)(2,1)S(1)} %fusion.9), channel_id=1, source_target_pairs={{4,1},{1,4},{6,3},{3,6},{12,9},{9,12},{14,11},{11,14},{20,17},{17,... | collective-permute-start | bytes 3145736 | tf_op jit(solution)/shard_map/ppermute | solution.py:603
  327.8 25.0 %collective-permute-start.51 = (bf16[3,288,256]{2,1,0:T(8,128)(2,1)S(1)}, bf16[3,288,256]{2,1,0:T(8,128)(2,1)S(1)}, u32[]{:S(2)}, u32[]{:S(2)}) collective-permute-start(bf16[3,288,256]{2,1,0:T(8,128)(2,1)S(1)} %get-tuple-element.154), channel_id=1, source_target_pairs={{0,8},{8,0},{1,9},{9,1},{2,10},{10,2},{3,11},{11,3},{4,12},{12,4},... | collective-permute-start | bytes 1327112 | tf_op jit(solution)/shard_map/ppermute | solution.py:603
  328.4 22.1 %collective-permute-start.48 = (bf16[400,256]{1,0:T(8,128)(2,1)S(1)}, bf16[400,256]{1,0:T(8,128)(2,1)S(1)}, u32[]{:S(2)}, u32[]{:S(2)}) collective-permute-start(bf16[400,256]{1,0:T(8,128)(2,1)S(1)} %pad_maximum_fusion.6), channel_id=1, source_target_pairs={{0,2},{1,3},{2,0},{3,1},{4,6},{5,7},{6,4},{7,5},{8,10},{9,11},{10,... | collective-permute-start | bytes 614408 | tf_op jit(solution)/shard_map/ppermute | solution.py:613
  (87 other events, 1166.8 us)

commit v5 on v4

--- a/solution.py
+++ b/solution.py
@@ -213,7 +213,7 @@
             jax.ShapeDtypeStruct((8 * groups, lanes), f32),
         ),
         scratch_shapes=[pltpu.VMEM((length, lanes), bf16)] * 3 + [pltpu.VMEM((length, lanes), f32)] * 3,
-        compiler_params=pltpu.CompilerParams(vmem_limit_bytes=58 * 2**20),
+        compiler_params=pltpu.CompilerParams(vmem_limit_bytes=28 * 2**20),
         cost_estimate=cost(12 * 10**9),
         name="attend_back",
     )(qkv, cosine, sine, seg_col, seg_row, gains, grad_context)
@@ -491,7 +491,7 @@
 
 
 def qkv_grads_kernel(groups, spaced, starts_ref, grads_0, grads_1, rows, weights, extra_ref, gain_ref, sums_0, sums_1, *refs):
-    outs, rest = refs[:4], refs[4:]
+    outs, rest = refs[: len(refs) - 8], refs[len(refs) - 8 :]
     grad_s, rows_s, weight_s, extra_s, gain_s, sums_s, out_s, sems = rest
     size = (grads_0.shape[1] + grads_1.shape[1]) // groups
     width = outs[0].shape[1]
@@ -504,7 +504,7 @@
     loads.start("b", (sums_0, sums_s.at[pl.ds(0, sums_0.shape[0])]))
     loads.start("b", (sums_1, sums_s.at[pl.ds(sums_0.shape[0], sums_1.shape[0])]))
     loads.wait("a")
-    for i in range(4):
+    for i in range(len(outs)):
         lanes = pl.ds(pl.multiple_of(starts_ref[i], width), width)
         block = dot(grad_s[...], rows_s[:, lanes], 0, 0)
         if i == 0:
@@ -535,13 +535,13 @@
 def qkv_grads(starts, grads, rows, weights, extra, gains, sums, groups, spaced):
     count, width = rows.shape
     columns, more = grads[0].shape[1] + grads[1].shape[1], extra.shape[0]
-    block = (columns + groups * more, width // 4)
+    block, blocks = (columns + groups * more, width // 4), len(starts)
     return call_local(
         functools.partial(qkv_grads_kernel, groups, spaced),
         jnp.stack(starts).astype(jnp.int32),
         [*grads, rows, weights, extra, gains, *sums],
-        [jax.ShapeDtypeStruct(block, bf16)] * 4,
-        [pl.ANY] * 4,
+        [jax.ShapeDtypeStruct(block, bf16)] * blocks,
+        [pl.ANY] * blocks,
         [
             pltpu.VMEM((count, columns), bf16),
             pltpu.VMEM((count, width), bf16),
@@ -549,9 +549,9 @@
             pltpu.VMEM((more, width), f32),
             pltpu.VMEM(gains.shape, f32),
             pltpu.VMEM((8 * groups, sums[0].shape[1]), f32),
-            pltpu.VMEM((4, *block), bf16),
+            pltpu.VMEM((blocks, *block), bf16),
         ],
-        12,
+        8 + blocks,
         10**9,
         "qkv_grads",
     )
@@ -919,9 +919,10 @@
         starts = [which[0] + i * (width // 4) for i in range(4)]
     else:
         starts = [(a * x_size + b) * pair for a, b in ((1 - y, 1 - x), (y, 1 - x), (1 - y, x), (y, x))]
-    blocks = qkv_grads(
-        starts, (grad_first, grad_last), normed_one, qkv_full, extra, gain_one, (sums_first, sums_last), z_size, spaced
-    )
+    given = (qkv_full, extra, gain_one, (sums_first, sums_last), z_size, spaced)
+    blocks = list(qkv_grads(starts[:1], (grad_first, grad_last), normed_one, *given))
+    grad_last = after(grad_last, blocks[0])
+    blocks += qkv_grads(starts[1:], (grad_first, grad_last), normed_one, *given)
     if y_size == 2:
         far_got = lanes.move(blocks[0], "x", [(0, 1), (1, 0)], None)
     grad_first = after(grad_first, blocks[3])
@@ -935,7 +936,6 @@
     sent = two_terms(1 - c).astype(bf16)
     grad_normed_one = two_terms(c) + lanes.swap(sent, "c").astype(f32)
     tokens_grad = (grad_mid + norm_back(grad_normed_one * gain_one, hat_one, root_one)).astype(bf16)
-    tokens_got = lanes.move(tokens_grad, ("c", "z"), pairs, None)
     if y_size > 2:
         qkv_part = plane_scatter(jnp.concatenate(blocks, axis=1), sizes, pair, lanes).astype(bf16)
     else:
@@ -974,6 +974,7 @@
         z_size,
         lanes,
     )
+    tokens_got = lanes.move(after(tokens_grad, lanes.last["z"][0]), ("c", "z"), pairs, None)
     value = after(value.astype(bf16), dealt)
     kept = lane_block(value, c, part)
     sent = lanes.swap(lane_block(value, 1 - c, part), "c")

time: 375 us -> 363 us (0.968)
  starting transfers between devices: 67 us -> 56.6 us
  waiting for transfers between devices: 90.8 us -> 99.5 us
  other arithmetic: 49.6 us -> 43.5 us
    ppermute x48, waiting for transfers between devices: 68.6 us -> 85 us  [move(): got = lax.ppermute(self.wait(value, lane), axes, pairs)]
    ppermute x48, starting transfers between devices: 57.3 us -> 48.3 us  [move(): got = lax.ppermute(self.wait(value, lane), axes, pairs)]
    ppermute x6, waiting for transfers between devices: 22.2 us -> 14.5 us  [around(): lax.ppermute(v, 'z', ring(size, signs * (i + 1)))]
    pallas_call x2, Pallas kernels: 26.2 us -> 22.3 us  [attend_back(): pl.pallas_call(functools.partial(attend_back_kernel, head), grid=(groups,...]
    pallas_call x5 -> x6, Pallas kernels: 73.2 us -> 76 us  [call_local(): pl.pallas_call(kernel, in_specs=[pl.BlockSpec(memory_space=pltpu.SMEM)] +...]
    unnamed x122 -> x136, local copies, waits for them, and re-layouts: 17.1 us -> 17.1 us
  transfers between devices with their start and end apart: 54 -> 54, of which waited for: 20 -> 23; matrix products, arithmetic and copies ran while one was open for 20% -> 19% of each run, Pallas kernels for 23% -> 23%
where the time goes in v5:
time: 363 us; the launch traced here: 356 us
  Pallas kernels  109 us (30%)
  waiting for transfers between devices  99.5 us (27%)
  starting transfers between devices  56.6 us (16%)
  other arithmetic  43.5 us (12%)
  local copies, waits for them, and re-layouts  29.3 us (8%)
  matrix products  15.5 us (4%)
    ppermute x48, waiting for transfers between devices, move(): got = lax.ppermute(self.wait(value, lane), axes, pairs)  85 us
    pallas_call x6, Pallas kernels, call_local(): pl.pallas_call(kernel, in_specs=[pl.BlockSpec(memory_space=pltpu.SMEM)] +...  76 us
    ppermute x48, starting transfers between devices, move(): got = lax.ppermute(self.wait(value, lane), axes, pairs)  48.3 us
    pallas_call x2, Pallas kernels, attend_back(): pl.pallas_call(functools.partial(attend_back_kernel, head), grid=(groups,...  22.3 us
    unnamed x136, local copies, waits for them, and re-layouts  17.1 us
    dot_general x9, matrix products, dot(): lax.dot_general(left, right, (((left_dim,), (right_dim,)), ((), ())), pre...  15.5 us
    ppermute x6, waiting for transfers between devices, around(): lax.ppermute(v, 'z', ring(size, signs * (i + 1)))  14.5 us
    pallas_call x2, Pallas kernels, attend(): pl.pallas_call(functools.partial(attend_kernel, head), grid=(groups,), in...  11 us
  transfers between devices with their start and end apart: 54, of which 23 were waited for; matrix products, arithmetic and copies ran while one was open for 19% of the time, Pallas kernels for 23%

profile of v5, /device:TPU:1, one launch (start us, length us, event | category | flops | bytes accessed | tf_op | source)
XLA Modules:
  0.0 356.2 jit_solution(6581062377473537950)
XLA Ops:
  4.4 4.2 %collective-permute-start.4 = (bf16[768,128]{1,0:T(8,128)(2,1)S(1)}, bf16[768,128]{1,0:T(8,128)(2,1)S(1)}, u32[]{:S(2)}, u32[]{:S(2)}) collective-permute-start(bf16[768,128]{1,0:T(8,128)(2,1)S(1)} %bitcast.112), channel_id=1, source_target_pairs={{0,3},{1,0},{2,1},{3,2},{4,7},{5,4},{6,5},{7,6},{8,11},{9,8},{10,9... | collective-permute-start | bytes 589832 | tf_op jit(solution)/shard_map/ppermute | solution.py:613
  13.1 5.8 %collective-permute-start = (bf16[512,1024]{1,0:T(8,128)(2,1)}, bf16[512,1024]{1,0:T(8,128)(2,1)}, u32[]{:S(2)}, u32[]{:S(2)}) collective-permute-start(bf16[512,1024]{1,0:T(8,128)(2,1)} %param.14), channel_id=1, source_target_pairs={{4,1},{1,4},{6,3},{3,6},{12,9},{9,12},{14,11},{11,14},{20,17},{17,... | collective-permute-start | bytes 3145736 | tf_op jit(solution)/shard_map/ppermute | solution.py:603
  21.0 3.9 %collective-permute-done.3 = bf16[768,128]{1,0:T(8,128)(2,1)S(1)} collective-permute-done((bf16[768,128]{1,0:T(8,128)(2,1)S(1)}, bf16[768,128]{1,0:T(8,128)(2,1)S(1)}, u32[]{:S(2)}, u32[]{:S(2)}) %collective-permute-start.3) | collective-permute-done | bytes 196640 | tf_op jit(solution)/shard_map/ppermute | solution.py:613
  44.3 5.0 %collective-permute-done.8.refs_2_ = bf16[1552,256]{1,0:T(8,128)(2,1)S(1)} collective-permute-done((bf16[1552,256]{1,0:T(8,128)(2,1)S(1)}, bf16[1552,256]{1,0:T(8,128)(2,1)S(1)}, u32[]{:S(2)}, u32[]{:S(2)}) %collective-permute-start.8) | collective-permute-done | bytes 794656 | tf_op jit(solution)/shard_map/ppermute | solution.py:603
  53.8 13.6 %collective-permute-done.12 = bf16[512,1024]{1,0:T(8,128)(2,1)} collective-permute-done((bf16[512,1024]{1,0:T(8,128)(2,1)}, bf16[512,1024]{1,0:T(8,128)(2,1)}, u32[]{:S(2)}, u32[]{:S(2)}) %collective-permute-start.12) | collective-permute-done | bytes 1048608 | tf_op jit(solution)/shard_map/ppermute | solution.py:603
  79.8 4.4 %fusion.2.rows = bf16[1024,1024]{1,0:T(8,128)(2,1)} fusion(f32[1024]{0:T(1024)S(1)} %bitcast.124, f32[1024]{0:T(1024)S(1)} %add_rsqrt_fusion, bf16[512,1024]{1,0:T(8,128)(2,1)} %get-tuple-element.201, bf16[512,1024]{1,0:T(8,128)(2,1)} %collective-permute-done.1, pred[]{:T(512)S(6)} %eq.12), kind=kLoop, calls=%fused_computation.4 | loop fusion | flops 13631488 | bytes 4202497 | tf_op jit(solution)/shard_map/convert_element_type | solution.py:805
  84.7 4.0 %convolution_convert_fusion.qkv_ref = bf16[1024,1024]{1,0:T(8,128)(2,1)S(1)} fusion(bf16[1024,1024]{1,0:T(8,128)(2,1)} %fusion.2.rows, bf16[1024,1024]{1,0:T(8,128)(2,1)S(1)} %get-tuple-element.92.weights), kind=kOutput, calls=%fused_computation.31 | convolution fusion | flops 2148532224 | bytes 6291456 | tf_op jit(solution)/shard_map/dot_general | solution.py:23
  88.9 5.5 %attend.2 = bf16[1024,256]{1,0:T(8,128)(2,1)S(1)} custom-call(bf16[1024,1024]{1,0:T(8,128)(2,1)S(1)} %convolution_convert_fusion.qkv_ref, f32[1024,128]{1,0:T(8,128)S(1)} %pad_maximum_fusion.3.cos_ref, f32[1024,128]{1,0:T(8,128)S(1)} %pad_maximum_fusion.4.sin_ref, s32[1024,1]{1,0:T(8,128)S(1)} %copy-done.5, s32[1,1024]{1,0:T(1,128)S(1)} %broadcast_select_fusion.4.seg_row, ...), custom_call_target="tpu_custom_call" | custom-call | flops 6000000 | bytes 100000 | tf_op jit(solution)/shard_map/attend/pallas_call | solution.py:111
  94.4 5.5 %attend.3 = bf16[1024,256]{1,0:T(8,128)(2,1)S(1)} custom-call(bf16[1024,1024]{1,0:T(8,128)(2,1)S(1)} %convolution_convert_fusion.qkv_ref, f32[1024,128]{1,0:T(8,128)S(1)} %pad_maximum_fusion.3.cos_ref, f32[1024,128]{1,0:T(8,128)S(1)} %pad_maximum_fusion.4.sin_ref, s32[1024,1]{1,0:T(8,128)S(1)} %copy-done.5, s32[1,1024]{1,0:T(1,128)S(1)} %broadcast_select_fusion.4.seg_row, ...), custom_call_target="tpu_custom_call" | custom-call | flops 6000000 | bytes 100000 | tf_op jit(solution)/shard_map/attend/pallas_call | solution.py:111
  100.0 5.5 %collective-permute-done.16.refs_3_.refs_5_ = bf16[864,512]{1,0:T(8,128)(2,1)} collective-permute-done((bf16[864,512]{1,0:T(8,128)(2,1)}, bf16[864,512]{1,0:T(8,128)(2,1)}, u32[]{:S(2)}, u32[]{:S(2)}) %collective-permute-start.16) | collective-permute-done | bytes 884768 | tf_op jit(solution)/shard_map/ppermute | solution.py:603
  117.3 19.1 %collective-permute-done.19.refs_6_ = bf16[864,512]{1,0:T(8,128)(2,1)} collective-permute-done((bf16[864,512]{1,0:T(8,128)(2,1)}, bf16[864,512]{1,0:T(8,128)(2,1)}, u32[]{:S(2)}, u32[]{:S(2)}) %collective-permute-start.19) | collective-permute-done | bytes 884768 | tf_op jit(solution)/shard_map/ppermute | solution.py:603
  144.2 20.5 %ffn_first.1 = (bf16[1152,2048]{1,0:T(8,128)(2,1)}, bf16[576,2048]{1,0:T(8,128)(2,1)}, bf16[1728,512]{1,0:T(8,128)(2,1)}, bf16[1728,512]{1,0:T(8,128)(2,1)}) custom-call(s32[1]{0:T(128)} %bitcast.36.which_ref, bf16[864,512]{1,0:T(8,128)(2,1)} %pad_maximum_fusion.2.refs_0_, bf16[864,512]{1,0:T(8,128)(2,1)} %collective-permute-done.11.refs_1_, ...), custom_call_target="tpu_custom_call" | custom-call | flops 14495514 | bytes 100000 | tf_op jit(solution)/shard_map/ffn_first/pallas_call | solution.py:241
  164.7 24.4 %ffn_second.1 = (bf16[1152,2048]{1,0:T(8,128)(2,1)}, bf16[576,2048]{1,0:T(8,128)(2,1)}, bf16[512,1024]{1,0:T(8,128)(2,1)}, bf16[512,1024]{1,0:T(8,128)(2,1)}, bf...) custom-call(s32[1]{0:T(128)} %bitcast.36.which_ref, bf16[864,512]{1,0:T(8,128)(2,1)} %pad_maximum_fusion.2.refs_0_, ...), custom_call_target="tpu_custom_call" | custom-call | flops 18119392 | bytes 100000 | tf_op jit(solution)/shard_map/ffn_second/pallas_call | solution.py:241
  195.9 18.8 %ffn_third.1 = (bf16[864,512]{1,0:T(8,128)(2,1)}, bf16[864,512]{1,0:T(8,128)(2,1)}, bf16[864,512]{1,0:T(8,128)(2,1)}, bf16[864,512]{1,0:T(8,128)(2,1)}, bf16[512...) custom-call(s32[1]{0:T(128)} %bitcast.36.which_ref, ...), custom_call_target="tpu_custom_call" | custom-call | flops 10871635 | bytes 100000 | tf_op jit(solution)/shard_map/ffn_third/pallas_call | solution.py:241
  215.7 3.7 %collective-permute-done.30 = bf16[512,1024]{1,0:T(8,128)(2,1)} collective-permute-done((bf16[512,1024]{1,0:T(8,128)(2,1)}, bf16[512,1024]{1,0:T(8,128)(2,1)}, u32[]{:S(2)}, u32[]{:S(2)}) %collective-permute-start.30) | collective-permute-done | bytes 1048608 | tf_op jit(solution)/shard_map/ppermute | solution.py:603
  228.5 6.9 %collective-permute-done.33 = bf16[1728,512]{1,0:T(8,128)(2,1)} collective-permute-done((bf16[1728,512]{1,0:T(8,128)(2,1)}, bf16[1728,512]{1,0:T(8,128)(2,1)}, u32[]{:S(2)}, u32[]{:S(2)}) %collective-permute-start.33) | collective-permute-done | bytes 1769504 | tf_op jit(solution)/shard_map/ppermute | solution.py:603
  242.8 11.1 %attend_back.2 = (bf16[1024,512]{1,0:T(8,128)(2,1)S(1)}, f32[16,128]{1,0:T(8,128)S(1)}) custom-call(bf16[1024,1024]{1,0:T(8,128)(2,1)S(1)} %copy-done.4, f32[1024,128]{1,0:T(8,128)S(1)} %pad_maximum_fusion.3.cos_ref, f32[1024,128]{1,0:T(8,128)S(1)} %pad_maximum_fusion.4.sin_ref, s32[1024,1]{1,0:T(8,128)S(1)} %copy-done.6, ...), custom_call_target="tpu_custom_call" | custom-call | flops 12000000 | bytes 100000 | tf_op jit(solution)/shard_map/attend_back/pallas_call | solution.py:195
  264.5 11.1 %attend_back.3 = (bf16[1024,512]{1,0:T(8,128)(2,1)S(1)}, f32[16,128]{1,0:T(8,128)S(1)}) custom-call(bf16[1024,1024]{1,0:T(8,128)(2,1)S(1)} %copy-done.4, f32[1024,128]{1,0:T(8,128)S(1)} %pad_maximum_fusion.3.cos_ref, f32[1024,128]{1,0:T(8,128)S(1)} %pad_maximum_fusion.4.sin_ref, s32[1024,1]{1,0:T(8,128)S(1)} %copy-done.6, ...), custom_call_target="tpu_custom_call" | custom-call | flops 12000000 | bytes 100000 | tf_op jit(solution)/shard_map/attend_back/pallas_call | solution.py:195
  280.6 4.3 %qkv_grads.2 = bf16[1088,256]{1,0:T(8,128)(2,1)} custom-call(s32[1]{0:T(128)} %bitcast.3.starts_ref, bf16[1024,512]{1,0:T(8,128)(2,1)} %copy-done.7, bf16[1024,512]{1,0:T(8,128)(2,1)} %copy-done.9, bf16[1024,1024]{1,0:T(8,128)(2,1)} %fusion.2.rows, bf16[1024,1024]{1,0:T(8,128)(2,1)} %copy-done, f32[16,1024]{1,0:T(8,128)} %maximum_maximum_fusion.extra_ref, ...), custom_call_target="tpu_custom_call" | custom-call | flops 1000000 | bytes 100000 | tf_op jit(solution)/shard_map/qkv_grads/pallas_call | solution.py:241
  286.6 6.7 %qkv_grads.3 = (bf16[1088,256]{1,0:T(8,128)(2,1)}, bf16[1088,256]{1,0:T(8,128)(2,1)}, bf16[1088,256]{1,0:T(8,128)(2,1)}) custom-call(s32[3]{0:T(128)} %pad_add_fusion.1.starts_ref, bf16[1024,512]{1,0:T(8,128)(2,1)} %copy-done.7, bf16[1024,512]{1,0:T(8,128)(2,1)} %copy-done.9, bf16[1024,1024]{1,0:T(8,128)(2,1)} %fusion.2.rows, bf16[1024,1024]{1,0:T(8,128)(2,1)} %copy-done, ...), custom_call_target="tpu_custom_call" | custom-call | flops 1000000 | bytes 100000 | tf_op jit(solution)/shard_map/qkv_grads/pallas_call | solution.py:241
  294.1 5.4 %collective-permute-start.42 = (bf16[512,1024]{1,0:T(8,128)(2,1)S(1)}, bf16[512,1024]{1,0:T(8,128)(2,1)S(1)}, u32[]{:S(2)}, u32[]{:S(2)}) collective-permute-start(bf16[512,1024]{1,0:T(8,128)(2,1)S(1)} %add_convert_fusion), channel_id=1, source_target_pairs={{0,4},{4,0},{1,5},{5,1},{2,6},{6,2},{3,7},{7,3},{8,12},{12,8},{9,1... | collective-permute-start | bytes 3145736 | tf_op jit(solution)/shard_map/ppermute | solution.py:603
  311.7 4.9 %collective-permute-done.44 = bf16[1088,256]{1,0:T(8,128)(2,1)S(1)} collective-permute-done((bf16[1088,256]{1,0:T(8,128)(2,1)S(1)}, bf16[1088,256]{1,0:T(8,128)(2,1)S(1)}, u32[]{:S(2)}, u32[]{:S(2)}) %collective-permute-start.44) | collective-permute-done | bytes 557088 | tf_op jit(solution)/shard_map/ppermute | solution.py:603
  325.7 10.5 %collective-permute-done.46 = bf16[400,256]{1,0:T(8,128)(2,1)S(1)} collective-permute-done((bf16[400,256]{1,0:T(8,128)(2,1)S(1)}, bf16[400,256]{1,0:T(8,128)(2,1)S(1)}, u32[]{:S(2)}, u32[]{:S(2)}) %collective-permute-start.46) | collective-permute-done | bytes 204832 | tf_op jit(solution)/shard_map/ppermute | solution.py:613
  336.2 4.7 %collective-permute-start.47 = (bf16[512,1024]{1,0:T(8,128)(2,1)S(1)}, bf16[512,1024]{1,0:T(8,128)(2,1)}, u32[]{:S(2)}, u32[]{:S(2)}) collective-permute-start(bf16[512,1024]{1,0:T(8,128)(2,1)S(1)} %fusion.9), channel_id=1, source_target_pairs={{4,1},{1,4},{6,3},{3,6},{12,9},{9,12},{14,11},{11,14},{20,17},{17,... | collective-permute-start | bytes 3145736 | tf_op jit(solution)/shard_map/ppermute | solution.py:603
  (340 shorter events, 144.1 us)
Async XLA Ops:
  13.1 24.0 %collective-permute-start = (bf16[512,1024]{1,0:T(8,128)(2,1)}, bf16[512,1024]{1,0:T(8,128)(2,1)}, u32[]{:S(2)}, u32[]{:S(2)}) collective-permute-start(bf16[512,1024]{1,0:T(8,128)(2,1)} %param.14), channel_id=1, source_target_pairs={{4,1},{1,4},{6,3},{3,6},{12,9},{9,12},{14,11},{11,14},{20,17},{17,... | collective-permute-start | bytes 3145736 | tf_op jit(solution)/shard_map/ppermute | solution.py:603
  19.0 48.3 %collective-permute-start.12 = (bf16[512,1024]{1,0:T(8,128)(2,1)}, bf16[512,1024]{1,0:T(8,128)(2,1)}, u32[]{:S(2)}, u32[]{:S(2)}) collective-permute-start(bf16[512,1024]{1,0:T(8,128)(2,1)} %param.16), channel_id=1, source_target_pairs={{4,1},{1,4},{6,3},{3,6},{12,9},{9,12},{14,11},{11,14},{20,17},{17,... | collective-permute-start | bytes 3145736 | tf_op jit(solution)/shard_map/ppermute | solution.py:603
  39.7 31.5 %collective-permute-start.1 = (bf16[512,1024]{1,0:T(8,128)(2,1)}, bf16[512,1024]{1,0:T(8,128)(2,1)}, u32[]{:S(2)}, u32[]{:S(2)}) collective-permute-start(bf16[512,1024]{1,0:T(8,128)(2,1)} %get-tuple-element.201), channel_id=1, source_target_pairs={{0,4},{4,0},{1,5},{5,1},{2,6},{6,2},{3,7},{7,3},{8,12},{12,8},{9,1... | collective-permute-start | bytes 3145736 | tf_op jit(solution)/shard_map/ppermute | solution.py:603
  41.4 29.6 %collective-permute-start.11 = (bf16[864,512]{1,0:T(8,128)(2,1)}, bf16[864,512]{1,0:T(8,128)(2,1)}, u32[]{:S(2)}, u32[]{:S(2)}) collective-permute-start(bf16[864,512]{1,0:T(8,128)(2,1)} %pad_maximum_fusion.2.refs_0_), channel_id=1, source_target_pairs={{0,1},{1,2},{2,3},{3,0},{4,5},{5,6},{6,7},{7,4},{8,9},{9,10},{10,1... | collective-permute-start | bytes 2654216 | tf_op jit(solution)/shard_map/ppermute | solution.py:603
  51.1 23.1 %collective-permute-start.9 = (bf16[1552,256]{1,0:T(8,128)(2,1)S(1)}, bf16[1552,256]{1,0:T(8,128)(2,1)S(1)}, u32[]{:S(2)}, u32[]{:S(2)}) collective-permute-start(bf16[1552,256]{1,0:T(8,128)(2,1)S(1)} %collective-permute-done.8.refs_2_), channel_id=1, source_target_pairs={{0,8},{8,0},{1,9},{9,1},{2,10},{10,2},{3,11},{11,3},{4,12},{12,4},... | collective-permute-start | bytes 2383880 | tf_op jit(solution)/shard_map/ppermute | solution.py:603
  71.0 23.4 %collective-permute-start.13 = (bf16[864,512]{1,0:T(8,128)(2,1)}, bf16[864,512]{1,0:T(8,128)(2,1)}, u32[]{:S(2)}, u32[]{:S(2)}) collective-permute-start(bf16[864,512]{1,0:T(8,128)(2,1)} %collective-permute-done.11.refs_1_), channel_id=1, source_target_pairs={{0,1},{1,2},{2,3},{3,0},{4,5},{5,6},{6,7},{7,4},{8,9},{9,10},{10,1... | collective-permute-start | bytes 2654216 | tf_op jit(solution)/shard_map/ppermute | solution.py:603
  75.1 30.5 %collective-permute-start.15 = (bf16[512,1024]{1,0:T(8,128)(2,1)}, bf16[512,1024]{1,0:T(8,128)(2,1)}, u32[]{:S(2)}, u32[]{:S(2)}) collective-permute-start(bf16[512,1024]{1,0:T(8,128)(2,1)} %broadcast_select_fusion.2.refs_8_.refs_12_), channel_id=1, source_target_pairs={{0,8},{8,0},{1,9},{9,1},{2,10},{10,2},{3,11},{11,3},{4,12},{12,4},... | collective-permute-start | bytes 3145736 | tf_op jit(solution)/shard_map/ppermute | solution.py:603
  84.5 21.1 %collective-permute-start.16 = (bf16[864,512]{1,0:T(8,128)(2,1)}, bf16[864,512]{1,0:T(8,128)(2,1)}, u32[]{:S(2)}, u32[]{:S(2)}) collective-permute-start(bf16[864,512]{1,0:T(8,128)(2,1)} %collective-permute-done.11.refs_1_), channel_id=1, source_target_pairs={{0,16},{16,0},{1,17},{17,1},{2,18},{18,2},{3,19},{19,3},{4,20},{20... | collective-permute-start | bytes 2654216 | tf_op jit(solution)/shard_map/ppermute | solution.py:603
  115.3 24.5 %collective-permute-start.22 = (bf16[512,1024]{1,0:T(8,128)(2,1)S(1)}, bf16[512,1024]{1,0:T(8,128)(2,1)S(1)}, u32[]{:S(2)}, u32[]{:S(2)}) collective-permute-start(bf16[512,1024]{1,0:T(8,128)(2,1)S(1)} %multiply_convert_fusion.refs_4_.refs_8_), channel_id=1, source_target_pairs={{0,8},{8,0},{1,9},{9,1},{2,10},{10,2},{3,11},{11,3},{4,12},{12,4},... | collective-permute-start | bytes 3145736 | tf_op jit(solution)/shard_map/ppermute | solution.py:603
  115.6 20.8 %collective-permute-start.19 = (bf16[864,512]{1,0:T(8,128)(2,1)}, bf16[864,512]{1,0:T(8,128)(2,1)}, u32[]{:S(2)}, u32[]{:S(2)}) collective-permute-start(bf16[864,512]{1,0:T(8,128)(2,1)} %collective-permute-done.13.refs_2_), channel_id=1, source_target_pairs={{0,16},{16,0},{1,17},{17,1},{2,18},{18,2},{3,19},{19,3},{4,20},{20... | collective-permute-start | bytes 2654216 | tf_op jit(solution)/shard_map/ppermute | solution.py:603
  115.9 25.1 %collective-permute-start.18 = (bf16[864,512]{1,0:T(8,128)(2,1)}, bf16[864,512]{1,0:T(8,128)(2,1)}, u32[]{:S(2)}, u32[]{:S(2)}) collective-permute-start(bf16[864,512]{1,0:T(8,128)(2,1)} %collective-permute-done.13.refs_2_), channel_id=1, source_target_pairs={{0,1},{1,2},{2,3},{3,0},{4,5},{5,6},{6,7},{7,4},{8,9},{9,10},{10,1... | collective-permute-start | bytes 2654216 | tf_op jit(solution)/shard_map/ppermute | solution.py:603
  116.3 24.9 %collective-permute-start.24 = (bf16[512,1024]{1,0:T(8,128)(2,1)}, bf16[512,1024]{1,0:T(8,128)(2,1)S(1)}, u32[]{:S(2)}, u32[]{:S(2)}) collective-permute-start(bf16[512,1024]{1,0:T(8,128)(2,1)} %broadcast_select_fusion.2.refs_8_.refs_12_), channel_id=1, source_target_pairs={{0,4},{4,0},{1,5},{5,1},{2,6},{6,2},{3,7},{7,3},{8,12},{12,8},{9,1... | collective-permute-start | bytes 3145736 | tf_op jit(solution)/shard_map/ppermute | solution.py:603
  117.3 23.9 %collective-permute-start.25 = (bf16[512,1024]{1,0:T(8,128)(2,1)}, bf16[512,1024]{1,0:T(8,128)(2,1)S(1)}, u32[]{:S(2)}, u32[]{:S(2)}) collective-permute-start(bf16[512,1024]{1,0:T(8,128)(2,1)} %collective-permute-done.15.refs_10_.refs_14_), channel_id=1, source_target_pairs={{0,4},{4,0},{1,5},{5,1},{2,6},{6,2},{3,7},{7,3},{8,12},{12,8},{9,1... | collective-permute-start | bytes 3145736 | tf_op jit(solution)/shard_map/ppermute | solution.py:603
  141.0 23.8 %collective-permute-start.20 = (bf16[864,512]{1,0:T(8,128)(2,1)}, bf16[864,512]{1,0:T(8,128)(2,1)}, u32[]{:S(2)}, u32[]{:S(2)}) collective-permute-start(bf16[864,512]{1,0:T(8,128)(2,1)} %collective-permute-done.18.refs_3_), channel_id=1, source_target_pairs={{0,16},{16,0},{1,17},{17,1},{2,18},{18,2},{3,19},{19,3},{4,20},{20... | collective-permute-start | bytes 2654216 | tf_op jit(solution)/shard_map/ppermute | solution.py:603
  189.6 26.1 %collective-permute-start.29 = (bf16[512,1024]{1,0:T(8,128)(2,1)}, bf16[512,1024]{1,0:T(8,128)(2,1)S(1)}, u32[]{:S(2)}, u32[]{:S(2)}) collective-permute-start(bf16[512,1024]{1,0:T(8,128)(2,1)} %get-tuple-element.118), channel_id=1, source_target_pairs={{0,4},{4,0},{1,5},{5,1},{2,6},{6,2},{3,7},{7,3},{8,12},{12,8},{9,1... | collective-permute-start | bytes 3145736 | tf_op jit(solution)/shard_map/ppermute | solution.py:603
  194.7 24.7 %collective-permute-start.30 = (bf16[512,1024]{1,0:T(8,128)(2,1)}, bf16[512,1024]{1,0:T(8,128)(2,1)}, u32[]{:S(2)}, u32[]{:S(2)}) collective-permute-start(bf16[512,1024]{1,0:T(8,128)(2,1)} %add_convert_fusion.3), channel_id=1, source_target_pairs={{0,8},{8,0},{1,9},{9,1},{2,10},{10,2},{3,11},{11,3},{4,12},{12,4},... | collective-permute-start | bytes 3145736 | tf_op jit(solution)/shard_map/ppermute | solution.py:603
  195.6 39.8 %collective-permute-start.33 = (bf16[1728,512]{1,0:T(8,128)(2,1)}, bf16[1728,512]{1,0:T(8,128)(2,1)}, u32[]{:S(2)}, u32[]{:S(2)}) collective-permute-start(bf16[1728,512]{1,0:T(8,128)(2,1)} %get-tuple-element.125), channel_id=1, source_target_pairs={{0,16},{16,0},{1,17},{17,1},{2,18},{18,2},{3,19},{19,3},{4,20},{20... | collective-permute-start | bytes 5308424 | tf_op jit(solution)/shard_map/ppermute | solution.py:603
  226.5 34.9 %collective-permute-start.27 = (bf16[512,1024]{1,0:T(8,128)(2,1)S(1)}, bf16[512,1024]{1,0:T(8,128)(2,1)S(1)}, u32[]{:S(2)}, u32[]{:S(2)}) collective-permute-start(bf16[512,1024]{1,0:T(8,128)(2,1)S(1)} %copy-done.60), channel_id=1, source_target_pairs={{0,4},{4,0},{1,5},{5,1},{2,6},{6,2},{3,7},{7,3},{8,12},{12,8},{9,1... | collective-permute-start | bytes 3145736 | tf_op jit(solution)/shard_map/ppermute | solution.py:603
  226.6 34.2 %collective-permute-start.35 = (bf16[864,512]{1,0:T(8,128)(2,1)S(1)}, bf16[864,512]{1,0:T(8,128)(2,1)S(1)}, u32[]{:S(2)}, u32[]{:S(2)}) collective-permute-start(bf16[864,512]{1,0:T(8,128)(2,1)S(1)} %copy-done.62), channel_id=1, source_target_pairs={{0,16},{16,0},{1,17},{17,1},{2,18},{18,2},{3,19},{19,3},{4,20},{20... | collective-permute-start | bytes 2654216 | tf_op jit(solution)/shard_map/ppermute | solution.py:603
  227.1 51.8 %collective-permute-start.41 = (bf16[864,512]{1,0:T(8,128)(2,1)S(1)}, bf16[864,512]{1,0:T(8,128)(2,1)S(1)}, u32[]{:S(2)}, u32[]{:S(2)}) collective-permute-start(bf16[864,512]{1,0:T(8,128)(2,1)S(1)} %copy-done.61), channel_id=1, source_target_pairs={{0,16},{16,0},{1,17},{17,1},{2,18},{18,2},{3,19},{19,3},{4,20},{20... | collective-permute-start | bytes 2654216 | tf_op jit(solution)/shard_map/ppermute | solution.py:603
  235.4 22.0 %collective-permute-start.31 = (bf16[512,1024]{1,0:T(8,128)(2,1)S(1)}, bf16[512,1024]{1,0:T(8,128)(2,1)S(1)}, u32[]{:S(2)}, u32[]{:S(2)}) collective-permute-start(bf16[512,1024]{1,0:T(8,128)(2,1)S(1)} %add_convert_fusion.2), channel_id=1, source_target_pairs={{0,8},{8,0},{1,9},{9,1},{2,10},{10,2},{3,11},{11,3},{4,12},{12,4},... | collective-permute-start | bytes 3145736 | tf_op jit(solution)/shard_map/ppermute | solution.py:603
  300.2 20.3 %collective-permute-start.37 = (bf16[512,1024]{1,0:T(8,128)(2,1)S(1)}, bf16[512,1024]{1,0:T(8,128)(2,1)S(1)}, u32[]{:S(2)}, u32[]{:S(2)}) collective-permute-start(bf16[512,1024]{1,0:T(8,128)(2,1)S(1)} %copy-done.37), channel_id=1, source_target_pairs={{4,1},{1,4},{6,3},{3,6},{12,9},{9,12},{14,11},{11,14},{20,17},{17,... | collective-permute-start | bytes 3145736 | tf_op jit(solution)/shard_map/ppermute | solution.py:603
  316.5 24.5 %collective-permute-start.51 = (bf16[3,288,256]{2,1,0:T(8,128)(2,1)S(1)}, bf16[3,288,256]{2,1,0:T(8,128)(2,1)S(1)}, u32[]{:S(2)}, u32[]{:S(2)}) collective-permute-start(bf16[3,288,256]{2,1,0:T(8,128)(2,1)S(1)} %get-tuple-element.156), channel_id=1, source_target_pairs={{0,8},{8,0},{1,9},{9,1},{2,10},{10,2},{3,11},{11,3},{4,12},{12,4},... | collective-permute-start | bytes 1327112 | tf_op jit(solution)/shard_map/ppermute | solution.py:603
  320.8 20.1 %collective-permute-start.48 = (bf16[400,256]{1,0:T(8,128)(2,1)S(1)}, bf16[400,256]{1,0:T(8,128)(2,1)S(1)}, u32[]{:S(2)}, u32[]{:S(2)}) collective-permute-start(bf16[400,256]{1,0:T(8,128)(2,1)S(1)} %pad_maximum_fusion.6), channel_id=1, source_target_pairs={{0,2},{1,3},{2,0},{3,1},{4,6},{5,7},{6,4},{7,5},{8,10},{9,11},{10,... | collective-permute-start | bytes 614408 | tf_op jit(solution)/shard_map/ppermute | solution.py:613
  (94 other events, 843.6 us)

commit v6 on v5

--- a/solution.py
+++ b/solution.py
@@ -237,7 +237,7 @@
     return pl.ds(first, half), pl.ds(second, half)
 
 
-def call_local(kernel, which, arrays, outs, out_spaces, scratch, copies, flops, name, limit=58):
+def call_local(kernel, which, arrays, outs, out_spaces, scratch, copies, flops, name, limit=44):
     return pl.pallas_call(
         kernel,
         in_specs=[pl.BlockSpec(memory_space=pltpu.SMEM)] + [pl.BlockSpec(memory_space=pltpu.HBM)] * len(arrays),

time: 363 us -> 359 us (0.989)
  other arithmetic: 43.5 us -> 36.6 us
  waiting for transfers between devices: 99.5 us -> 106 us
  Pallas kernels: 109 us -> 105 us
    ppermute x48, waiting for transfers between devices: 85 us -> 93.2 us  [move(): got = lax.ppermute(self.wait(value, lane), axes, pairs)]
    ppermute x48, starting transfers between devices: 48.3 us -> 44.1 us  [move(): got = lax.ppermute(self.wait(value, lane), axes, pairs)]
    pallas_call x6, Pallas kernels: 76 us -> 72 us  [call_local(): pl.pallas_call(kernel, in_specs=[pl.BlockSpec(memory_space=pltpu.SMEM)] +...]
    unnamed x136 -> x118, local copies, waits for them, and re-layouts: 17.1 us -> 19.7 us
  transfers between devices with their start and end apart: 54 -> 54, of which waited for: 23 -> 25; matrix products, arithmetic and copies ran while one was open for 19% -> 17% of each run, Pallas kernels for 23% -> 22%
where the time goes in v6:
time: 359 us; the launch traced here: 352 us
  waiting for transfers between devices  106 us (30%)
  Pallas kernels  105 us (29%)
  starting transfers between devices  54.5 us (15%)
  other arithmetic  36.6 us (10%)
  local copies, waits for them, and re-layouts  29.7 us (8%)
  matrix products  18.3 us (5%)
    ppermute x48, waiting for transfers between devices, move(): got = lax.ppermute(self.wait(value, lane), axes, pairs)  93.2 us
    pallas_call x6, Pallas kernels, call_local(): pl.pallas_call(kernel, in_specs=[pl.BlockSpec(memory_space=pltpu.SMEM)] +...  72 us
    ppermute x48, starting transfers between devices, move(): got = lax.ppermute(self.wait(value, lane), axes, pairs)  44.1 us
    pallas_call x2, Pallas kernels, attend_back(): pl.pallas_call(functools.partial(attend_back_kernel, head), grid=(groups,...  22 us
    unnamed x118, local copies, waits for them, and re-layouts  19.7 us
    dot_general x9, matrix products, dot(): lax.dot_general(left, right, (((left_dim,), (right_dim,)), ((), ())), pre...  18.3 us
    ppermute x6, waiting for transfers between devices, around(): lax.ppermute(v, 'z', ring(size, signs * (i + 1)))  12.6 us
    pallas_call x2, Pallas kernels, attend(): pl.pallas_call(functools.partial(attend_kernel, head), grid=(groups,), in...  11.1 us
  transfers between devices with their start and end apart: 54, of which 25 were waited for; matrix products, arithmetic and copies ran while one was open for 17% of the time, Pallas kernels for 22%

profile of v6, /device:TPU:1, one launch (start us, length us, event | category | flops | bytes accessed | tf_op | source)
XLA Modules:
  0.0 352.4 jit_solution(12489874970308332309)
XLA Ops:
  4.4 4.2 %collective-permute-start.4 = (bf16[768,128]{1,0:T(8,128)(2,1)S(1)}, bf16[768,128]{1,0:T(8,128)(2,1)S(1)}, u32[]{:S(2)}, u32[]{:S(2)}) collective-permute-start(bf16[768,128]{1,0:T(8,128)(2,1)S(1)} %bitcast.115), channel_id=1, source_target_pairs={{0,3},{1,0},{2,1},{3,2},{4,7},{5,4},{6,5},{7,6},{8,11},{9,8},{10,9... | collective-permute-start | bytes 589832 | tf_op jit(solution)/shard_map/ppermute | solution.py:613
  13.1 5.8 %collective-permute-start = (bf16[512,1024]{1,0:T(8,128)(2,1)}, bf16[512,1024]{1,0:T(8,128)(2,1)}, u32[]{:S(2)}, u32[]{:S(2)}) collective-permute-start(bf16[512,1024]{1,0:T(8,128)(2,1)} %param.14), channel_id=1, source_target_pairs={{4,1},{1,4},{6,3},{3,6},{12,9},{9,12},{14,11},{11,14},{20,17},{17,... | collective-permute-start | bytes 3145736 | tf_op jit(solution)/shard_map/ppermute | solution.py:603
  21.0 3.9 %collective-permute-done.3 = bf16[768,128]{1,0:T(8,128)(2,1)S(1)} collective-permute-done((bf16[768,128]{1,0:T(8,128)(2,1)S(1)}, bf16[768,128]{1,0:T(8,128)(2,1)S(1)}, u32[]{:S(2)}, u32[]{:S(2)}) %collective-permute-start.3) | collective-permute-done | bytes 196640 | tf_op jit(solution)/shard_map/ppermute | solution.py:613
  43.8 4.5 %collective-permute-done.8.refs_2_ = bf16[1552,256]{1,0:T(8,128)(2,1)S(1)} collective-permute-done((bf16[1552,256]{1,0:T(8,128)(2,1)S(1)}, bf16[1552,256]{1,0:T(8,128)(2,1)S(1)}, u32[]{:S(2)}, u32[]{:S(2)}) %collective-permute-start.8) | collective-permute-done | bytes 794656 | tf_op jit(solution)/shard_map/ppermute | solution.py:603
  52.7 14.7 %collective-permute-done.12 = bf16[512,1024]{1,0:T(8,128)(2,1)} collective-permute-done((bf16[512,1024]{1,0:T(8,128)(2,1)}, bf16[512,1024]{1,0:T(8,128)(2,1)}, u32[]{:S(2)}, u32[]{:S(2)}) %collective-permute-start.12) | collective-permute-done | bytes 1048608 | tf_op jit(solution)/shard_map/ppermute | solution.py:603
  79.0 3.8 %fusion.2.rows = bf16[1024,1024]{1,0:T(8,128)(2,1)} fusion(f32[1024]{0:T(1024)S(1)} %bitcast.103, f32[1024]{0:T(1024)S(1)} %add_rsqrt_fusion, bf16[512,1024]{1,0:T(8,128)(2,1)} %get-tuple-element.201, bf16[512,1024]{1,0:T(8,128)(2,1)} %collective-permute-done.1, pred[]{:T(512)S(6)} %eq.12), kind=kLoop, calls=%fused_computation.4 | loop fusion | flops 13631488 | bytes 4202497 | tf_op jit(solution)/shard_map/convert_element_type | solution.py:805
  83.4 4.1 %convolution_convert_fusion.qkv_ref = bf16[1024,1024]{1,0:T(8,128)(2,1)S(1)} fusion(bf16[1024,1024]{1,0:T(8,128)(2,1)} %fusion.2.rows, bf16[1024,1024]{1,0:T(8,128)(2,1)S(1)} %get-tuple-element.92.weights), kind=kOutput, calls=%fused_computation.31 | convolution fusion | flops 2148532224 | bytes 6291456 | tf_op jit(solution)/shard_map/dot_general | solution.py:23
  87.6 5.5 %attend.2 = bf16[1024,256]{1,0:T(8,128)(2,1)S(1)} custom-call(bf16[1024,1024]{1,0:T(8,128)(2,1)S(1)} %convolution_convert_fusion.qkv_ref, f32[1024,128]{1,0:T(8,128)S(1)} %copy-done.6, f32[1024,128]{1,0:T(8,128)S(1)} %copy-done.8, s32[1024,1]{1,0:T(8,128)S(1)} %copy-done.10, s32[1,1024]{1,0:T(1,128)S(1)} %broadcast_select_fusion.4.seg_row, ...), custom_call_target="tpu_custom_call" | custom-call | flops 6000000 | bytes 100000 | tf_op jit(solution)/shard_map/attend/pallas_call | solution.py:111
  93.2 5.5 %attend.3 = bf16[1024,256]{1,0:T(8,128)(2,1)S(1)} custom-call(bf16[1024,1024]{1,0:T(8,128)(2,1)S(1)} %convolution_convert_fusion.qkv_ref, f32[1024,128]{1,0:T(8,128)S(1)} %copy-done.6, f32[1024,128]{1,0:T(8,128)S(1)} %copy-done.8, s32[1024,1]{1,0:T(8,128)S(1)} %copy-done.10, s32[1,1024]{1,0:T(1,128)S(1)} %broadcast_select_fusion.4.seg_row, ...), custom_call_target="tpu_custom_call" | custom-call | flops 6000000 | bytes 100000 | tf_op jit(solution)/shard_map/attend/pallas_call | solution.py:111
  99.8 4.2 %collective-permute-done.16.refs_3_.refs_5_ = bf16[864,512]{1,0:T(8,128)(2,1)S(1)} collective-permute-done((bf16[864,512]{1,0:T(8,128)(2,1)}, bf16[864,512]{1,0:T(8,128)(2,1)S(1)}, u32[]{:S(2)}, u32[]{:S(2)}) %collective-permute-start.16) | collective-permute-done | bytes 884768 | tf_op jit(solution)/shard_map/ppermute | solution.py:603
  117.9 19.5 %collective-permute-done.19.refs_6_ = bf16[864,512]{1,0:T(8,128)(2,1)S(1)} collective-permute-done((bf16[864,512]{1,0:T(8,128)(2,1)}, bf16[864,512]{1,0:T(8,128)(2,1)S(1)}, u32[]{:S(2)}, u32[]{:S(2)}) %collective-permute-start.19) | collective-permute-done | bytes 884768 | tf_op jit(solution)/shard_map/ppermute | solution.py:603
  144.2 20.1 %ffn_first.1 = (bf16[1152,2048]{1,0:T(8,128)(2,1)}, bf16[576,2048]{1,0:T(8,128)(2,1)}, bf16[1728,512]{1,0:T(8,128)(2,1)}, bf16[1728,512]{1,0:T(8,128)(2,1)}) custom-call(s32[1]{0:T(128)} %bitcast.36.which_ref, bf16[864,512]{1,0:T(8,128)(2,1)} %pad_maximum_fusion.2.refs_0_, bf16[864,512]{1,0:T(8,128)(2,1)} %collective-permute-done.11.refs_1_, ...), custom_call_target="tpu_custom_call" | custom-call | flops 14495514 | bytes 100000 | tf_op jit(solution)/shard_map/ffn_first/pallas_call | solution.py:241
  164.4 24.6 %ffn_second.1 = (bf16[1152,2048]{1,0:T(8,128)(2,1)}, bf16[576,2048]{1,0:T(8,128)(2,1)}, bf16[512,1024]{1,0:T(8,128)(2,1)S(1)}, bf16[512,1024]{1,0:T(8,128)(2,1)}...) custom-call(s32[1]{0:T(128)} %bitcast.36.which_ref, bf16[864,512]{1,0:T(8,128)(2,1)} %pad_maximum_fusion.2.refs_0_, ...), custom_call_target="tpu_custom_call" | custom-call | flops 18119392 | bytes 100000 | tf_op jit(solution)/shard_map/ffn_second/pallas_call | solution.py:241
  197.3 18.9 %ffn_third.1 = (bf16[864,512]{1,0:T(8,128)(2,1)S(1)}, bf16[864,512]{1,0:T(8,128)(2,1)S(1)}, bf16[864,512]{1,0:T(8,128)(2,1)S(1)}, bf16[864,512]{1,0:T(8,128)(2,1...) custom-call(s32[1]{0:T(128)} %bitcast.36.which_ref, ...), custom_call_target="tpu_custom_call" | custom-call | flops 10871635 | bytes 100000 | tf_op jit(solution)/shard_map/ffn_third/pallas_call | solution.py:241
  227.6 7.0 %collective-permute-done.33 = bf16[1728,512]{1,0:T(8,128)(2,1)} collective-permute-done((bf16[1728,512]{1,0:T(8,128)(2,1)}, bf16[1728,512]{1,0:T(8,128)(2,1)}, u32[]{:S(2)}, u32[]{:S(2)}) %collective-permute-start.33) | collective-permute-done | bytes 1769504 | tf_op jit(solution)/shard_map/ppermute | solution.py:603
  243.8 10.9 %attend_back.2 = (bf16[1024,512]{1,0:T(8,128)(2,1)S(1)}, f32[16,128]{1,0:T(8,128)S(1)}) custom-call(bf16[1024,1024]{1,0:T(8,128)(2,1)S(1)} %copy-done.3, f32[1024,128]{1,0:T(8,128)S(1)} %copy-done.7, f32[1024,128]{1,0:T(8,128)S(1)} %copy-done.9, s32[1024,1]{1,0:T(8,128)S(1)} %copy-done.11, s32[1,1024]{1,0:T(1,128)S(1)} %broadcast_select_fusion.4.seg_row, ...), custom_call_target="tpu_custom_call" | custom-call | flops 12000000 | bytes 100000 | tf_op jit(solution)/shard_map/attend_back/pallas_call | solution.py:195
  263.0 11.1 %attend_back.3 = (bf16[1024,512]{1,0:T(8,128)(2,1)S(1)}, f32[16,128]{1,0:T(8,128)S(1)}) custom-call(bf16[1024,1024]{1,0:T(8,128)(2,1)S(1)} %copy-done.3, f32[1024,128]{1,0:T(8,128)S(1)} %copy-done.7, f32[1024,128]{1,0:T(8,128)S(1)} %copy-done.9, s32[1024,1]{1,0:T(8,128)S(1)} %copy-done.11, s32[1,1024]{1,0:T(1,128)S(1)} %broadcast_select_fusion.4.seg_row, ...), custom_call_target="tpu_custom_call" | custom-call | flops 12000000 | bytes 100000 | tf_op jit(solution)/shard_map/attend_back/pallas_call | solution.py:195
  274.1 4.0 %collective-permute-done.40 = bf16[512,256]{1,0:T(8,128)(2,1)S(1)} collective-permute-done((bf16[512,256]{1,0:T(8,128)(2,1)S(1)}, bf16[512,256]{1,0:T(8,128)(2,1)S(1)}, u32[]{:S(2)}, u32[]{:S(2)}) %collective-permute-start.40) | collective-permute-done | bytes 262176 | tf_op jit(solution)/shard_map/ppermute | solution.py:603
  283.4 5.2 %qkv_grads.3 = (bf16[1088,256]{1,0:T(8,128)(2,1)S(1)}, bf16[1088,256]{1,0:T(8,128)(2,1)S(1)}, bf16[1088,256]{1,0:T(8,128)(2,1)S(1)}) custom-call(s32[3]{0:T(128)S(1)} %pad_add_fusion.1.starts_ref, bf16[1024,512]{1,0:T(8,128)(2,1)S(1)} %get-tuple-element.148.grads_0, bf16[1024,512]{1,0:T(8,128)(2,1)S(1)} %get-tuple-element.146.grads_1, ...), custom_call_target="tpu_custom_call" | custom-call | flops 1000000 | bytes 100000 | tf_op jit(solution)/shard_map/qkv_grads/pallas_call | solution.py:241
  289.3 5.3 %collective-permute-start.42 = (bf16[512,1024]{1,0:T(8,128)(2,1)S(1)}, bf16[512,1024]{1,0:T(8,128)(2,1)S(1)}, u32[]{:S(2)}, u32[]{:S(2)}) collective-permute-start(bf16[512,1024]{1,0:T(8,128)(2,1)S(1)} %add_convert_fusion), channel_id=1, source_target_pairs={{0,4},{4,0},{1,5},{5,1},{2,6},{6,2},{3,7},{7,3},{8,12},{12,8},{9,1... | collective-permute-start | bytes 3145736 | tf_op jit(solution)/shard_map/ppermute | solution.py:603
  305.8 6.0 %collective-permute-done.44 = bf16[1088,256]{1,0:T(8,128)(2,1)S(1)} collective-permute-done((bf16[1088,256]{1,0:T(8,128)(2,1)S(1)}, bf16[1088,256]{1,0:T(8,128)(2,1)S(1)}, u32[]{:S(2)}, u32[]{:S(2)}) %collective-permute-start.44) | collective-permute-done | bytes 557088 | tf_op jit(solution)/shard_map/ppermute | solution.py:603
  312.6 4.8 %collective-permute-done.37 = bf16[512,1024]{1,0:T(8,128)(2,1)S(1)} collective-permute-done((bf16[512,1024]{1,0:T(8,128)(2,1)S(1)}, bf16[512,1024]{1,0:T(8,128)(2,1)S(1)}, u32[]{:S(2)}, u32[]{:S(2)}) %collective-permute-start.37) | collective-permute-done | bytes 1048608 | tf_op jit(solution)/shard_map/ppermute | solution.py:603
  324.7 8.7 %collective-permute-done.46 = bf16[400,256]{1,0:T(8,128)(2,1)S(1)} collective-permute-done((bf16[400,256]{1,0:T(8,128)(2,1)S(1)}, bf16[400,256]{1,0:T(8,128)(2,1)S(1)}, u32[]{:S(2)}, u32[]{:S(2)}) %collective-permute-start.46) | collective-permute-done | bytes 204832 | tf_op jit(solution)/shard_map/ppermute | solution.py:613
  344.7 4.9 %collective-permute-done.47 = bf16[512,1024]{1,0:T(8,128)(2,1)} collective-permute-done((bf16[512,1024]{1,0:T(8,128)(2,1)S(1)}, bf16[512,1024]{1,0:T(8,128)(2,1)}, u32[]{:S(2)}, u32[]{:S(2)}) %collective-permute-start.47) | collective-permute-done | bytes 1048608 | tf_op jit(solution)/shard_map/ppermute | solution.py:603
  (322 shorter events, 142.9 us)
Async XLA Ops:
  13.1 24.0 %collective-permute-start = (bf16[512,1024]{1,0:T(8,128)(2,1)}, bf16[512,1024]{1,0:T(8,128)(2,1)}, u32[]{:S(2)}, u32[]{:S(2)}) collective-permute-start(bf16[512,1024]{1,0:T(8,128)(2,1)} %param.14), channel_id=1, source_target_pairs={{4,1},{1,4},{6,3},{3,6},{12,9},{9,12},{14,11},{11,14},{20,17},{17,... | collective-permute-start | bytes 3145736 | tf_op jit(solution)/shard_map/ppermute | solution.py:603
  19.0 48.3 %collective-permute-start.12 = (bf16[512,1024]{1,0:T(8,128)(2,1)}, bf16[512,1024]{1,0:T(8,128)(2,1)}, u32[]{:S(2)}, u32[]{:S(2)}) collective-permute-start(bf16[512,1024]{1,0:T(8,128)(2,1)} %param.16), channel_id=1, source_target_pairs={{4,1},{1,4},{6,3},{3,6},{12,9},{9,12},{14,11},{11,14},{20,17},{17,... | collective-permute-start | bytes 3145736 | tf_op jit(solution)/shard_map/ppermute | solution.py:603
  39.7 30.7 %collective-permute-start.1 = (bf16[512,1024]{1,0:T(8,128)(2,1)}, bf16[512,1024]{1,0:T(8,128)(2,1)}, u32[]{:S(2)}, u32[]{:S(2)}) collective-permute-start(bf16[512,1024]{1,0:T(8,128)(2,1)} %get-tuple-element.201), channel_id=1, source_target_pairs={{0,4},{4,0},{1,5},{5,1},{2,6},{6,2},{3,7},{7,3},{8,12},{12,8},{9,1... | collective-permute-start | bytes 3145736 | tf_op jit(solution)/shard_map/ppermute | solution.py:603
  40.6 29.5 %collective-permute-start.11 = (bf16[864,512]{1,0:T(8,128)(2,1)}, bf16[864,512]{1,0:T(8,128)(2,1)}, u32[]{:S(2)}, u32[]{:S(2)}) collective-permute-start(bf16[864,512]{1,0:T(8,128)(2,1)} %pad_maximum_fusion.2.refs_0_), channel_id=1, source_target_pairs={{0,1},{1,2},{2,3},{3,0},{4,5},{5,6},{6,7},{7,4},{8,9},{9,10},{10,1... | collective-permute-start | bytes 2654216 | tf_op jit(solution)/shard_map/ppermute | solution.py:603
  49.2 24.3 %collective-permute-start.9 = (bf16[1552,256]{1,0:T(8,128)(2,1)S(1)}, bf16[1552,256]{1,0:T(8,128)(2,1)S(1)}, u32[]{:S(2)}, u32[]{:S(2)}) collective-permute-start(bf16[1552,256]{1,0:T(8,128)(2,1)S(1)} %collective-permute-done.8.refs_2_), channel_id=1, source_target_pairs={{0,8},{8,0},{1,9},{9,1},{2,10},{10,2},{3,11},{11,3},{4,12},{12,4},... | collective-permute-start | bytes 2383880 | tf_op jit(solution)/shard_map/ppermute | solution.py:603
  70.1 23.0 %collective-permute-start.13 = (bf16[864,512]{1,0:T(8,128)(2,1)}, bf16[864,512]{1,0:T(8,128)(2,1)}, u32[]{:S(2)}, u32[]{:S(2)}) collective-permute-start(bf16[864,512]{1,0:T(8,128)(2,1)} %collective-permute-done.11.refs_1_), channel_id=1, source_target_pairs={{0,1},{1,2},{2,3},{3,0},{4,5},{5,6},{6,7},{7,4},{8,9},{9,10},{10,1... | collective-permute-start | bytes 2654216 | tf_op jit(solution)/shard_map/ppermute | solution.py:603
  74.4 30.5 %collective-permute-start.15 = (bf16[512,1024]{1,0:T(8,128)(2,1)S(1)}, bf16[512,1024]{1,0:T(8,128)(2,1)}, u32[]{:S(2)}, u32[]{:S(2)}) collective-permute-start(bf16[512,1024]{1,0:T(8,128)(2,1)S(1)} %broadcast_select_fusion.2.refs_8_.refs_12_), channel_id=1, source_target_pairs={{0,8},{8,0},{1,9},{9,1},{2,10},{10,2},{3,11},{11,3},{4,12},{12,4},... | collective-permute-start | bytes 3145736 | tf_op jit(solution)/shard_map/ppermute | solution.py:603
  83.1 20.8 %collective-permute-start.16 = (bf16[864,512]{1,0:T(8,128)(2,1)}, bf16[864,512]{1,0:T(8,128)(2,1)S(1)}, u32[]{:S(2)}, u32[]{:S(2)}) collective-permute-start(bf16[864,512]{1,0:T(8,128)(2,1)} %collective-permute-done.11.refs_1_), channel_id=1, source_target_pairs={{0,16},{16,0},{1,17},{17,1},{2,18},{18,2},{3,19},{19,3},{4,20},{20... | collective-permute-start | bytes 2654216 | tf_op jit(solution)/shard_map/ppermute | solution.py:603
  116.3 24.4 %collective-permute-start.22 = (bf16[512,1024]{1,0:T(8,128)(2,1)S(1)}, bf16[512,1024]{1,0:T(8,128)(2,1)S(1)}, u32[]{:S(2)}, u32[]{:S(2)}) collective-permute-start(bf16[512,1024]{1,0:T(8,128)(2,1)S(1)} %multiply_convert_fusion.refs_4_.refs_8_), channel_id=1, source_target_pairs={{0,8},{8,0},{1,9},{9,1},{2,10},{10,2},{3,11},{11,3},{4,12},{12,4},... | collective-permute-start | bytes 3145736 | tf_op jit(solution)/shard_map/ppermute | solution.py:603
  116.7 20.8 %collective-permute-start.19 = (bf16[864,512]{1,0:T(8,128)(2,1)}, bf16[864,512]{1,0:T(8,128)(2,1)S(1)}, u32[]{:S(2)}, u32[]{:S(2)}) collective-permute-start(bf16[864,512]{1,0:T(8,128)(2,1)} %collective-permute-done.13.refs_2_), channel_id=1, source_target_pairs={{0,16},{16,0},{1,17},{17,1},{2,18},{18,2},{3,19},{19,3},{4,20},{20... | collective-permute-start | bytes 2654216 | tf_op jit(solution)/shard_map/ppermute | solution.py:603
  117.0 24.9 %collective-permute-start.18 = (bf16[864,512]{1,0:T(8,128)(2,1)}, bf16[864,512]{1,0:T(8,128)(2,1)S(1)}, u32[]{:S(2)}, u32[]{:S(2)}) collective-permute-start(bf16[864,512]{1,0:T(8,128)(2,1)} %collective-permute-done.13.refs_2_), channel_id=1, source_target_pairs={{0,1},{1,2},{2,3},{3,0},{4,5},{5,6},{6,7},{7,4},{8,9},{9,10},{10,1... | collective-permute-start | bytes 2654216 | tf_op jit(solution)/shard_map/ppermute | solution.py:603
  117.0 25.3 %collective-permute-start.24 = (bf16[512,1024]{1,0:T(8,128)(2,1)S(1)}, bf16[512,1024]{1,0:T(8,128)(2,1)S(1)}, u32[]{:S(2)}, u32[]{:S(2)}) collective-permute-start(bf16[512,1024]{1,0:T(8,128)(2,1)S(1)} %broadcast_select_fusion.2.refs_8_.refs_12_), channel_id=1, source_target_pairs={{0,4},{4,0},{1,5},{5,1},{2,6},{6,2},{3,7},{7,3},{8,12},{12,8},{9,1... | collective-permute-start | bytes 3145736 | tf_op jit(solution)/shard_map/ppermute | solution.py:603
  117.9 24.4 %collective-permute-start.25 = (bf16[512,1024]{1,0:T(8,128)(2,1)}, bf16[512,1024]{1,0:T(8,128)(2,1)S(1)}, u32[]{:S(2)}, u32[]{:S(2)}) collective-permute-start(bf16[512,1024]{1,0:T(8,128)(2,1)} %collective-permute-done.15.refs_10_.refs_14_), channel_id=1, source_target_pairs={{0,4},{4,0},{1,5},{5,1},{2,6},{6,2},{3,7},{7,3},{8,12},{12,8},{9,1... | collective-permute-start | bytes 3145736 | tf_op jit(solution)/shard_map/ppermute | solution.py:603
  141.9 22.4 %collective-permute-start.20 = (bf16[864,512]{1,0:T(8,128)(2,1)S(1)}, bf16[864,512]{1,0:T(8,128)(2,1)S(1)}, u32[]{:S(2)}, u32[]{:S(2)}) collective-permute-start(bf16[864,512]{1,0:T(8,128)(2,1)S(1)} %collective-permute-done.18.refs_3_), channel_id=1, source_target_pairs={{0,16},{16,0},{1,17},{17,1},{2,18},{18,2},{3,19},{19,3},{4,20},{20... | collective-permute-start | bytes 2654216 | tf_op jit(solution)/shard_map/ppermute | solution.py:603
  190.4 26.8 %collective-permute-start.29 = (bf16[512,1024]{1,0:T(8,128)(2,1)}, bf16[512,1024]{1,0:T(8,128)(2,1)}, u32[]{:S(2)}, u32[]{:S(2)}) collective-permute-start(bf16[512,1024]{1,0:T(8,128)(2,1)} %get-tuple-element.118), channel_id=1, source_target_pairs={{0,4},{4,0},{1,5},{5,1},{2,6},{6,2},{3,7},{7,3},{8,12},{12,8},{9,1... | collective-permute-start | bytes 3145736 | tf_op jit(solution)/shard_map/ppermute | solution.py:603
  194.3 24.7 %collective-permute-start.30 = (bf16[512,1024]{1,0:T(8,128)(2,1)}, bf16[512,1024]{1,0:T(8,128)(2,1)}, u32[]{:S(2)}, u32[]{:S(2)}) collective-permute-start(bf16[512,1024]{1,0:T(8,128)(2,1)} %add_convert_fusion.3), channel_id=1, source_target_pairs={{0,8},{8,0},{1,9},{9,1},{2,10},{10,2},{3,11},{11,3},{4,12},{12,4},... | collective-permute-start | bytes 3145736 | tf_op jit(solution)/shard_map/ppermute | solution.py:603
  194.8 39.8 %collective-permute-start.33 = (bf16[1728,512]{1,0:T(8,128)(2,1)}, bf16[1728,512]{1,0:T(8,128)(2,1)}, u32[]{:S(2)}, u32[]{:S(2)}) collective-permute-start(bf16[1728,512]{1,0:T(8,128)(2,1)} %get-tuple-element.125), channel_id=1, source_target_pairs={{0,16},{16,0},{1,17},{17,1},{2,18},{18,2},{3,19},{19,3},{4,20},{20... | collective-permute-start | bytes 5308424 | tf_op jit(solution)/shard_map/ppermute | solution.py:603
  225.3 35.2 %collective-permute-start.27 = (bf16[512,1024]{1,0:T(8,128)(2,1)S(1)}, bf16[512,1024]{1,0:T(8,128)(2,1)S(1)}, u32[]{:S(2)}, u32[]{:S(2)}) collective-permute-start(bf16[512,1024]{1,0:T(8,128)(2,1)S(1)} %copy-done.54), channel_id=1, source_target_pairs={{0,4},{4,0},{1,5},{5,1},{2,6},{6,2},{3,7},{7,3},{8,12},{12,8},{9,1... | collective-permute-start | bytes 3145736 | tf_op jit(solution)/shard_map/ppermute | solution.py:603
  225.7 34.3 %collective-permute-start.35 = (bf16[864,512]{1,0:T(8,128)(2,1)S(1)}, bf16[864,512]{1,0:T(8,128)(2,1)S(1)}, u32[]{:S(2)}, u32[]{:S(2)}) collective-permute-start(bf16[864,512]{1,0:T(8,128)(2,1)S(1)} %get-tuple-element.132), channel_id=1, source_target_pairs={{0,16},{16,0},{1,17},{17,1},{2,18},{18,2},{3,19},{19,3},{4,20},{20... | collective-permute-start | bytes 2654216 | tf_op jit(solution)/shard_map/ppermute | solution.py:603
  226.1 52.1 %collective-permute-start.41 = (bf16[864,512]{1,0:T(8,128)(2,1)S(1)}, bf16[864,512]{1,0:T(8,128)(2,1)S(1)}, u32[]{:S(2)}, u32[]{:S(2)}) collective-permute-start(bf16[864,512]{1,0:T(8,128)(2,1)S(1)} %get-tuple-element.139), channel_id=1, source_target_pairs={{0,16},{16,0},{1,17},{17,1},{2,18},{18,2},{3,19},{19,3},{4,20},{20... | collective-permute-start | bytes 2654216 | tf_op jit(solution)/shard_map/ppermute | solution.py:603
  234.6 22.0 %collective-permute-start.31 = (bf16[512,1024]{1,0:T(8,128)(2,1)S(1)}, bf16[512,1024]{1,0:T(8,128)(2,1)S(1)}, u32[]{:S(2)}, u32[]{:S(2)}) collective-permute-start(bf16[512,1024]{1,0:T(8,128)(2,1)S(1)} %add_convert_fusion.2), channel_id=1, source_target_pairs={{0,8},{8,0},{1,9},{9,1},{2,10},{10,2},{3,11},{11,3},{4,12},{12,4},... | collective-permute-start | bytes 3145736 | tf_op jit(solution)/shard_map/ppermute | solution.py:603
  239.6 20.0 %collective-permute-start.34 = (bf16[864,512]{1,0:T(8,128)(2,1)S(1)}, bf16[864,512]{1,0:T(8,128)(2,1)S(1)}, u32[]{:S(2)}, u32[]{:S(2)}) collective-permute-start(bf16[864,512]{1,0:T(8,128)(2,1)S(1)} %slice.199), channel_id=1, source_target_pairs={{0,1},{1,2},{2,3},{3,0},{4,5},{5,6},{6,7},{7,4},{8,9},{9,10},{10,1... | collective-permute-start | bytes 2654216 | tf_op jit(solution)/shard_map/ppermute | solution.py:603
  295.4 22.0 %collective-permute-start.37 = (bf16[512,1024]{1,0:T(8,128)(2,1)S(1)}, bf16[512,1024]{1,0:T(8,128)(2,1)S(1)}, u32[]{:S(2)}, u32[]{:S(2)}) collective-permute-start(bf16[512,1024]{1,0:T(8,128)(2,1)S(1)} %add_convert_fusion.1), channel_id=1, source_target_pairs={{4,1},{1,4},{6,3},{3,6},{12,9},{9,12},{14,11},{11,14},{20,17},{17,... | collective-permute-start | bytes 3145736 | tf_op jit(solution)/shard_map/ppermute | solution.py:603
  311.9 23.7 %collective-permute-start.51 = (bf16[3,288,256]{2,1,0:T(8,128)(2,1)S(1)}, bf16[3,288,256]{2,1,0:T(8,128)(2,1)S(1)}, u32[]{:S(2)}, u32[]{:S(2)}) collective-permute-start(bf16[3,288,256]{2,1,0:T(8,128)(2,1)S(1)} %get-tuple-element.156), channel_id=1, source_target_pairs={{0,8},{8,0},{1,9},{9,1},{2,10},{10,2},{3,11},{11,3},{4,12},{12,4},... | collective-permute-start | bytes 1327112 | tf_op jit(solution)/shard_map/ppermute | solution.py:603
  (85 other events, 932.5 us)
